TPU v7x, 128 devices: a whole 4x4x4 slice. The times are simulated.
128 devices in a mesh: row: 8 (over z, x_hi), col: 16 (over x_lo, y, core).
Axes of the slice: x: 4 (x_hi: 2, x_lo: 2; x = x_hi * 2 + x_lo), y: 4, z: 4, core: 2. Of those that a mesh axis runs over, the one named last changes fastest.
Arguments:
- rects: int32 [4, 65536], P(None, ('row', 'col')), may hold values from 0 to 2048, as said below
- owner: int32 [65536], P(('row', 'col')), may hold values from 0 to 127, as said below
- counts: int32 [128], P(('row', 'col')), may hold values from 256 to 512
- target: int32 [1024, 8192], P('row', 'col'), may hold values 0 or 1
- loss_weight: float32 [1024, 8192], P('row', 'col'), may hold values from 0.03 to 30, as said below
- kernel: bfloat16 [8, 33, 33], replicated, may hold values from -0.1875 to 0.1875
- socs_weight: float32 [4], replicated, may hold values from 0.25 to 1
Outputs:
- mask_grad: float32 [1024, 8192], P('row', 'col')
- loss: float32 [1], replicated
Inputs may be any that keep to these rules, and one draw needn't show every extreme that they name: `owner`: tiles are numbered row index times 16 plus col index. Among the live slots of one layout partition, no tile is named more than 8 times; some tile is named exactly 8 times by the live slots of every partition. Dead slots hold arbitrary tiles. `rects`: every slot has x_lo < x_hi <= 2048, y_lo < y_hi <= 512, x_hi - x_lo at most 64 and y_hi - y_lo at most 48. `loss_weight`: Positive.
All inputs are finite; a program needn't handle non-finite values. No bound on the sum of `target` on one device may be relied on, other than what follows from the above.
Results may differ from a plain program's by a relative error of at most 0.0027.
Values may be sent and summed in bfloat16 or wider, within the bound.
No kernel may reach another device: no remote copies, remote signals or barrier semaphores. Data moves between devices by JAX's collectives and lax.ppermute only.
A program may use at most 64 MiB of HBM per device.

v0:
```python
import jax
import jax.numpy as jnp
from jax import lax
from jax.sharding import PartitionSpec as P

RAD = 16
CAP = 8
KS = 33


def padded_2(x, sides, width):
    for axis, dim in sides:
        count, length = (lax.axis_size(axis), x.shape[dim])
        up = [(i, (i + 1) % count) for i in range(count - 1)]
        down = [(j, i) for i, j in up]
        last = lax.slice_in_dim(x, length - width, length, axis=dim)
        initial = lax.slice_in_dim(x, 0, width, axis=dim)
        before = lax.ppermute(last, axis, up)
        after = lax.ppermute(initial, axis, down)
        x = jnp.concatenate([before, x, after], axis=dim)
    return x


def cover_cells(lower_edge, upper_edge, cell_count):
    cell_edges = 4.0 * jnp.arange(cell_count, dtype=jnp.float32)[None, :]
    spans = jnp.minimum(upper_edge[:, None], cell_edges + 4.0) - jnp.maximum(
        lower_edge[:, None], cell_edges
    )
    return jnp.clip(spans, 0.0, 4.0) / 4.0


def spread_columns(extended, radius):
    blocks = (extended.shape[-1] - 2 * radius) // 128
    leading = extended.shape[:-1]
    padded = jnp.pad(extended, [(0, 0)] * (extended.ndim - 1) + [(0, 128 - 2 * radius)])
    head_part = padded[..., : blocks * 128].reshape(leading + (blocks, 128))
    tail_part = padded[..., 128:].reshape(leading + (blocks, 128))[..., : 2 * radius]
    return jnp.concatenate([head_part, tail_part], axis=-1)


def band_table(kernel_slab, window_width):
    support = kernel_slab.shape[-1]
    offsets = jnp.arange(window_width)[:, None] - jnp.arange(128)[None, :]
    one_hot = (offsets[:, :, None] == jnp.arange(support)[None, None, :]).astype(jnp.float32)
    return jnp.einsum("ctx,pqx->tpcq", kernel_slab, one_hot, precision=lax.Precision.HIGHEST)


def forward_fields(extended, kernel, rows_out):
    window_width = 128 + 2 * RAD
    windows = spread_columns(extended, RAD)
    blocks = windows.shape[1]
    channels = kernel.shape[0]
    kernel_wide = kernel.astype(jnp.float32)

    def forward_one_turn(group_index, running):
        kernel_slab = lax.dynamic_slice_in_dim(kernel_wide, 3 * group_index, 3, 1)
        band_values = band_table(kernel_slab, window_width).astype(jnp.bfloat16)
        row_slab = jnp.stack(
            [
                lax.dynamic_slice_in_dim(windows, 3 * group_index + offset_row, rows_out, 0)
                for offset_row in range(3)
            ]
        )
        return running + jnp.einsum(
            "trbp,tpcq->crbq", row_slab, band_values, preferred_element_type=jnp.float32
        )

    initial = jnp.zeros((channels, rows_out, blocks, 128), jnp.float32)
    result = lax.fori_loop(0, KS // 3, forward_one_turn, initial)
    return result.reshape(channels, rows_out, blocks * 128)


def adjoint_grad(extended, kernel, rows_out):
    window_width = 128 + 2 * RAD
    windows = spread_columns(extended, RAD)
    blocks = windows.shape[2]
    flipped = kernel.astype(jnp.float32)[:, ::-1, ::-1]

    def adjoint_one_turn(group_index, running):
        kernel_slab = lax.dynamic_slice_in_dim(flipped, 3 * group_index, 3, 1)
        band_values = band_table(kernel_slab, window_width).astype(jnp.bfloat16)
        row_slab = jnp.stack(
            [
                lax.dynamic_slice_in_dim(windows, 3 * group_index + offset_row, rows_out, 1)
                for offset_row in range(3)
            ],
            axis=1,
        )
        return running + jnp.einsum(
            "ctrbp,tpcq->rbq", row_slab, band_values, preferred_element_type=jnp.float32
        )

    initial = jnp.zeros((rows_out, blocks, 128), jnp.float32)
    result = lax.fori_loop(0, KS // 3, adjoint_one_turn, initial)
    return result.reshape(rows_out, blocks * 128)


def resist_terms(fields, weight_pair, socs_weight):
    channels, row_count, col_count = fields.shape
    squared = (fields * fields).reshape(channels // 2, 2, row_count, col_count)
    intensity = jnp.sum(socs_weight[:, None, None, None] * squared, axis=(0, 1))
    resist = jax.nn.sigmoid(intensity - 3.0)
    slope = 2.0 * (weight_pair[0] * resist - weight_pair[1]) * resist * (1.0 - resist)
    gradient_fields = (
        2.0 * jnp.repeat(socs_weight, 2)[:, None, None] * fields * slope[None]
    ).astype(jnp.bfloat16)
    return (resist, gradient_fields)


def shards(rects, owner, counts, target, loss_weight, kernel, socs_weight):
    row_devices = lax.axis_size("row")
    col_devices = lax.axis_size("col")
    devices = row_devices * col_devices
    slot_count = owner.shape[0]
    tile_rows, tile_cols = target.shape
    live = jnp.arange(slot_count) < counts[0]
    hits = ((owner[:, None] == jnp.arange(devices)[None, :]) & live[:, None]).astype(jnp.int32)
    earlier = jnp.cumsum(hits, axis=0) - hits
    ranking = jnp.sum(earlier * hits, axis=1)
    placing = jnp.where(live, owner * CAP + ranking, devices * CAP)
    outbox = (
        jnp.zeros((4, devices * CAP), jnp.float32)
        .at[:, placing]
        .set(rects.astype(jnp.float32), mode="drop")
    )
    inbox = lax.all_to_all(
        outbox.reshape(4, devices, CAP), ("row", "col"), split_axis=1, concat_axis=1, tiled=True
    )
    inbox = inbox.reshape(4, devices * CAP)
    row_cover = cover_cells(inbox[2], inbox[3], tile_rows).astype(jnp.bfloat16)
    col_cover = cover_cells(inbox[0], inbox[1], tile_cols).astype(jnp.bfloat16)
    coverage = jnp.einsum("sr,sc->rc", row_cover, col_cover, preferred_element_type=jnp.float32)
    mask = coverage.astype(jnp.bfloat16)
    target_float = target.astype(jnp.float32)
    weight_pair = jnp.stack([loss_weight, loss_weight * target_float])
    extended = padded_2(mask, (("row", 0), ("col", 1)), RAD)
    fields = forward_fields(extended, kernel, tile_rows)
    resist, gradient_fields = resist_terms(fields, weight_pair, socs_weight)
    margin_fields = padded_2(gradient_fields, (("row", 1), ("col", 2)), RAD)
    mask_grad = adjoint_grad(margin_fields, kernel, tile_rows)
    local_loss = jnp.sum(loss_weight * (resist - target_float) ** 2)
    total_loss = lax.psum(local_loss, ("row", "col"))
    window_area = tile_rows * row_devices * tile_cols * col_devices
    return (mask_grad, (total_loss / window_area).reshape(1))


def solution(mesh):
    placed = (
        P(None, ("row", "col")),
        P(("row", "col")),
        P(("row", "col")),
        P("row", "col"),
        P("row", "col"),
        P(),
        P(),
    )
    return jax.shard_map(
        shards, mesh=mesh, in_specs=placed, out_specs=(P("row", "col"), P()), check_vma=False
    )
```

profile of v0, /device:TPU:1, one launch (start us, length us, event | category | flops | bytes accessed | tf_op | source)
XLA Modules:
  0.0 234.7 jit_solution(6212392668529351614)
XLA Ops:
  5.1 1.8 scatter_custom_fusion
  8.4 11.5 %all-to-all-start = ((f32[4,128,8]{2,0,1:T(4,128)}), f32[4,128,8]{2,0,1:T(4,128)S(1)}, u32[]{:S(2)}, u32[]{:S(2)}) async-start(f32[4,128,8]{2,0,1:T(4,128)} %copy.30), calls=%async_computation | async-start | bytes 524288 | tf_op jit(solution)/shard_map/all_to_all | solution.py:126
  20.0 11.0 %all-to-all-done = f32[4,128,8]{2,0,1:T(4,128)S(1)} async-done(((f32[4,128,8]{2,0,1:T(4,128)}), f32[4,128,8]{2,0,1:T(4,128)S(1)}, u32[]{:S(2)}, u32[]{:S(2)}) %all-to-all-start) | async-done | bytes 16416 | tf_op jit(solution)/shard_map/all_to_all | solution.py:126
  33.2 3.1 %collective-permute-start = (bf16[16,512]{1,0:T(8,128)(2,1)S(1)}, bf16[16,512]{1,0:T(8,128)(2,1)S(1)}, u32[]{:S(2)}, u32[]{:S(2)}) collective-permute-start(bf16[16,512]{1,0:T(8,128)(2,1)S(1)} %get-tuple-element.302), channel_id=1, source_target_pairs={{0,16},{16,32},{32,48},{48,64},{64,80},{80,96},{96,112},{1,17},{17... | collective-permute-start | bytes 49160 | tf_op jit(solution)/shard_map/ppermute | solution.py:18
  37.8 4.5 %collective-permute-done.1 = bf16[16,512]{1,0:T(8,128)(2,1)S(1)} collective-permute-done((bf16[16,512]{1,0:T(8,128)(2,1)S(1)}, bf16[16,512]{1,0:T(8,128)(2,1)S(1)}, u32[]{:S(2)}, u32[]{:S(2)}) %collective-permute-start.1) | collective-permute-done | bytes 16416 | tf_op jit(solution)/shard_map/ppermute | solution.py:19
  42.4 4.0 %collective-permute-start.2 = (bf16[160,16]{1,0:T(8,128)(2,1)S(1)}, bf16[160,16]{1,0:T(8,128)(2,1)S(1)}, u32[]{:S(2)}, u32[]{:S(2)}) collective-permute-start(bf16[160,16]{1,0:T(8,128)(2,1)S(1)} %get-tuple-element.300), channel_id=1, source_target_pairs={{0,1},{1,2},{2,3},{3,4},{4,5},{5,6},{6,7},{7,8},{8,9},{9,10},{10,1... | collective-permute-start | bytes 15368 | tf_op jit(solution)/shard_map/ppermute | solution.py:18
  46.4 1.9 collective-permute-start.3
  48.4 3.3 %collective-permute-done.3 = bf16[160,16]{1,0:T(8,128)(2,1)S(1)} collective-permute-done((bf16[160,16]{1,0:T(8,128)(2,1)S(1)}, bf16[160,16]{1,0:T(8,128)(2,1)S(1)}, u32[]{:S(2)}, u32[]{:S(2)}) %collective-permute-start.3) | collective-permute-done | bytes 5152 | tf_op jit(solution)/shard_map/ppermute | solution.py:19
  52.2 29.7 %while.32 = (s32[]{:T(128)}, f32[8,128,4,128]{1,3,2,0:T(8,128)S(1)}, f32[8,33,33]{2,0,1:T(8,128)S(1)}, bf16[160,4,160]{0,2,1:T(8,128)(2,1)S(1)}, s32[]{:T(128)},...) while((s32[]{:T(128)}, ...), condition=%wide.region_5.6_spmd.clone, body=%wide.region_4.5_spmd.clone.sunk | while | flops 701669376 | bytes 7811386 | solution.py:69
  82.4 1.9 copy.33
  85.0 2.0 multiply_convert_fusion
  87.0 4.2 %collective-permute-start.4 = (bf16[8,16,512]{2,1,0:T(8,128)(2,1)S(1)}, bf16[8,16,512]{2,1,0:T(8,128)(2,1)S(1)}, u32[]{:S(2)}, u32[]{:S(2)}) collective-permute-start(bf16[8,16,512]{2,1,0:T(8,128)(2,1)S(1)} %get-tuple-element.294), channel_id=1, source_target_pairs={{0,16},{16,32},{32,48},{48,64},{64,80},{80,96},{96,112},{1,17},{17... | collective-permute-start | bytes 393224 | tf_op jit(solution)/shard_map/ppermute | solution.py:18
  93.2 5.3 %collective-permute-done.5 = bf16[8,16,512]{2,1,0:T(8,128)(2,1)S(1)} collective-permute-done((bf16[8,16,512]{2,1,0:T(8,128)(2,1)S(1)}, bf16[8,16,512]{2,1,0:T(8,128)(2,1)S(1)}, u32[]{:S(2)}, u32[]{:S(2)}) %collective-permute-start.5) | collective-permute-done | bytes 131104 | tf_op jit(solution)/shard_map/ppermute | solution.py:19
  98.7 4.3 %collective-permute-start.6 = (bf16[8,160,16]{2,1,0:T(8,128)(2,1)S(1)}, bf16[8,160,16]{2,1,0:T(8,128)(2,1)S(1)}, u32[]{:S(2)}, u32[]{:S(2)}) collective-permute-start(bf16[8,160,16]{2,1,0:T(8,128)(2,1)S(1)} %get-tuple-element.292), channel_id=1, source_target_pairs={{0,1},{1,2},{2,3},{3,4},{4,5},{5,6},{6,7},{7,8},{8,9},{9,10},{10,1... | collective-permute-start | bytes 122888 | tf_op jit(solution)/shard_map/ppermute | solution.py:18
  103.0 1.9 collective-permute-start.7
  105.0 66.6 %psum.7 = f32[]{:T(128)} all-reduce(f32[]{:T(128)} %get-tuple-element.296), channel_id=1, replica_groups=mesh['row'=8,'col'=16] {'row','col'}, use_global_device_ids=true, to_apply=%region_10.11 | all-reduce | flops 1 | bytes 8 | tf_op jit(solution)/shard_map/psum | solution.py:142
  172.3 2.9 %pad_maximum_fusion.1 = (bf16[8,160,512]{2,1,0:T(8,128)(2,1)S(1)}, bf16[8,160,512]{2,1,0:T(8,128)(2,1)}) fusion(bf16[8,160,16]{2,1,0:T(8,128)(2,1)S(1)} %collective-permute-done.6, bf16[8,16,512]{2,1,0:T(8,128)(2,1)S(1)} %collective-permute-done.5, bf16[8,128,512]{2,1,0:T(8,128)(2,1)S(1)} %multiply_convert_fusion, ...), kind=kLoop, calls=%fused_computation.59 | loop fusion | flops 16384000 | bytes 4014080 | tf_op jit(solution)/shard_map/concatenate | solution.py:20
  175.6 2.7 %reshape.132 = bf16[8,160,4,128]{3,2,1,0:T(4,128)(2,1)S(1)} reshape(bf16[8,160,512]{2,1,0:T(8,128)(2,1)} %get-tuple-element.291) | data formatting | bytes 2621440 | tf_op jit(solution)/shard_map/reshape | solution.py:37
  178.3 3.1 %pad_maximum_fusion = bf16[8,160,4,160]{3,2,1,0:T(4,128)(2,1)} fusion(bf16[8,160,4,32]{3,2,1,0:T(4,128)(2,1)S(1)} %bitcast.114, bf16[8,160,4,128]{3,2,1,0:T(4,128)(2,1)S(1)} %reshape.131), kind=kLoop, calls=%fused_computation.51 | loop fusion | flops 3276800 | bytes 3276800 | tf_op jit(solution)/shard_map/concatenate | solution.py:38
  181.4 5.2 %copy.37 = bf16[8,160,4,160]{1,3,2,0:T(8,128)(2,1)S(1)} copy(bf16[8,160,4,160]{3,2,1,0:T(4,128)(2,1)} %pad_maximum_fusion) | data formatting | bytes 3276800
  186.6 46.2 %while.33 = (s32[]{:T(128)}, f32[128,4,128]{2,0,1:T(8,128)S(1)}, bf16[8,160,4,160]{1,3,2,0:T(8,128)(2,1)S(1)}, f32[8,33,33]{2,0,1:T(8,128)S(1)}, s32[]{:T(128)},...) while((s32[]{:T(128)}, f32[128,4,128]{2,0,1:T(8,128)S(1)}, ...), condition=%wide.region_8.9_spmd.clone, body=%wide.region_7.8_spmd.clone.sunk | while | flops 703209472 | bytes 14463290 | solution.py:94
  188.0 1.5 dynamic-slice_bitcast_fusion.9
  192.2 1.5 dynamic-slice_bitcast_fusion.9
  196.4 1.5 dynamic-slice_bitcast_fusion.9
  (147 shorter events, 83.8 us)
Async XLA Ops:
  8.4 22.6 %all-to-all-start = ((f32[4,128,8]{2,0,1:T(4,128)}), f32[4,128,8]{2,0,1:T(4,128)S(1)}, u32[]{:S(2)}, u32[]{:S(2)}) async-start(f32[4,128,8]{2,0,1:T(4,128)} %copy.30), calls=%async_computation | async-start | bytes 524288 | tf_op jit(solution)/shard_map/all_to_all | solution.py:126
  20.0 17.6 %copy-start.4 = (f32[4]{0:T(128)S(1)}, f32[4]{0:T(128)}, u32[]{:S(2)}) copy-start(f32[4]{0:T(128)} %param.17) | copy-start | bytes 52
  31.8 16.6 %copy-start = (bf16[8,33,33]{2,0,1:T(8,128)(2,1)S(1)}, bf16[8,33,33]{2,0,1:T(8,128)(2,1)}, u32[]{:S(2)}) copy-start(bf16[8,33,33]{2,0,1:T(8,128)(2,1)} %param.16) | copy-start | bytes 52276
  33.2 4.6 %collective-permute-start = (bf16[16,512]{1,0:T(8,128)(2,1)S(1)}, bf16[16,512]{1,0:T(8,128)(2,1)S(1)}, u32[]{:S(2)}, u32[]{:S(2)}) collective-permute-start(bf16[16,512]{1,0:T(8,128)(2,1)S(1)} %get-tuple-element.302), channel_id=1, source_target_pairs={{0,16},{16,32},{32,48},{48,64},{64,80},{80,96},{96,112},{1,17},{17... | collective-permute-start | bytes 49160 | tf_op jit(solution)/shard_map/ppermute | solution.py:18
  36.3 6.0 %collective-permute-start.1 = (bf16[16,512]{1,0:T(8,128)(2,1)S(1)}, bf16[16,512]{1,0:T(8,128)(2,1)S(1)}, u32[]{:S(2)}, u32[]{:S(2)}) collective-permute-start(bf16[16,512]{1,0:T(8,128)(2,1)S(1)} %get-tuple-element.303), channel_id=1, source_target_pairs={{16,0},{32,16},{48,32},{64,48},{80,64},{96,80},{112,96},{17,1},{33... | collective-permute-start | bytes 49160 | tf_op jit(solution)/shard_map/ppermute | solution.py:19
  42.4 6.0 %collective-permute-start.2 = (bf16[160,16]{1,0:T(8,128)(2,1)S(1)}, bf16[160,16]{1,0:T(8,128)(2,1)S(1)}, u32[]{:S(2)}, u32[]{:S(2)}) collective-permute-start(bf16[160,16]{1,0:T(8,128)(2,1)S(1)} %get-tuple-element.300), channel_id=1, source_target_pairs={{0,1},{1,2},{2,3},{3,4},{4,5},{5,6},{6,7},{7,8},{8,9},{9,10},{10,1... | collective-permute-start | bytes 15368 | tf_op jit(solution)/shard_map/ppermute | solution.py:18
  46.4 5.3 %collective-permute-start.3 = (bf16[160,16]{1,0:T(8,128)(2,1)S(1)}, bf16[160,16]{1,0:T(8,128)(2,1)S(1)}, u32[]{:S(2)}, u32[]{:S(2)}) collective-permute-start(bf16[160,16]{1,0:T(8,128)(2,1)S(1)} %get-tuple-element.301), channel_id=1, source_target_pairs={{1,0},{2,1},{3,2},{4,3},{5,4},{6,5},{7,6},{8,7},{9,8},{10,9},{11,1... | collective-permute-start | bytes 15368 | tf_op jit(solution)/shard_map/ppermute | solution.py:19
  82.4 1.9 copy-start.2
  82.4 1.9 copy-start.3
  87.0 6.1 %collective-permute-start.4 = (bf16[8,16,512]{2,1,0:T(8,128)(2,1)S(1)}, bf16[8,16,512]{2,1,0:T(8,128)(2,1)S(1)}, u32[]{:S(2)}, u32[]{:S(2)}) collective-permute-start(bf16[8,16,512]{2,1,0:T(8,128)(2,1)S(1)} %get-tuple-element.294), channel_id=1, source_target_pairs={{0,16},{16,32},{32,48},{48,64},{64,80},{80,96},{96,112},{1,17},{17... | collective-permute-start | bytes 393224 | tf_op jit(solution)/shard_map/ppermute | solution.py:18
  91.2 7.3 %collective-permute-start.5 = (bf16[8,16,512]{2,1,0:T(8,128)(2,1)S(1)}, bf16[8,16,512]{2,1,0:T(8,128)(2,1)S(1)}, u32[]{:S(2)}, u32[]{:S(2)}) collective-permute-start(bf16[8,16,512]{2,1,0:T(8,128)(2,1)S(1)} %get-tuple-element.295), channel_id=1, source_target_pairs={{16,0},{32,16},{48,32},{64,48},{80,64},{96,80},{112,96},{17,1},{33... | collective-permute-start | bytes 393224 | tf_op jit(solution)/shard_map/ppermute | solution.py:19
  98.7 73.6 %collective-permute-start.6 = (bf16[8,160,16]{2,1,0:T(8,128)(2,1)S(1)}, bf16[8,160,16]{2,1,0:T(8,128)(2,1)S(1)}, u32[]{:S(2)}, u32[]{:S(2)}) collective-permute-start(bf16[8,160,16]{2,1,0:T(8,128)(2,1)S(1)} %get-tuple-element.292), channel_id=1, source_target_pairs={{0,1},{1,2},{2,3},{3,4},{4,5},{5,6},{6,7},{7,8},{8,9},{9,10},{10,1... | collective-permute-start | bytes 122888 | tf_op jit(solution)/shard_map/ppermute | solution.py:18
  103.0 69.3 %collective-permute-start.7 = (bf16[8,160,16]{2,1,0:T(8,128)(2,1)S(1)}, bf16[8,160,16]{2,1,0:T(8,128)(2,1)S(1)}, u32[]{:S(2)}, u32[]{:S(2)}) collective-permute-start(bf16[8,160,16]{2,1,0:T(8,128)(2,1)S(1)} %get-tuple-element.293), channel_id=1, source_target_pairs={{1,0},{2,1},{3,2},{4,3},{5,4},{6,5},{7,6},{8,7},{9,8},{10,9},{11,1... | collective-permute-start | bytes 122888 | tf_op jit(solution)/shard_map/ppermute | solution.py:19
  181.4 5.2 %copy-start.1 = (f32[128,4,128]{2,0,1:T(8,128)S(1)}, f32[128,4,128]{2,0,1:T(8,128)}, u32[]{:S(2)}) copy-start(f32[128,4,128]{2,0,1:T(8,128)} %custom-call.1) | copy-start | bytes 786436
where the time goes:
time: 235 us
  blocking collectives  66.6 us (28%)
  matrix products  55.7 us (24%)
  local copies, waits for them, and re-layouts  36.5 us (16%)
  starting transfers between devices  33.5 us (14%)
  waiting for transfers between devices  24.9 us (11%)
  other arithmetic  12.6 us (5%)
  between operations  3.47 us (1%)
    psum x1, blocking collectives, shards(): total_loss = lax.psum(local_loss, ('row', 'col'))  66.6 us
    dot_general x22, matrix products, band_table(): jnp.einsum('ctx,pqx->tpcq', kernel_slab, one_hot, precision=lax.Precision...  29 us
    another operation x11, local copies, waits for them, and re-layouts, adjoint_one_turn(): jnp.stack([lax.dynamic_slice_in_dim(windows, 3 * group_index + offset_row...  16.9 us
    ppermute x4, starting transfers between devices, padded_2(): before = lax.ppermute(last, axis, up)  15.6 us
    dot_general x11, matrix products, adjoint_one_turn(): jnp.einsum('ctrbp,tpcq->rbq', row_slab, band_values, preferred_element_ty...  14 us
    ppermute x4, waiting for transfers between devices, padded_2(): after = lax.ppermute(initial, axis, down)  13.2 us
    dot_general x11, matrix products, forward_one_turn(): jnp.einsum('trbp,tpcq->crbq', row_slab, band_values, preferred_element_ty...  11.7 us
    all_to_all x1, starting transfers between devices, shards(): lax.all_to_all(outbox.reshape(4, devices, CAP), ('row', 'col'), split_axi...  11.5 us
  transfers between devices with their start and end apart: 9, of which 5 were waited for; matrix products, arithmetic and copies ran while one was open for 0% of the time, Pallas kernels for 0%

commit v1 on v0

v1 whole, which is shorter than its diff:
```python
import jax
import jax.numpy as jnp
from jax import lax
from jax.experimental import pallas as pl
from jax.experimental.pallas import tpu as pltpu
from jax.sharding import PartitionSpec as P

RAD = 16
CAP = 8
KS = 33
BLK = 32
AROWS = 36
PITCH = 20
NEIGHBOURS = [(dr, dc) for dr in (-1, 0, 1) for dc in (-1, 0, 1) if (dr, dc) != (0, 0)]
F32 = jnp.float32
BF16 = jnp.bfloat16
VMEM_LIMIT = 48 * 1024 * 1024


def dot_nt(a, b):
    return lax.dot_general(a, b, (((1,), (1,)), ((), ())), preferred_element_type=F32)


def iota(shape, dim):
    return lax.broadcasted_iota(jnp.int32, shape, dim)


def outbox_kernel(tile_cols, counts_ref, rects_ref, owner_ref, out_ref, pad_ref):
    slots = owner_ref.shape[1]
    tiles = out_ref.shape[0]
    live = iota((1, slots), 1) < counts_ref[0]
    own = jnp.where(live, owner_ref[...], -1)
    hit = iota((tiles, slots), 0) == own
    hits = jnp.where(hit, 1.0, 0.0).astype(BF16)
    before = jnp.where(iota((slots, slots), 0) < iota((slots, slots), 1), 1.0, 0.0).astype(BF16)
    earlier = jnp.dot(hits, before, preferred_element_type=F32)
    rank = jnp.sum(jnp.where(hit, earlier, 0.0), axis=0, keepdims=True).astype(jnp.int32)
    row = iota((128, slots), 0)
    chosen = rank == ((row >> 1) & 7)
    vertical = (row & 1) == 1

    def placed(first, second):
        value = jnp.where(vertical, second, first)
        value = jnp.where(chosen, value, 0)
        high = (value >> 4).astype(F32).astype(BF16)
        low = (value & 15).astype(F32).astype(BF16)
        return (16.0 * dot_nt(hits, high) + dot_nt(hits, low)).astype(jnp.int32)

    lower = placed(rects_ref[0:1, :], rects_ref[2:3, :])
    upper = placed(rects_ref[1:2, :], rects_ref[3:4, :])
    word = lower + (upper << 16)
    pad_ref[...] = jnp.zeros(pad_ref.shape, jnp.int32)
    pad_ref[24 : 24 + tiles, :] = word
    column = iota((tiles, 128), 0) % tile_cols
    group = iota((tiles, 128), 1) >> 4
    result = jnp.zeros((tiles, 128), jnp.int32)
    for n, (dr, dc) in enumerate(NEIGHBOURS):
        start = 24 + dr * tile_cols + dc
        inside = (column + dc >= 0) & (column + dc < tile_cols) & (group == n)
        result = jnp.where(inside, pad_ref[start : start + tiles, :], result)
    out_ref[:, 0, :] = result
    out_ref[:, 1, :] = word


def make_outbox(rects, owner, counts, tiles, tile_cols):
    slots = owner.shape[0]
    return pl.pallas_call(
        lambda *refs: outbox_kernel(tile_cols, *refs),
        out_shape=jax.ShapeDtypeStruct((tiles, 2, 128), jnp.int32),
        in_specs=[
            pl.BlockSpec(memory_space=pltpu.SMEM),
            pl.BlockSpec(memory_space=pltpu.VMEM),
            pl.BlockSpec(memory_space=pltpu.VMEM),
        ],
        scratch_shapes=[pltpu.VMEM((tiles + 48, 128), jnp.int32)],
        cost_estimate=pl.CostEstimate(flops=10**8, bytes_accessed=10**5, transcendentals=0),
    )(counts, rects, owner.reshape(1, slots))


def toeplitz_pair(taps, edge):
    shape = (BLK, 128)
    rolled = pltpu.roll(jnp.broadcast_to(taps, shape), 0, 1, stride=1, stride_axis=0)
    p = iota(shape, 0)
    co = iota(shape, 1) & (BLK - 1)
    near = jnp.where(co >= p, rolled, 0.0)
    far = pltpu.roll(jnp.where(co < p, rolled, 0.0), 128 - BLK, 1)
    far = far + jnp.where(co == p, jnp.broadcast_to(edge, shape), 0.0)
    return near.astype(BF16), far.astype(BF16)


def tables_kernel(uf_ref, df_ref, ua_ref, da_ref, wf_ref, t_ref):
    def forward_row(a, carry):
        for h in range(2):
            lanes = slice(128 * h, 128 * h + 128)
            near, far = toeplitz_pair(uf_ref[a, :, lanes], df_ref[a, :, lanes])
            wf_ref[a, 0:BLK, lanes] = far
            wf_ref[a, BLK : 2 * BLK, lanes] = near
        return carry

    lax.fori_loop(0, AROWS, forward_row, 0)
    channels = 8

    def adjoint_row(j, carry):
        c, turn = j // 4, j % 4
        rows = pl.ds(pl.multiple_of(c * BLK, BLK), BLK)
        for q in range(ua_ref.shape[2] // 128):
            lanes = slice(128 * q, 128 * q + 128)
            near, far = toeplitz_pair(ua_ref[j, :, lanes], da_ref[j, :, lanes])
            t_ref[0, turn, rows, lanes] = far
            t_ref[1, turn, rows, lanes] = near
        return carry

    lax.fori_loop(0, 4 * channels, adjoint_row, 0)


def make_tables(kernel):
    channels = kernel.shape[0]
    k = kernel.astype(F32)
    by_row = jnp.pad(k.transpose(1, 0, 2), ((0, AROWS - KS), (0, 0), (0, 0)))
    uf = by_row[:, :, KS - 1 : 0 : -1].reshape(AROWS, 1, channels * BLK)
    df = jnp.repeat(by_row[:, :, 0], BLK, axis=1).reshape(AROWS, 1, channels * BLK)
    padded = jnp.pad(k, ((0, 0), (7, 11), (0, 0)))
    turns = jnp.stack([padded[:, t : t + 48] for t in range(4)], axis=1)
    ua = turns[..., : KS - 1].reshape(channels * 4, 1, 48 * BLK)
    da = jnp.repeat(turns[..., KS - 1], BLK, axis=2).reshape(channels * 4, 1, 48 * BLK)
    return pl.pallas_call(
        tables_kernel,
        out_shape=(
            jax.ShapeDtypeStruct((AROWS, 2 * BLK, channels * BLK), BF16),
            jax.ShapeDtypeStruct((2, 4, channels * BLK, 48 * BLK), BF16),
        ),
        compiler_params=pltpu.CompilerParams(vmem_limit_bytes=VMEM_LIMIT),
        cost_estimate=pl.CostEstimate(flops=10**8, bytes_accessed=8 * 10**6, transcendentals=0),
    )(uf, df, ua, da)


def weights_kernel(center_ref, top_ref, bottom_ref, left_ref, right_ref, sw_ref, lw_ref, x_ref):
    rows, cols = center_ref.shape
    ext = rows + 2 * RAD
    x_ref[0:RAD, 0:cols] = top_ref[...]
    x_ref[RAD : RAD + rows, 0:cols] = center_ref[...]
    x_ref[RAD + rows : ext, 0:cols] = bottom_ref[...]
    x_ref[:, cols : cols + RAD] = right_ref[...]
    sw_ref[...] = jnp.zeros(sw_ref.shape, F32)
    lw_ref[...] = jnp.zeros(lw_ref.shape, F32)
    blocks = cols // BLK + 1
    r = iota((ext, 128), 0)
    own_rows = (r >= RAD) & (r < RAD + rows)
    co = iota((ext, 128), 1) & (BLK - 1)
    for b in range(blocks):
        if b == 0:
            piece = jnp.concatenate([left_ref[...], x_ref[:, 0:RAD]], axis=1)
        else:
            piece = x_ref[:, BLK * b - RAD : BLK * b + RAD]
        piece = jnp.concatenate([piece] * 4, axis=1)
        own = own_rows
        if b == 0:
            own = own & (co >= RAD)
        if b == blocks - 1:
            own = own & (co < RAD)
        sw_ref[pl.ds(b, ext, stride=PITCH), :] = piece
        lw_ref[pl.ds(b, ext, stride=PITCH), :] = jnp.where(own, 0.25 * jnp.abs(piece), 0.0)


def make_weights(target, loss_weight):
    rows, cols = target.shape
    signed = jnp.where(target > 0, loss_weight, -loss_weight)

    def beside(x, axis, dim):
        count, length = lax.axis_size(axis), x.shape[dim]
        up = [(i, i + 1) for i in range(count - 1)]
        down = [(j, i) for i, j in up]
        before = lax.ppermute(lax.slice_in_dim(x, length - RAD, length, axis=dim), axis, up)
        after = lax.ppermute(lax.slice_in_dim(x, 0, RAD, axis=dim), axis, down)
        return before, after

    top, bottom = beside(signed, "row", 0)
    ends = jnp.concatenate([signed[:, :RAD], signed[:, cols - RAD :]], axis=1)
    corner = [jnp.concatenate([x[:, :RAD], x[:, cols - RAD :]], axis=1) for x in (top, bottom)]
    ends = jnp.concatenate([corner[0], ends, corner[1]], axis=0)
    left, right = beside(ends, "col", 1)
    ext = rows + 2 * RAD
    shape = jax.ShapeDtypeStruct((ext * PITCH, 128), F32)
    return pl.pallas_call(
        weights_kernel,
        out_shape=(shape, shape),
        scratch_shapes=[pltpu.VMEM((ext, cols + 128), F32)],
        compiler_params=pltpu.CompilerParams(vmem_limit_bytes=VMEM_LIMIT),
        cost_estimate=pl.CostEstimate(flops=10**7, bytes_accessed=4 * 10**6, transcendentals=0),
    )(signed, top, bottom, left, right)


def imaging_kernel(rows, cols, inbox_ref, wf_ref, sw_ref, lw_ref, wv_ref, g_ref, loss_ref, mask_ref, s_ref, a_ref, gs_ref):
    halo = 2 * RAD
    ext = rows + 2 * RAD
    tall = rows + 2 * halo
    words = [inbox_ref[:, 0, :].T, inbox_ref[:, 1, :].T]
    lower = [(x & 0xFFFF).astype(F32) * 0.25 for x in words]
    upper = [(x >> 16).astype(F32) * 0.25 for x in words]

    def covers(group, base, first, count):
        cell = iota((count, 128), 0).astype(F32) + float(first)
        parts = []
        for rank in range(CAP):
            at = base + 2 * rank
            low, high = lower[group][at : at + 1, :], upper[group][at : at + 1, :]
            parts.append((jnp.clip(high - cell, 0.0, 1.0) - jnp.clip(low - cell, 0.0, 1.0)).astype(BF16))
        return jnp.concatenate(parts, axis=1)

    row_span = {-1: (rows - halo, halo, 0), 0: (0, rows, halo), 1: (0, halo, halo + rows)}
    col_span = {-1: (cols - halo, halo, cols + halo), 0: (0, cols, 0), 1: (0, halo, cols)}
    for n, (dr, dc) in enumerate(NEIGHBOURS + [(0, 0)]):
        group, base = (1, 0) if n == 8 else (0, 16 * n)
        r_first, r_count, r_at = row_span[dr]
        c_first, c_count, c_at = col_span[dc]
        row_cover = covers(group, base + 1, r_first, r_count)
        col_cover = covers(group, base, c_first, c_count)
        part = dot_nt(row_cover, col_cover).astype(BF16).astype(F32)
        mask_ref[r_at : r_at + r_count, c_at : c_at + c_count] = part

    s_ref[...] = jnp.zeros(s_ref.shape, F32)
    blocks = cols // BLK + 1
    for b in range(blocks):
        if b == 0:
            window = jnp.concatenate([mask_ref[:, cols + halo : cols + 2 * halo], mask_ref[:, 0:BLK]], axis=1)
        else:
            window = mask_ref[:, BLK * (b - 1) : BLK * (b + 1)]
        s_ref[pl.ds(b, tall, stride=PITCH), :] = jnp.concatenate([window, window], axis=1)
    step = 16 * PITCH
    first_half = iota((step, 128), 1) < 64
    for m in range(0, tall * PITCH, step):
        for h in range(2):
            even = s_ref[m + 2 * h * PITCH : m + 2 * h * PITCH + step, :]
            odd = s_ref[m + (2 * h + 1) * PITCH : m + (2 * h + 1) * PITCH + step, :]
            a_ref[m : m + step, 128 * h : 128 * h + 128] = jnp.where(first_half, even, odd).astype(BF16)

    wv = wv_ref[...]
    total = jnp.zeros((1, 128), F32)
    chunk_rows = ext // 4
    chunk = chunk_rows * PITCH
    for k in range(4):
        m = k * chunk
        fields = jnp.zeros((chunk, 256), F32)
        for g in range(AROWS // 4):
            fields = fields + jnp.dot(
                a_ref[m + 4 * PITCH * g : m + 4 * PITCH * g + chunk, :],
                wf_ref[256 * g : 256 * g + 256, :],
                preferred_element_type=F32,
            )
        square = fields * fields * wv
        intensity = square[:, :128] + square[:, 128:]
        intensity = intensity + pltpu.roll(intensity, 64, 1)
        intensity = intensity + pltpu.roll(intensity, 32, 1)
        resist = 1.0 / (1.0 + jnp.exp(3.0 - intensity))
        signed = sw_ref[m : m + chunk, :]
        slope = 2.0 * (jnp.abs(signed) * resist - jnp.maximum(signed, 0.0)) * resist * (1.0 - resist)
        miss = resist - jnp.where(signed > 0.0, 1.0, 0.0)
        total = total + jnp.sum(lw_ref[m : m + chunk, :] * miss * miss, axis=0, keepdims=True)
        gs_ref[m : m + chunk, 0:128] = (2.0 * wv[:, :128]) * fields[:, :128] * slope
        gs_ref[m : m + chunk, 128:256] = (2.0 * wv[:, 128:]) * fields[:, 128:] * slope
        for r in range(k * chunk_rows, (k + 1) * chunk_rows):
            for s in range(2):
                at = r * PITCH + s
                g_ref[s, r % 8, r // 8] = gs_ref[at : at + 16, :].astype(BF16)
    loss_ref[...] = jnp.broadcast_to(jnp.sum(total, axis=1, keepdims=True), loss_ref.shape)


def imaging(inbox, wf, sw, lw, socs_weight, rows, cols, channels):
    ext = rows + 2 * RAD
    tall = rows + 4 * RAD
    wv = jnp.repeat(socs_weight, 2 * BLK).reshape(1, channels * BLK)
    return pl.pallas_call(
        lambda *refs: imaging_kernel(rows, cols, *refs),
        out_shape=(
            jax.ShapeDtypeStruct((2, 8, ext // 8, 16, channels * BLK), BF16),
            jax.ShapeDtypeStruct((1, 128), F32),
        ),
        scratch_shapes=[
            pltpu.VMEM((tall, cols + 128), F32),
            pltpu.VMEM(((tall + 4) * PITCH, 128), F32),
            pltpu.VMEM((tall * PITCH, 256), BF16),
            pltpu.VMEM((ext * PITCH, 256), F32),
        ],
        compiler_params=pltpu.CompilerParams(vmem_limit_bytes=VMEM_LIMIT),
        cost_estimate=pl.CostEstimate(flops=4 * 10**9, bytes_accessed=8 * 10**6, transcendentals=10**6),
    )(inbox, wf.reshape(AROWS * 2 * BLK, channels * BLK), sw, lw, wv)


def adjoint_kernel(g_ref, t_ref, out_ref):
    total = jnp.zeros(out_ref.shape, F32)
    for i in range(40):
        q, turn = divmod(39 - i, 4)
        for s in range(2):
            left = g_ref[s, i % 8, i // 8 : i // 8 + 16].reshape(256, 256)
            total = total + jnp.dot(left, t_ref[s, turn, :, 128 * q : 128 * q + 256], preferred_element_type=F32)
    out_ref[...] = total


def adjoint(g, tables, rows, cols):
    out = pl.pallas_call(
        adjoint_kernel,
        out_shape=jax.ShapeDtypeStruct((256, 256), F32),
        compiler_params=pltpu.CompilerParams(vmem_limit_bytes=VMEM_LIMIT),
        cost_estimate=pl.CostEstimate(flops=4 * 10**9, bytes_accessed=10**7, transcendentals=0),
    )(g, tables)
    return out.reshape(rows // 8, cols // BLK, 8, BLK).transpose(0, 2, 1, 3).reshape(rows, cols)


def shards(rects, owner, counts, target, loss_weight, kernel, socs_weight):
    row_devices = lax.axis_size("row")
    col_devices = lax.axis_size("col")
    devices = row_devices * col_devices
    rows, cols = target.shape
    outbox = make_outbox(rects, owner, counts, devices, col_devices)
    inbox = lax.all_to_all(outbox, ("row", "col"), split_axis=0, concat_axis=0, tiled=True)
    wf, tables = make_tables(kernel)
    sw, lw = make_weights(target, loss_weight)
    g, local = imaging(inbox, wf, sw, lw, socs_weight, rows, cols, kernel.shape[0])
    losses = lax.all_to_all(local.reshape(devices), ("row", "col"), split_axis=0, concat_axis=0, tiled=True)
    mask_grad = adjoint(g, tables, rows, cols)
    window_area = rows * row_devices * cols * col_devices
    return (mask_grad, (jnp.sum(losses) / window_area).reshape(1))


def solution(mesh):
    placed = (
        P(None, ("row", "col")),
        P(("row", "col")),
        P(("row", "col")),
        P("row", "col"),
        P("row", "col"),
        P(),
        P(),
    )
    return jax.shard_map(
        shards, mesh=mesh, in_specs=placed, out_specs=(P("row", "col"), P()), check_vma=False
    )
```

time: 235 us -> 89 us (0.38)
  blocking collectives: 66.6 us -> 0 us
  matrix products: 55.7 us -> 0 us
  Pallas kernels: 0 us -> 33.7 us
  local copies, waits for them, and re-layouts: 36.5 us -> 11.8 us
  waiting for transfers between devices: 24.9 us -> 0.99 us
  other arithmetic: 12.6 us -> 1.96 us
  starting transfers between devices: 33.5 us -> 36.7 us
    psum x1 -> x0, blocking collectives: 66.6 us -> none  [shards(): total_loss = lax.psum(local_loss, ('row', 'col'))]
    dot_general x45 -> x0, matrix products: 55.7 us -> none  [the longest x22 29 us: band_table(): jnp.einsum('ctx,pqx->tpcq', kernel_slab, one_hot, precision=lax.Precision...]
    pallas_call x0 -> x5, Pallas kernels: none -> 33.7 us  [the longest x1 14 us: make_tables(): pl.pallas_call(tables_kernel, out_shape=(jax.ShapeDtypeStruct((AROWS, 2 *...]
    another operation x26 -> x4, local copies, waits for them, and re-layouts: 19.6 us -> 0.77 us  [the longest x1 0.36 us: make_tables(): jnp.repeat(turns[..., KS - 1], BLK, axis=2)]
    ppermute x8 -> x4, waiting for transfers between devices: 13.8 us -> 0.34 us  [the longest x2 0.33 us: beside(): lax.ppermute(lax.slice_in_dim(x, length - RAD, length, axis=dim), axis, up)]
    all_to_all x1 -> x2, starting transfers between devices: 11.5 us -> 23.3 us  [the longest x1 11.8 us: shards(): lax.all_to_all(local.reshape(devices), ('row', 'col'), split_axis=0, conc...]
    all_to_all x1 -> x2, waiting for transfers between devices: 11 us -> 0.65 us  [the longest x1 0.65 us: shards(): lax.all_to_all(local.reshape(devices), ('row', 'col'), split_axis=0, conc...]
    ppermute x8 -> x4, starting transfers between devices: 22 us -> 13.4 us  [the longest x2 7.98 us: beside(): lax.ppermute(lax.slice_in_dim(x, length - RAD, length, axis=dim), axis, up)]
  transfers between devices with their start and end apart: 9 -> 6, of which waited for: 5 -> 2; matrix products, arithmetic and copies ran while one was open for 0% -> 6% of each run, Pallas kernels for 0% -> 24%
where the time goes in v1:
time: 89 us; the launch traced here: 88.5 us
  starting transfers between devices  36.7 us (41%)
  Pallas kernels  33.7 us (38%)
  local copies, waits for them, and re-layouts  11.8 us (13%)
  between operations  3.36 us (4%)
  other arithmetic  1.96 us (2%)
  waiting for transfers between devices  0.99 us (1%)
    pallas_call x1, Pallas kernels, make_tables(): pl.pallas_call(tables_kernel, out_shape=(jax.ShapeDtypeStruct((AROWS, 2 *...  14 us
    all_to_all x1, starting transfers between devices, shards(): lax.all_to_all(local.reshape(devices), ('row', 'col'), split_axis=0, conc...  11.8 us
    all_to_all x1, starting transfers between devices, shards(): lax.all_to_all(outbox, ('row', 'col'), split_axis=0, concat_axis=0, tiled...  11.5 us
    pallas_call x1, Pallas kernels, imaging(): pl.pallas_call(lambda *refs: imaging_kernel(rows, cols, *refs), out_shape...  9.96 us
    ppermute x2, starting transfers between devices, beside(): lax.ppermute(lax.slice_in_dim(x, length - RAD, length, axis=dim), axis, up)  7.98 us
    unnamed x15, local copies, waits for them, and re-layouts  6.9 us
    pallas_call x1, Pallas kernels, adjoint(): pl.pallas_call(adjoint_kernel, out_shape=jax.ShapeDtypeStruct((256, 256),...  5.64 us
    ppermute x2, starting transfers between devices, beside(): after = lax.ppermute(lax.slice_in_dim(x, 0, RAD, axis=dim), axis, down)  5.4 us
  transfers between devices with their start and end apart: 6, of which 2 were waited for; matrix products, arithmetic and copies ran while one was open for 6% of the time, Pallas kernels for 24%

profile of v1, /device:TPU:1, one launch (start us, length us, event | category | flops | bytes accessed | tf_op | source)
XLA Modules:
  0.0 88.5 jit_solution(14579230718468735559)
XLA Ops:
  1.3 2.0 %shard_map.86 = s32[128,2,128]{2,1,0:T(2,128)} custom-call(s32[1]{0:T(128)S(6)} %copy.64.refs_0_, s32[4,512]{1,0:T(4,128)} %refs_1_.1, s32[1,512]{1,0:T(1,128)} %bitcast.28), custom_call_target="tpu_custom_call" | custom-call | flops 100000000 | bytes 100000 | tf_op jit(solution)/shard_map/pallas_call | solution.py:67
  3.3 11.5 %all-to-all-start = ((s32[128,2,128]{2,1,0:T(2,128)}), s32[128,2,128]{2,1,0:T(2,128)S(1)}, u32[]{:S(2)}, u32[]{:S(2)}) async-start(s32[128,2,128]{2,1,0:T(2,128)} %shard_map.86), calls=%async_computation | async-start | bytes 262144 | tf_op jit(solution)/shard_map/all_to_all | solution.py:315
  14.8 1.1 %negate_select_fusion.center_ref = f32[128,512]{1,0:T(8,128)S(1)} fusion(f32[128,512]{1,0:T(8,128)} %param.11, s32[128,512]{1,0:T(8,128)} %param.10), kind=kLoop, calls=%fused_computation.1 | loop fusion | flops 196608 | bytes 786432 | tf_op jit(solution)/shard_map/jit(_where)/select_n | solution.py:167
  15.9 1.3 %collective-permute-start.1 = (f32[16,512]{1,0:T(8,128)S(1)}, f32[16,512]{1,0:T(8,128)S(1)}, u32[]{:S(2)}, u32[]{:S(2)}) collective-permute-start(f32[16,512]{1,0:T(8,128)S(1)} %get-tuple-element.16), channel_id=1, source_target_pairs={{16,0},{32,16},{48,32},{64,48},{80,64},{96,80},{112,96},{17,1},{33... | collective-permute-start | bytes 98312 | tf_op jit(solution)/shard_map/ppermute | solution.py:174
  17.2 5.5 %collective-permute-start = (f32[16,512]{1,0:T(8,128)S(1)}, f32[16,512]{1,0:T(8,128)S(1)}, u32[]{:S(2)}, u32[]{:S(2)}) collective-permute-start(f32[16,512]{1,0:T(8,128)S(1)} %get-tuple-element.17), channel_id=1, source_target_pairs={{0,16},{16,32},{32,48},{48,64},{64,80},{80,96},{96,112},{1,17},{17... | collective-permute-start | bytes 98312 | tf_op jit(solution)/shard_map/ppermute | solution.py:173
  23.4 0.3 collective-permute-done.top_ref
  24.0 4.1 %collective-permute-start.3 = (f32[160,16]{1,0:T(8,128)S(1)}, f32[160,16]{1,0:T(8,128)S(1)}, u32[]{:S(2)}, u32[]{:S(2)}) collective-permute-start(f32[160,16]{1,0:T(8,128)S(1)} %get-tuple-element.22), channel_id=1, source_target_pairs={{1,0},{2,1},{3,2},{4,3},{5,4},{6,5},{7,6},{8,7},{9,8},{10,9},{11,1... | collective-permute-start | bytes 30728 | tf_op jit(solution)/shard_map/ppermute | solution.py:174
  28.1 2.5 %collective-permute-start.2 = (f32[160,16]{1,0:T(8,128)S(1)}, f32[160,16]{1,0:T(8,128)S(1)}, u32[]{:S(2)}, u32[]{:S(2)}) collective-permute-start(f32[160,16]{1,0:T(8,128)S(1)} %get-tuple-element.23), channel_id=1, source_target_pairs={{0,1},{1,2},{2,3},{3,4},{4,5},{5,6},{6,7},{7,8},{8,9},{9,10},{10,1... | collective-permute-start | bytes 30728 | tf_op jit(solution)/shard_map/ppermute | solution.py:173
  31.8 0.4 reshape.37.ua_ref
  32.4 0.4 reshape_reshape.13.da_ref
  32.8 14.0 %shard_map.87 = (bf16[36,64,256]{2,1,0:T(8,128)(2,1)S(1)}, bf16[2,4,256,1536]{3,2,1,0:T(8,128)(2,1)}) custom-call(f32[36,1,256]{2,1,0:T(1,128)S(1)} %reshape.36.uf_ref, f32[36,1,256]{2,1,0:T(1,128)S(1)} %reshape_reshape.12.df_ref, f32[32,1,1536]{2,1,0:T(1,128)S(1)} %reshape.37.ua_ref, f32[32,1,1536]{2,1,0:T(1,128)S(1)} %reshape_reshape.13.da_ref), custom_call_target="tpu_custom_call" | custom-call | flops 100000000 | bytes 8000000 | tf_op jit(solution)/shard_map/pallas_call | solution.py:126
  46.8 1.1 %copy-done.2 = bf16[36,64,256]{2,1,0:T(8,128)(2,1)} copy-done((bf16[36,64,256]{2,1,0:T(8,128)(2,1)}, bf16[36,64,256]{2,1,0:T(8,128)(2,1)S(1)}, u32[]{:S(2)}) %copy-start.2) | copy-done | bytes 1179672
  47.9 2.0 %shard_map.88 = (f32[3200,128]{1,0:T(8,128)S(1)}, f32[3200,128]{1,0:T(8,128)S(1)}) custom-call(f32[128,512]{1,0:T(8,128)S(1)} %negate_select_fusion.center_ref, f32[16,512]{1,0:T(8,128)S(1)} %collective-permute-done.top_ref, f32[16,512]{1,0:T(8,128)S(1)} %collective-permute-done.1.bottom_ref, f32[160,16]{1,0:T(8,128)S(1)} %collective-permute-done.2.left_ref, ...), custom_call_target="tpu_custom_call" | custom-call | flops 10000000 | bytes 4000000 | tf_op jit(solution)/shard_map/pallas_call | solution.py:184
  50.0 1.2 %copy-done = f32[3200,128]{1,0:T(8,128)} copy-done((f32[3200,128]{1,0:T(8,128)}, f32[3200,128]{1,0:T(8,128)S(1)}, u32[]{:S(2)}) %copy-start) | copy-done | bytes 1638424
  51.1 1.4 %copy-done.1 = f32[3200,128]{1,0:T(8,128)S(1)} copy-done((f32[3200,128]{1,0:T(8,128)S(1)}, f32[3200,128]{1,0:T(8,128)}, u32[]{:S(2)}) %copy-start.1) | copy-done | bytes 1638424
  52.6 1.3 %copy-done.3 = bf16[36,64,256]{2,1,0:T(8,128)(2,1)S(1)} copy-done((bf16[36,64,256]{2,1,0:T(8,128)(2,1)S(1)}, bf16[36,64,256]{2,1,0:T(8,128)(2,1)}, u32[]{:S(2)}) %copy-start.3) | copy-done | bytes 1179672
  53.8 10.0 %shard_map.89 = (bf16[2,8,20,16,256]{4,3,2,1,0:T(8,128)(2,1)}, f32[1,128]{1,0:T(1,128)S(1)}) custom-call(s32[128,2,128]{2,1,0:T(2,128)S(1)} %all-to-all-done.refs_0_, bf16[2304,256]{1,0:T(8,128)(2,1)S(1)} %bitcast.26, f32[3200,128]{1,0:T(8,128)S(1)} %get-tuple-element.9.refs_2_, f32[3200,128]{1,0:T(8,128)S(1)} %copy-done.1, f32[1,256]{1,0:T(1,128)S(1)} %reshape_reshape.11.refs_4_), custom_call_target="tpu_custom_call" | custom-call | flops 4000000000 | bytes 8000000 | tf_op jit(solution)/shard_map/pallas_call | solution.py:272
  63.8 0.7 copy.63
  64.5 11.8 %all-to-all-start.1 = ((f32[128,1,1]{2,1,0:T(1,128)}), f32[128,1,1]{2,1,0:T(1,128)S(1)}, u32[]{:S(2)}, u32[]{:S(2)}) async-start(f32[128,1,1]{2,1,0:T(1,128)} %copy.63), calls=%async_computation.1 | async-start | bytes 131072 | tf_op jit(solution)/shard_map/all_to_all | solution.py:319
  76.4 1.7 %copy-done.4 = bf16[2,8,20,16,256]{4,3,2,1,0:T(8,128)(2,1)S(1)} copy-done((bf16[2,8,20,16,256]{4,3,2,1,0:T(8,128)(2,1)S(1)}, bf16[2,8,20,16,256]{4,3,2,1,0:T(8,128)(2,1)}, u32[]{:S(2)}) %copy-start.4) | copy-done | bytes 2621464
  78.1 5.6 %shard_map.90 = f32[256,256]{1,0:T(8,128)S(1)} custom-call(bf16[2,8,20,16,256]{4,3,2,1,0:T(8,128)(2,1)S(1)} %copy-done.4, bf16[2,4,256,1536]{3,2,1,0:T(8,128)(2,1)} %get-tuple-element.12.t_ref), custom_call_target="tpu_custom_call" | custom-call | flops 4000000000 | bytes 10000000 | tf_op jit(solution)/shard_map/pallas_call | solution.py:300
  84.2 1.1 %reshape.34 = f32[128,512]{1,0:T(8,128)} reshape(f32[16,8,16,32]{3,2,1,0:T(8,128)S(1)} %copy.62) | data formatting | bytes 524288 | tf_op jit(solution)/shard_map/reshape | solution.py:306
  85.3 0.7 all-to-all-done.1
  86.0 0.7 reduce_sum.9
  (40 shorter events, 2.7 us)
Async XLA Ops:
  0.6 22.2 %copy-start.5 = (bf16[8,33,33]{2,0,1:T(8,128)(2,1)S(1)}, bf16[8,33,33]{2,0,1:T(8,128)(2,1)}, u32[]{:S(2)}) copy-start(bf16[8,33,33]{2,0,1:T(8,128)(2,1)} %param.12) | copy-start | bytes 52276
  3.3 47.8 %all-to-all-start = ((s32[128,2,128]{2,1,0:T(2,128)}), s32[128,2,128]{2,1,0:T(2,128)S(1)}, u32[]{:S(2)}, u32[]{:S(2)}) async-start(s32[128,2,128]{2,1,0:T(2,128)} %shard_map.86), calls=%async_computation | async-start | bytes 262144 | tf_op jit(solution)/shard_map/all_to_all | solution.py:315
  15.9 7.4 %collective-permute-start.1 = (f32[16,512]{1,0:T(8,128)S(1)}, f32[16,512]{1,0:T(8,128)S(1)}, u32[]{:S(2)}, u32[]{:S(2)}) collective-permute-start(f32[16,512]{1,0:T(8,128)S(1)} %get-tuple-element.16), channel_id=1, source_target_pairs={{16,0},{32,16},{48,32},{64,48},{80,64},{96,80},{112,96},{17,1},{33... | collective-permute-start | bytes 98312 | tf_op jit(solution)/shard_map/ppermute | solution.py:174
  17.2 6.5 %collective-permute-start = (f32[16,512]{1,0:T(8,128)S(1)}, f32[16,512]{1,0:T(8,128)S(1)}, u32[]{:S(2)}, u32[]{:S(2)}) collective-permute-start(f32[16,512]{1,0:T(8,128)S(1)} %get-tuple-element.17), channel_id=1, source_target_pairs={{0,16},{16,32},{32,48},{48,64},{64,80},{80,96},{96,112},{1,17},{17... | collective-permute-start | bytes 98312 | tf_op jit(solution)/shard_map/ppermute | solution.py:173
  23.0 7.6 %copy-start.6 = (f32[4]{0:T(128)S(1)}, f32[4]{0:T(128)}, u32[]{:S(2)}) copy-start(f32[4]{0:T(128)} %param.13) | copy-start | bytes 52
  24.0 23.9 %collective-permute-start.3 = (f32[160,16]{1,0:T(8,128)S(1)}, f32[160,16]{1,0:T(8,128)S(1)}, u32[]{:S(2)}, u32[]{:S(2)}) collective-permute-start(f32[160,16]{1,0:T(8,128)S(1)} %get-tuple-element.22), channel_id=1, source_target_pairs={{1,0},{2,1},{3,2},{4,3},{5,4},{6,5},{7,6},{8,7},{9,8},{10,9},{11,1... | collective-permute-start | bytes 30728 | tf_op jit(solution)/shard_map/ppermute | solution.py:174
  28.1 19.8 %collective-permute-start.2 = (f32[160,16]{1,0:T(8,128)S(1)}, f32[160,16]{1,0:T(8,128)S(1)}, u32[]{:S(2)}, u32[]{:S(2)}) collective-permute-start(f32[160,16]{1,0:T(8,128)S(1)} %get-tuple-element.23), channel_id=1, source_target_pairs={{0,1},{1,2},{2,3},{3,4},{4,5},{5,6},{6,7},{7,8},{8,9},{9,10},{10,1... | collective-permute-start | bytes 30728 | tf_op jit(solution)/shard_map/ppermute | solution.py:173
  46.8 1.1 %copy-start.2 = (bf16[36,64,256]{2,1,0:T(8,128)(2,1)}, bf16[36,64,256]{2,1,0:T(8,128)(2,1)S(1)}, u32[]{:S(2)}) copy-start(bf16[36,64,256]{2,1,0:T(8,128)(2,1)S(1)} %get-tuple-element.8) | copy-start | bytes 3538948
  49.9 1.2 %copy-start = (f32[3200,128]{1,0:T(8,128)}, f32[3200,128]{1,0:T(8,128)S(1)}, u32[]{:S(2)}) copy-start(f32[3200,128]{1,0:T(8,128)S(1)} %get-tuple-element.10.refs_3_) | copy-start | bytes 4915204
  51.1 1.4 %copy-start.1 = (f32[3200,128]{1,0:T(8,128)S(1)}, f32[3200,128]{1,0:T(8,128)}, u32[]{:S(2)}) copy-start(f32[3200,128]{1,0:T(8,128)} %copy-done) | copy-start | bytes 4915204
  52.6 1.3 %copy-start.3 = (bf16[36,64,256]{2,1,0:T(8,128)(2,1)S(1)}, bf16[36,64,256]{2,1,0:T(8,128)(2,1)}, u32[]{:S(2)}) copy-start(bf16[36,64,256]{2,1,0:T(8,128)(2,1)} %copy-done.2) | copy-start | bytes 3538948
  64.5 21.4 %all-to-all-start.1 = ((f32[128,1,1]{2,1,0:T(1,128)}), f32[128,1,1]{2,1,0:T(1,128)S(1)}, u32[]{:S(2)}, u32[]{:S(2)}) async-start(f32[128,1,1]{2,1,0:T(1,128)} %copy.63), calls=%async_computation.1 | async-start | bytes 131072 | tf_op jit(solution)/shard_map/all_to_all | solution.py:319
  76.4 1.7 %copy-start.4 = (bf16[2,8,20,16,256]{4,3,2,1,0:T(8,128)(2,1)S(1)}, bf16[2,8,20,16,256]{4,3,2,1,0:T(8,128)(2,1)}, u32[]{:S(2)}) copy-start(bf16[2,8,20,16,256]{4,3,2,1,0:T(8,128)(2,1)} %get-tuple-element.11.g_ref) | copy-start | bytes 7864324

commit v2 on v1

v2 whole, which is shorter than its diff:
```python
import jax
import jax.numpy as jnp
from jax import lax
from jax.experimental import pallas as pl
from jax.experimental.pallas import tpu as pltpu
from jax.sharding import PartitionSpec as P

RAD = 16
CAP = 8
KS = 33
BLK = 32
AROWS = 36
LEAD = 7
TABLE = 47
PITCH = 20
NEIGHBOURS = [(dr, dc) for dr in (-1, 0, 1) for dc in (-1, 0, 1) if (dr, dc) != (0, 0)]
F32 = jnp.float32
BF16 = jnp.bfloat16
VMEM_LIMIT = 32 * 1024 * 1024


def dot_nt(a, b):
    return lax.dot_general(a, b, (((1,), (1,)), ((), ())), preferred_element_type=F32)


def iota(shape, dim):
    return lax.broadcasted_iota(jnp.int32, shape, dim)


def outbox_kernel(tile_cols, counts_ref, rects_ref, owner_ref, out_ref, pad_ref):
    slots = owner_ref.shape[1]
    tiles = out_ref.shape[0]
    live = iota((1, slots), 1) < counts_ref[0]
    own = jnp.where(live, owner_ref[...], -1)
    hit = iota((tiles, slots), 0) == own
    hits = jnp.where(hit, 1.0, 0.0).astype(BF16)
    before = jnp.where(iota((slots, slots), 0) < iota((slots, slots), 1), 1.0, 0.0).astype(BF16)
    earlier = jnp.dot(hits, before, preferred_element_type=F32)
    rank = jnp.sum(jnp.where(hit, earlier, 0.0), axis=0, keepdims=True).astype(jnp.int32)
    row = iota((128, slots), 0)
    chosen = rank == (row & 7)
    vertical = (row & 8) == 8

    def placed(first, second):
        value = jnp.where(vertical, second, first)
        value = jnp.where(chosen, value, 0)
        high = (value >> 4).astype(F32).astype(BF16)
        low = (value & 15).astype(F32).astype(BF16)
        return (16.0 * dot_nt(hits, high) + dot_nt(hits, low)).astype(jnp.int32)

    lower = placed(rects_ref[0:1, :], rects_ref[2:3, :])
    upper = placed(rects_ref[1:2, :], rects_ref[3:4, :])
    word = lower + (upper << 16)
    pad_ref[...] = jnp.zeros(pad_ref.shape, jnp.int32)
    pad_ref[24 : 24 + tiles, :] = word
    column = iota((tiles, 128), 0) % tile_cols
    group = iota((tiles, 128), 1) >> 4
    result = jnp.zeros((tiles, 128), jnp.int32)
    for n, (dr, dc) in enumerate(NEIGHBOURS):
        start = 24 + dr * tile_cols + dc
        inside = (column + dc >= 0) & (column + dc < tile_cols) & (group == n)
        result = jnp.where(inside, pad_ref[start : start + tiles, :], result)
    out_ref[:, 0, :] = result
    out_ref[:, 1, :] = word


def make_outbox(rects, owner, counts, tiles, tile_cols):
    slots = owner.shape[0]
    return pl.pallas_call(
        lambda *refs: outbox_kernel(tile_cols, *refs),
        out_shape=jax.ShapeDtypeStruct((tiles, 2, 128), jnp.int32),
        in_specs=[
            pl.BlockSpec(memory_space=pltpu.SMEM),
            pl.BlockSpec(memory_space=pltpu.VMEM),
            pl.BlockSpec(memory_space=pltpu.VMEM),
        ],
        scratch_shapes=[pltpu.VMEM((tiles + 48, 128), jnp.int32)],
        cost_estimate=pl.CostEstimate(flops=10**8, bytes_accessed=10**5, transcendentals=0),
    )(counts, rects, owner.reshape(1, slots))


def tables_kernel(taps_ref, edge_ref, table_ref):
    zero = jnp.zeros((2 * BLK, table_ref.shape[2]), BF16)
    for a in range(TABLE):
        if a < LEAD or a >= LEAD + KS:
            table_ref[a] = zero
    shape = (BLK, 128)
    p = iota(shape, 0)
    co = iota(shape, 1) & (BLK - 1)
    for a in range(KS):
        for h in range(table_ref.shape[2] // 128):
            lanes = slice(128 * h, 128 * h + 128)
            taps = jnp.broadcast_to(taps_ref[a : a + 1, lanes], shape)
            rolled = pltpu.roll(taps, 0, 1, stride=1, stride_axis=0)
            far = pltpu.roll(jnp.where(co < p, rolled, 0.0), 128 - BLK, 1)
            far = far + jnp.where(co == p, jnp.broadcast_to(edge_ref[a : a + 1, lanes], shape), 0.0)
            table_ref[LEAD + a, 0:BLK, lanes] = far.astype(BF16)
            table_ref[LEAD + a, BLK : 2 * BLK, lanes] = jnp.where(co >= p, rolled, 0.0).astype(BF16)


def make_tables(kernel):
    channels = kernel.shape[0]
    by_row = kernel.astype(F32).transpose(1, 0, 2)
    taps = by_row[:, :, KS - 1 : 0 : -1].reshape(KS, channels * BLK)
    edge = jnp.repeat(by_row[:, :, 0], BLK, axis=1)
    return pl.pallas_call(
        tables_kernel,
        out_shape=pltpu.VMEM((TABLE, 2 * BLK, channels * BLK), BF16),
        compiler_params=pltpu.CompilerParams(vmem_limit_bytes=VMEM_LIMIT // 2),
        cost_estimate=pl.CostEstimate(flops=10**8, bytes_accessed=10**6, transcendentals=0),
    )(taps, edge)


def weight_strips(target, loss_weight):
    rows, cols = target.shape

    def signed(*at):
        return jnp.where(target[at] > 0, loss_weight[at], -loss_weight[at])

    def beside(first, last, axis):
        count = lax.axis_size(axis)
        up = [(i, (i + 1) % count) for i in range(count)]
        down = [(j, i) for i, j in up]
        return lax.ppermute(last, axis, up), lax.ppermute(first, axis, down)

    row_top, row_bottom = slice(0, RAD), slice(rows - RAD, rows)
    col_left, col_right = slice(0, RAD), slice(cols - RAD, cols)
    top, bottom = beside(signed(row_top, slice(None)), signed(row_bottom, slice(None)), "row")
    left, right = beside(
        jnp.concatenate([top[:, col_left], signed(slice(None), col_left), bottom[:, col_left]], axis=0),
        jnp.concatenate([top[:, col_right], signed(slice(None), col_right), bottom[:, col_right]], axis=0),
        "col",
    )
    r, c = lax.axis_index("row"), lax.axis_index("col")
    inside = jnp.stack([r > 0, r < lax.axis_size("row") - 1, c > 0, c < lax.axis_size("col") - 1])
    return top, bottom, left, right, inside.astype(jnp.int32)


def spread(x_ref, left, right, out_ref, rows, cols):
    for b in range(cols // BLK + 1):
        if b == 0:
            piece = jnp.concatenate([left, x_ref[:, 0:RAD]], axis=1)
        elif b == cols // BLK:
            piece = jnp.concatenate([x_ref[:, cols - RAD : cols], right], axis=1)
        else:
            piece = x_ref[:, BLK * b - RAD : BLK * b + RAD]
        out_ref[pl.ds(b, rows, stride=PITCH), :] = jnp.concatenate([piece] * 4, axis=1)
    for b in range(cols // BLK + 1, PITCH):
        out_ref[pl.ds(b, rows, stride=PITCH), :] = jnp.zeros((rows, 128), F32)


def correlate(a_ref, starts, count, table_ref):
    fields = None
    for g in range(AROWS // 4):
        parts = [a_ref[m + 4 * PITCH * g : m + 4 * PITCH * g + count, :] for m in starts]
        left = parts[0] if len(parts) == 1 else jnp.concatenate(parts, axis=0)
        right = table_ref[LEAD + 4 * g : LEAD + 4 * g + 4].reshape(8 * BLK, 256)
        term = jnp.dot(left, right, preferred_element_type=F32)
        fields = term if fields is None else fields + term
    return fields


def resist_and_gradient(fields, signed, wv, gs_ref, at):
    square = fields * fields * wv
    intensity = square[:, :128] + square[:, 128:]
    intensity = intensity + pltpu.roll(intensity, 64, 1)
    intensity = intensity + pltpu.roll(intensity, 32, 1)
    resist = 1.0 / (1.0 + jnp.exp(3.0 - intensity))
    slope = 2.0 * (jnp.abs(signed) * resist - jnp.maximum(signed, 0.0)) * resist * (1.0 - resist)
    for h in range(2):
        lanes = slice(128 * h, 128 * h + 128)
        gs_ref[at : at + fields.shape[0], lanes] = (2.0 * wv[:, lanes]) * fields[:, lanes] * slope
    return resist


def imaging_kernel(
    inbox_ref, table_ref, target_ref, weight_ref, left_ref, right_ref, wv_ref, inside_ref,
    loss_ref, a_ref, gs_ref, mask_ref, s_ref, x_ref, sw_ref,
):
    rows, cols = target_ref.shape
    halo = 2 * RAD
    tall = rows + 2 * halo
    words = [inbox_ref[:, 0, :].T, inbox_ref[:, 1, :].T]
    lower = [(x & 0xFFFF).astype(F32) * 0.25 for x in words]
    upper = [(x >> 16).astype(F32) * 0.25 for x in words]
    cell = iota((BLK, 128), 0).astype(F32).astype(BF16)
    cell_end = (iota((BLK, 128), 0) + 1).astype(F32).astype(BF16)

    def covers(group, at, first, count):
        low8, high8 = lower[group][at : at + CAP, :], upper[group][at : at + CAP, :]
        stacked = []
        for base in range(first, first + count, BLK):
            low = jnp.clip(low8 - float(base), 0.0, float(BLK))
            high = jnp.clip(high8 - float(base), 0.0, float(BLK))
            parts = []
            for rank in range(CAP):
                lo = jnp.broadcast_to(low[rank : rank + 1, :], (BLK, 128)).astype(BF16)
                hi = jnp.broadcast_to(high[rank : rank + 1, :], (BLK, 128)).astype(BF16)
                parts.append(jnp.maximum(jnp.minimum(hi, cell_end) - jnp.maximum(lo, cell), 0.0))
            stacked.append(jnp.concatenate(parts, axis=1))
        return stacked[0] if len(stacked) == 1 else jnp.concatenate(stacked, axis=0)

    row_span = {-1: (rows - halo, halo, 0), 0: (0, rows, halo), 1: (0, halo, halo + rows)}
    col_span = {-1: (cols - halo, halo, cols + halo), 0: (0, cols, 0), 1: (0, halo, cols)}
    for n, (dr, dc) in enumerate(NEIGHBOURS + [(0, 0)]):
        group, at = (1, 0) if n == 8 else (0, 16 * n)
        r_first, r_count, r_at = row_span[dr]
        c_first, c_count, c_at = col_span[dc]
        row_cover = covers(group, at + 8, r_first, r_count)
        col_cover = covers(group, at, c_first, c_count)
        part = dot_nt(row_cover, col_cover).astype(BF16).astype(F32)
        mask_ref[r_at : r_at + r_count, c_at : c_at + c_count] = part

    s_ref[...] = jnp.zeros(s_ref.shape, F32)
    for b in range(cols // BLK + 1):
        if b == 0:
            window = jnp.concatenate([mask_ref[:, cols + halo : cols + 2 * halo], mask_ref[:, 0:BLK]], axis=1)
        else:
            window = mask_ref[:, BLK * (b - 1) : BLK * (b + 1)]
        s_ref[pl.ds(b, tall, stride=PITCH), :] = jnp.concatenate([window, window], axis=1)
    step = 16 * PITCH
    first_half = iota((step, 128), 1) < 64
    for m in range(0, tall * PITCH, step):
        for h in range(2):
            even = s_ref[m + 2 * h * PITCH : m + 2 * h * PITCH + step, :]
            odd = s_ref[m + (2 * h + 1) * PITCH : m + (2 * h + 1) * PITCH + step, :]
            a_ref[m : m + step, 128 * h : 128 * h + 128] = jnp.where(first_half, even, odd).astype(BF16)

    x_ref[...] = jnp.where(target_ref[...] > 0, weight_ref[...], -weight_ref[...])
    left = jnp.where(inside_ref[2] > 0, left_ref[RAD : RAD + rows, :], 0.0)
    right = jnp.where(inside_ref[3] > 0, right_ref[RAD : RAD + rows, :], 0.0)
    spread(x_ref, left, right, sw_ref, rows, cols)

    wv = wv_ref[...]
    chunk = rows // 4 * PITCH
    block = iota((chunk, 128), 0) % PITCH
    co = iota((chunk, 128), 1) & (BLK - 1)
    own = ((block > 0) | (co >= RAD)) & ((block < cols // BLK) | (co < RAD)) & (block <= cols // BLK)
    total = jnp.zeros((1, 128), F32)
    for k in range(4):
        m = k * chunk
        fields = correlate(a_ref, [RAD * PITCH + m], chunk, table_ref)
        signed = sw_ref[m : m + chunk, :]
        resist = resist_and_gradient(fields, signed, wv, gs_ref, m)
        miss = resist - jnp.where(signed > 0.0, 1.0, 0.0)
        part = jnp.where(own, jnp.abs(signed), 0.0) * miss * miss
        total = total + jnp.sum(part, axis=0, keepdims=True)
    total = 0.25 * jnp.sum(total, axis=1, keepdims=True)
    loss_ref[...] = jnp.broadcast_to(total, loss_ref.shape)


SMALL = pl.BlockSpec(memory_space=pltpu.SMEM)
WHOLE = pl.BlockSpec(memory_space=pltpu.VMEM)


def imaging(inbox, table, target, weight, left, right, wv, inside):
    rows, cols = target.shape
    tall = rows + 4 * RAD
    return pl.pallas_call(
        imaging_kernel,
        out_shape=(
            jax.ShapeDtypeStruct((1, 128), F32),
            pltpu.VMEM((tall * PITCH, 256), BF16),
            pltpu.VMEM((rows * PITCH, 256), F32),
        ),
        in_specs=[WHOLE] * 7 + [SMALL],
        scratch_shapes=[
            pltpu.VMEM((tall, cols + 128), F32),
            pltpu.VMEM(((tall + 4) * PITCH, 128), F32),
            pltpu.VMEM((rows, cols), F32),
            pltpu.VMEM((rows * PITCH, 128), F32),
        ],
        compiler_params=pltpu.CompilerParams(vmem_limit_bytes=VMEM_LIMIT),
        cost_estimate=pl.CostEstimate(flops=4 * 10**9, bytes_accessed=8 * 10**6, transcendentals=10**6),
    )(inbox, table, target, weight, left, right, wv, inside)


def adjoint_kernel(
    a_ref, table_ref, gs_ref, top_ref, bottom_ref, left_ref, right_ref, wv_ref, inside_ref,
    out_ref, x_ref, sw_ref, gh_ref, g_ref, acc_ref, tile_ref,
):
    rows, cols = out_ref.shape
    ext = rows + 2 * RAD
    x_ref[0:RAD, :] = jnp.where(inside_ref[0] > 0, top_ref[...], 0.0)
    x_ref[RAD : 2 * RAD, :] = jnp.where(inside_ref[1] > 0, bottom_ref[...], 0.0)

    def corners(ref, flag):
        first = jnp.where((inside_ref[flag] > 0) & (inside_ref[0] > 0), ref[0:RAD, :], 0.0)
        last = jnp.where((inside_ref[flag] > 0) & (inside_ref[1] > 0), ref[ext - RAD : ext, :], 0.0)
        return jnp.concatenate([first, last], axis=0)

    spread(x_ref, corners(left_ref, 2), corners(right_ref, 3), sw_ref, 2 * RAD, cols)
    fields = correlate(a_ref, [0, (rows + RAD) * PITCH], RAD * PITCH, table_ref)
    resist_and_gradient(fields, sw_ref[...], wv_ref[...], gh_ref, 0)

    for r in range(ext):
        for s in range(2):
            if r < RAD:
                source, at = gh_ref, r * PITCH + s
            elif r >= RAD + rows:
                source, at = gh_ref, (r - rows) * PITCH + s
            else:
                source, at = gs_ref, (r - RAD) * PITCH + s
            g_ref[s, r % 8, r // 8] = source[at : at + 16, :].astype(BF16)

    total = jnp.zeros((256, 256), F32)
    for i in range(40):
        for s in range(2):
            fields = g_ref[s, i % 8, i // 8 : i // 8 + 16].reshape(256, 256)
            taps = table_ref[39 - i : 47 - i, BLK * (1 - s) : BLK * (2 - s), :].reshape(256, 256)
            total = total + dot_nt(fields, taps)
    for h in range(2):
        acc_ref[h] = total[:, 128 * h : 128 * h + 128]
    for q in range(cols // 128):
        for h in range(2):
            per_block = [acc_ref[h, pl.ds(4 * q + j, 16, stride=16), :] for j in range(4)]
            for j in range(4):
                pieces = [x[:, BLK * j : BLK * j + BLK] for x in per_block]
                tile_ref[q, pl.ds(4 * h + j, 16, stride=8), :] = jnp.concatenate(pieces, axis=1)
        out_ref[:, 128 * q : 128 * q + 128] = tile_ref[q]


def adjoint(a, table, gs, top, bottom, left, right, wv, inside, rows, cols):
    ext = rows + 2 * RAD
    return pl.pallas_call(
        adjoint_kernel,
        out_shape=jax.ShapeDtypeStruct((rows, cols), F32),
        in_specs=[WHOLE] * 8 + [SMALL],
        scratch_shapes=[
            pltpu.VMEM((2 * RAD, cols), F32),
            pltpu.VMEM((2 * RAD * PITCH, 128), F32),
            pltpu.VMEM((2 * RAD * PITCH, 256), F32),
            pltpu.VMEM((2, 8, ext // 8, 16, 256), BF16),
            pltpu.VMEM((2, 256, 128), F32),
            pltpu.VMEM((cols // 128, rows, 128), F32),
        ],
        compiler_params=pltpu.CompilerParams(vmem_limit_bytes=VMEM_LIMIT),
        cost_estimate=pl.CostEstimate(flops=4 * 10**9, bytes_accessed=10**7, transcendentals=0),
    )(a, table, gs, top, bottom, left, right, wv, inside)


def shards(rects, owner, counts, target, loss_weight, kernel, socs_weight):
    row_devices = lax.axis_size("row")
    col_devices = lax.axis_size("col")
    devices = row_devices * col_devices
    rows, cols = target.shape
    outbox = make_outbox(rects, owner, counts, devices, col_devices)
    inbox = lax.all_to_all(outbox, ("row", "col"), split_axis=0, concat_axis=0, tiled=True)
    table = make_tables(kernel)
    top, bottom, left, right, inside = weight_strips(target, loss_weight)
    wv = jnp.repeat(socs_weight, 2 * BLK).reshape(1, 256)
    local, a, gs = imaging(inbox, table, target, loss_weight, left, right, wv, inside)
    losses = lax.all_to_all(local.reshape(devices), ("row", "col"), split_axis=0, concat_axis=0, tiled=True)
    mask_grad = adjoint(a, table, gs, top, bottom, left, right, wv, inside, rows, cols)
    window_area = rows * row_devices * cols * col_devices
    return (mask_grad, (jnp.sum(losses) / window_area).reshape(1))


def solution(mesh):
    placed = (
        P(None, ("row", "col")),
        P(("row", "col")),
        P(("row", "col")),
        P("row", "col"),
        P("row", "col"),
        P(),
        P(),
    )
    return jax.shard_map(
        shards, mesh=mesh, in_specs=placed, out_specs=(P("row", "col"), P()), check_vma=False
    )
```

time: 89 us -> 61.7 us (0.69)
  Pallas kernels: 33.7 us -> 19.7 us
  starting transfers between devices: 36.7 us -> 25.7 us
  local copies, waits for them, and re-layouts: 11.8 us -> 8.73 us
    pallas_call x4 -> x3, Pallas kernels: 31.6 us -> 17.7 us  [the longest x1 7.13 us: adjoint(): pl.pallas_call(adjoint_kernel, out_shape=jax.ShapeDtypeStruct((rows, cols...]
    ppermute x4, starting transfers between devices: 13.4 us -> 8.98 us  [beside(): return (lax.ppermute(last, axis, up), lax.ppermute(first, axis, down))]
    all_to_all x1, starting transfers between devices: 11.5 us -> 7.9 us  [shards(): lax.all_to_all(outbox, ('row', 'col'), split_axis=0, concat_axis=0, tiled...]
    all_to_all x1, starting transfers between devices: 11.8 us -> 8.78 us  [shards(): lax.all_to_all(local.reshape(devices), ('row', 'col'), split_axis=0, conc...]
    reshape x4 -> x2, local copies, waits for them, and re-layouts: 1.83 us -> 0.21 us  [the longest x1 0.11 us: make_tables(): taps = by_row[:, :, KS - 1:0:-1].reshape(KS, channels * BLK)]
    all_to_all x1, waiting for transfers between devices: 0.01 us -> 1.11 us  [shards(): lax.all_to_all(outbox, ('row', 'col'), split_axis=0, concat_axis=0, tiled...]
    select_n x1 -> x2, other arithmetic: 1.07 us -> 1.92 us  [signed(): return jnp.where(target[at] > 0, loss_weight[at], -loss_weight[at])]
  transfers between devices with their start and end apart: 6 -> 6, of which waited for: 2 -> 1; matrix products, arithmetic and copies ran while one was open for 6% -> 5% of each run, Pallas kernels for 24% -> 21%
where the time goes in v2:
time: 61.7 us; the launch traced here: 61.2 us
  starting transfers between devices  25.7 us (42%)
  Pallas kernels  19.7 us (32%)
  local copies, waits for them, and re-layouts  8.73 us (14%)
  between operations  3.23 us (5%)
  other arithmetic  2.76 us (4%)
  waiting for transfers between devices  1.12 us (2%)
    ppermute x4, starting transfers between devices, beside(): return (lax.ppermute(last, axis, up), lax.ppermute(first, axis, down))  8.98 us
    all_to_all x1, starting transfers between devices, shards(): lax.all_to_all(local.reshape(devices), ('row', 'col'), split_axis=0, conc...  8.78 us
    all_to_all x1, starting transfers between devices, shards(): lax.all_to_all(outbox, ('row', 'col'), split_axis=0, concat_axis=0, tiled...  7.9 us
    unnamed x15, local copies, waits for them, and re-layouts  7.14 us
    pallas_call x1, Pallas kernels, adjoint(): pl.pallas_call(adjoint_kernel, out_shape=jax.ShapeDtypeStruct((rows, cols...  7.13 us
    pallas_call x1, Pallas kernels, imaging(): pl.pallas_call(imaging_kernel, out_shape=(jax.ShapeDtypeStruct((1, 128),...  6.72 us
    pallas_call x1, Pallas kernels, make_tables(): pl.pallas_call(tables_kernel, out_shape=pltpu.VMEM((TABLE, 2 * BLK, chann...  3.87 us
    pallas_call x1, Pallas kernels, make_outbox(): pl.pallas_call(lambda *refs: outbox_kernel(tile_cols, *refs), out_shape=j...  2.01 us
  transfers between devices with their start and end apart: 6, of which 1 were waited for; matrix products, arithmetic and copies ran while one was open for 5% of the time, Pallas kernels for 21%

profile of v2, /device:TPU:1, one launch (start us, length us, event | category | flops | bytes accessed | tf_op | source)
XLA Modules:
  0.0 61.2 jit_solution(12361649676225749553)
XLA Ops:
  0.6 0.8 %negate_select_fusion.3 = (f32[16,512]{1,0:T(8,128)S(1)}, f32[16,512]{1,0:T(8,128)S(1)}) fusion(f32[128,512]{1,0:T(8,128)} %weight_ref.1, s32[128,512]{1,0:T(8,128)} %target_ref.1), kind=kLoop, calls=%fused_computation.8 | loop fusion | flops 49152 | bytes 196608 | tf_op jit(solution)/shard_map/jit(_where)/select_n | solution.py:118
  1.5 3.6 %collective-permute-start = (f32[16,512]{1,0:T(8,128)S(1)}, f32[16,512]{1,0:T(8,128)S(1)}, u32[]{:S(2)}, u32[]{:S(2)}) collective-permute-start(f32[16,512]{1,0:T(8,128)S(1)} %get-tuple-element.10), channel_id=1, source_target_pairs={{0,16},{16,32},{32,48},{48,64},{64,80},{80,96},{96,112},{112,0},{1... | collective-permute-start | bytes 98312 | tf_op jit(solution)/shard_map/ppermute | solution.py:124
  5.1 3.6 %collective-permute-start.1 = (f32[16,512]{1,0:T(8,128)S(1)}, f32[16,512]{1,0:T(8,128)S(1)}, u32[]{:S(2)}, u32[]{:S(2)}) collective-permute-start(f32[16,512]{1,0:T(8,128)S(1)} %get-tuple-element.11), channel_id=1, source_target_pairs={{16,0},{32,16},{48,32},{64,48},{80,64},{96,80},{112,96},{0,112},{1... | collective-permute-start | bytes 98312 | tf_op jit(solution)/shard_map/ppermute | solution.py:124
  9.3 2.0 %shard_map.86 = s32[128,2,128]{2,1,0:T(2,128)} custom-call(s32[1]{0:T(128)S(6)} %copy.30.refs_0_, s32[4,512]{1,0:T(4,128)} %refs_1_.1, s32[1,512]{1,0:T(1,128)} %bitcast.12), custom_call_target="tpu_custom_call" | custom-call | flops 100000000 | bytes 100000 | tf_op jit(solution)/shard_map/pallas_call | solution.py:69
  11.3 7.9 %all-to-all-start = ((s32[128,2,128]{2,1,0:T(2,128)}), s32[128,2,128]{2,1,0:T(2,128)S(1)}, u32[]{:S(2)}, u32[]{:S(2)}) async-start(s32[128,2,128]{2,1,0:T(2,128)} %shard_map.86), calls=%async_computation | async-start | bytes 262144 | tf_op jit(solution)/shard_map/all_to_all | solution.py:348
  19.3 1.1 %negate_select_fusion = (f32[128,16]{1,0:T(8,128)S(1)}, f32[128,16]{1,0:T(8,128)S(1)}) fusion(f32[128,512]{1,0:T(8,128)} %weight_ref.1, s32[128,512]{1,0:T(8,128)} %target_ref.1), kind=kLoop, calls=%fused_computation.1 | loop fusion | flops 12288 | bytes 49152 | tf_op jit(solution)/shard_map/jit(_where)/select_n | solution.py:118
  20.4 1.1 %copy.26 = bf16[8,33,33]{1,0,2:T(8,128)(2,1)S(1)} copy(bf16[8,33,33]{2,0,1:T(8,128)(2,1)} %param.12) | data formatting | bytes 34848 | tf_op args[5]
  21.6 1.7 %collective-permute-start.2 = (f32[160,16]{1,0:T(8,128)S(1)}, f32[160,16]{1,0:T(8,128)S(1)}, u32[]{:S(2)}, u32[]{:S(2)}) collective-permute-start(f32[160,16]{1,0:T(8,128)S(1)} %pad_maximum_fusion), channel_id=1, source_target_pairs={{0,1},{1,2},{2,3},{3,4},{4,5},{5,6},{6,7},{7,8},{8,9},{9,10},{10,1... | collective-permute-start | bytes 30728 | tf_op jit(solution)/shard_map/ppermute | solution.py:124
  23.7 0.1 copy.27
  23.9 0.1 reshape.21.taps_ref
  24.0 0.1 copy.28
  24.1 0.1 broadcast_in_dim.6
  24.1 0.1 reshape.22.edge_ref
  24.3 3.9 %shard_map.87.table_ref = bf16[47,64,256]{2,1,0:T(8,128)(2,1)S(1)} custom-call(f32[33,256]{1,0:T(8,128)S(1)} %reshape.21.taps_ref, f32[33,256]{1,0:T(8,128)S(1)} %reshape.22.edge_ref), custom_call_target="tpu_custom_call" | custom-call | flops 100000000 | bytes 1000000 | tf_op jit(solution)/shard_map/pallas_call | solution.py:106
  28.2 1.1 %all-to-all-done.inbox_ref = s32[128,2,128]{2,1,0:T(2,128)S(1)} async-done(((s32[128,2,128]{2,1,0:T(2,128)}), s32[128,2,128]{2,1,0:T(2,128)S(1)}, u32[]{:S(2)}, u32[]{:S(2)}) %all-to-all-start) | async-done | bytes 131104 | tf_op jit(solution)/shard_map/all_to_all | solution.py:348
  29.3 6.7 %shard_map.88 = (f32[1,128]{1,0:T(1,128)S(1)}, bf16[3840,256]{1,0:T(8,128)(2,1)S(1)}, f32[2560,256]{1,0:T(8,128)S(1)}) custom-call(s32[128,2,128]{2,1,0:T(2,128)S(1)} %all-to-all-done.inbox_ref, bf16[47,64,256]{2,1,0:T(8,128)(2,1)S(1)} %shard_map.87.table_ref, s32[128,512]{1,0:T(8,128)S(1)} %copy-done, f32[128,512]{1,0:T(8,128)S(1)} %copy-done.1, ...), custom_call_target="tpu_custom_call" | custom-call | flops 4000000000 | bytes 8000000 | tf_op jit(solution)/shard_map/pallas_call | solution.py:259
  36.0 1.5 %copy-done.2 = f32[2560,256]{1,0:T(8,128)} copy-done((f32[2560,256]{1,0:T(8,128)}, f32[2560,256]{1,0:T(8,128)S(1)}, u32[]{:S(2)}) %copy-start.2) | copy-done | bytes 2621464
  37.5 1.3 %copy-done.4 = bf16[3840,256]{1,0:T(8,128)(2,1)} copy-done((bf16[3840,256]{1,0:T(8,128)(2,1)}, bf16[3840,256]{1,0:T(8,128)(2,1)S(1)}, u32[]{:S(2)}) %copy-start.4) | copy-done | bytes 1966104
  38.8 0.7 %copy.29 = f32[128,1,1]{2,1,0:T(1,128)} copy(f32[128,1,1]{0,2,1:T(1,128)S(1)} %bitcast.11) | data formatting | bytes 1024 | tf_op jit(solution)/shard_map/all_to_all | solution.py:353
  39.5 8.8 %all-to-all-start.1 = ((f32[128,1,1]{2,1,0:T(1,128)}), f32[128,1,1]{2,1,0:T(1,128)S(1)}, u32[]{:S(2)}, u32[]{:S(2)}) async-start(f32[128,1,1]{2,1,0:T(1,128)} %copy.29), calls=%async_computation.1 | async-start | bytes 131072 | tf_op jit(solution)/shard_map/all_to_all | solution.py:353
  48.3 1.7 %copy-done.3 = f32[2560,256]{1,0:T(8,128)S(1)} copy-done((f32[2560,256]{1,0:T(8,128)S(1)}, f32[2560,256]{1,0:T(8,128)}, u32[]{:S(2)}) %copy-start.3) | copy-done | bytes 2621464
  50.0 1.5 %copy-done.5 = bf16[3840,256]{1,0:T(8,128)(2,1)S(1)} copy-done((bf16[3840,256]{1,0:T(8,128)(2,1)S(1)}, bf16[3840,256]{1,0:T(8,128)(2,1)}, u32[]{:S(2)}) %copy-start.5) | copy-done | bytes 1966104
  51.6 7.1 %shard_map.89 = f32[128,512]{1,0:T(8,128)} custom-call(bf16[3840,256]{1,0:T(8,128)(2,1)S(1)} %copy-done.5, bf16[47,64,256]{2,1,0:T(8,128)(2,1)S(1)} %shard_map.87.table_ref, f32[2560,256]{1,0:T(8,128)S(1)} %copy-done.3, f32[16,512]{1,0:T(8,128)S(1)} %collective-permute-done.top_ref, f32[16,512]{1,0:T(8,128)S(1)} %collective-permute-done.1.bottom_ref, ...), custom_call_target="tpu_custom_call" | custom-call | flops 4000000000 | bytes 10000000 | tf_op jit(solution)/shard_map/pallas_call | solution.py:325
  58.7 0.7 %reduce_sum.9 = f32[]{:T(128)} reduce(f32[128,1,1]{2,1,0:T(1,128)S(1)} %all-to-all-done.1, f32[]{:T(128)} %constant.20.clone.1), dimensions={0,1,2}, to_apply=%region_0.1 | reduce | flops 127 | bytes 520 | tf_op jit(solution)/shard_map/reduce_sum | solution.py:356
  (27 shorter events, 0.5 us)
Async XLA Ops:
  0.6 22.9 %copy-start.6 = (f32[4]{0:T(128)S(1)}, f32[4]{0:T(128)}, u32[]{:S(2)}) copy-start(f32[4]{0:T(128)} %param.13) | copy-start | bytes 52
  1.5 20.0 %collective-permute-start = (f32[16,512]{1,0:T(8,128)S(1)}, f32[16,512]{1,0:T(8,128)S(1)}, u32[]{:S(2)}, u32[]{:S(2)}) collective-permute-start(f32[16,512]{1,0:T(8,128)S(1)} %get-tuple-element.10), channel_id=1, source_target_pairs={{0,16},{16,32},{32,48},{48,64},{64,80},{80,96},{96,112},{112,0},{1... | collective-permute-start | bytes 98312 | tf_op jit(solution)/shard_map/ppermute | solution.py:124
  5.1 16.4 %collective-permute-start.1 = (f32[16,512]{1,0:T(8,128)S(1)}, f32[16,512]{1,0:T(8,128)S(1)}, u32[]{:S(2)}, u32[]{:S(2)}) collective-permute-start(f32[16,512]{1,0:T(8,128)S(1)} %get-tuple-element.11), channel_id=1, source_target_pairs={{16,0},{32,16},{48,32},{64,48},{80,64},{96,80},{112,96},{0,112},{1... | collective-permute-start | bytes 98312 | tf_op jit(solution)/shard_map/ppermute | solution.py:124
  11.3 17.9 %all-to-all-start = ((s32[128,2,128]{2,1,0:T(2,128)}), s32[128,2,128]{2,1,0:T(2,128)S(1)}, u32[]{:S(2)}, u32[]{:S(2)}) async-start(s32[128,2,128]{2,1,0:T(2,128)} %shard_map.86), calls=%async_computation | async-start | bytes 262144 | tf_op jit(solution)/shard_map/all_to_all | solution.py:348
  19.2 10.0 %copy-start = (s32[128,512]{1,0:T(8,128)S(1)}, s32[128,512]{1,0:T(8,128)}, u32[]{:S(2)}) copy-start(s32[128,512]{1,0:T(8,128)} %target_ref.1) | copy-start | bytes 786436
  19.3 10.0 %copy-start.1 = (f32[128,512]{1,0:T(8,128)S(1)}, f32[128,512]{1,0:T(8,128)}, u32[]{:S(2)}) copy-start(f32[128,512]{1,0:T(8,128)} %weight_ref.1) | copy-start | bytes 786436
  21.6 6.5 %collective-permute-start.2 = (f32[160,16]{1,0:T(8,128)S(1)}, f32[160,16]{1,0:T(8,128)S(1)}, u32[]{:S(2)}, u32[]{:S(2)}) collective-permute-start(f32[160,16]{1,0:T(8,128)S(1)} %pad_maximum_fusion), channel_id=1, source_target_pairs={{0,1},{1,2},{2,3},{3,4},{4,5},{5,6},{6,7},{7,8},{8,9},{9,10},{10,1... | collective-permute-start | bytes 30728 | tf_op jit(solution)/shard_map/ppermute | solution.py:124
  23.3 4.8 %collective-permute-start.3 = (f32[160,16]{1,0:T(8,128)S(1)}, f32[160,16]{1,0:T(8,128)S(1)}, u32[]{:S(2)}, u32[]{:S(2)}) collective-permute-start(f32[160,16]{1,0:T(8,128)S(1)} %pad_maximum_fusion.1), channel_id=1, source_target_pairs={{1,0},{2,1},{3,2},{4,3},{5,4},{6,5},{7,6},{8,7},{9,8},{10,9},{11,1... | collective-permute-start | bytes 30728 | tf_op jit(solution)/shard_map/ppermute | solution.py:124
  36.0 1.5 %copy-start.2 = (f32[2560,256]{1,0:T(8,128)}, f32[2560,256]{1,0:T(8,128)S(1)}, u32[]{:S(2)}) copy-start(f32[2560,256]{1,0:T(8,128)S(1)} %get-tuple-element.6.gs_ref) | copy-start | bytes 7864324
  37.5 1.3 %copy-start.4 = (bf16[3840,256]{1,0:T(8,128)(2,1)}, bf16[3840,256]{1,0:T(8,128)(2,1)S(1)}, u32[]{:S(2)}) copy-start(bf16[3840,256]{1,0:T(8,128)(2,1)S(1)} %get-tuple-element.5.a_ref) | copy-start | bytes 5898244
  39.5 19.2 %all-to-all-start.1 = ((f32[128,1,1]{2,1,0:T(1,128)}), f32[128,1,1]{2,1,0:T(1,128)S(1)}, u32[]{:S(2)}, u32[]{:S(2)}) async-start(f32[128,1,1]{2,1,0:T(1,128)} %copy.29), calls=%async_computation.1 | async-start | bytes 131072 | tf_op jit(solution)/shard_map/all_to_all | solution.py:353
  48.3 1.7 %copy-start.3 = (f32[2560,256]{1,0:T(8,128)S(1)}, f32[2560,256]{1,0:T(8,128)}, u32[]{:S(2)}) copy-start(f32[2560,256]{1,0:T(8,128)} %copy-done.2) | copy-start | bytes 7864324
  50.0 1.5 %copy-start.5 = (bf16[3840,256]{1,0:T(8,128)(2,1)S(1)}, bf16[3840,256]{1,0:T(8,128)(2,1)}, u32[]{:S(2)}) copy-start(bf16[3840,256]{1,0:T(8,128)(2,1)} %copy-done.4) | copy-start | bytes 5898244

commit v3 on v2

v3 whole, which is shorter than its diff:
```python
import jax
import jax.numpy as jnp
from jax import lax
from jax.experimental import pallas as pl
from jax.experimental.pallas import tpu as pltpu
from jax.sharding import PartitionSpec as P

RAD = 16
CAP = 8
KS = 33
BLK = 32
AROWS = 36
LEAD = 7
TABLE = 47
WIDE = 2 * BLK + 1
PITCH = 20
NEIGHBOURS = [(dr, dc) for dr in (-1, 0, 1) for dc in (-1, 0, 1) if (dr, dc) != (0, 0)]
F32 = jnp.float32
BF16 = jnp.bfloat16
VMEM_LIMIT = 32 * 1024 * 1024


def dot_nt(a, b):
    return lax.dot_general(a, b, (((1,), (1,)), ((), ())), preferred_element_type=F32)


def iota(shape, dim):
    return lax.broadcasted_iota(jnp.int32, shape, dim)


def outbox_kernel(
    tile_cols, counts_ref, rects_ref, owner_ref, target_ref, weight_ref,
    out_ref, signed_ref, top_ref, bottom_ref, left_ref, right_ref,
    pad_ref, target_buf, weight_buf, sems,
):
    rows, cols = signed_ref.shape
    load_target = pltpu.make_async_copy(target_ref, target_buf, sems.at[0])
    load_weight = pltpu.make_async_copy(weight_ref, weight_buf, sems.at[1])
    load_target.start()
    load_weight.start()
    slots = owner_ref.shape[1]
    tiles = out_ref.shape[0]
    live = iota((1, slots), 1) < counts_ref[0]
    own = jnp.where(live, owner_ref[...], -1)
    hit = iota((tiles, slots), 0) == own
    hits = jnp.where(hit, 1.0, 0.0).astype(BF16)
    before = jnp.where(iota((slots, slots), 0) < iota((slots, slots), 1), 1.0, 0.0).astype(BF16)
    earlier = jnp.dot(hits, before, preferred_element_type=F32)
    rank = jnp.sum(jnp.where(hit, earlier, 0.0), axis=0, keepdims=True).astype(jnp.int32)
    row = iota((16, slots), 0)
    chosen = rank == (row & 7)
    vertical = (row & 8) == 8

    def placed(first, second):
        value = jnp.where(vertical, second, first)
        value = jnp.where(chosen, value, 0)
        high = (value >> 4).astype(F32).astype(BF16)
        low = (value & 15).astype(F32).astype(BF16)
        return (16.0 * dot_nt(hits, high) + dot_nt(hits, low)).astype(jnp.int32)

    lower = placed(rects_ref[0:1, :], rects_ref[2:3, :])
    upper = placed(rects_ref[1:2, :], rects_ref[3:4, :])
    word = lower + (upper << 16)
    word = jnp.concatenate([word] * 8, axis=1)
    pad_ref[...] = jnp.zeros(pad_ref.shape, jnp.int32)
    pad_ref[24 : 24 + tiles, :] = word
    column = iota((tiles, 128), 0) % tile_cols
    group = iota((tiles, 128), 1) >> 4
    result = jnp.zeros((tiles, 128), jnp.int32)
    for n, (dr, dc) in enumerate(NEIGHBOURS):
        start = 24 + dr * tile_cols + dc
        inside = (column + dc >= 0) & (column + dc < tile_cols) & (group == n)
        result = jnp.where(inside, pad_ref[start : start + tiles, :], result)
    out_ref[:, 0, :] = result
    out_ref[:, 1, :] = word
    load_target.wait()
    load_weight.wait()
    signed_ref[...] = jnp.where(target_buf[...] > 0, weight_buf[...], -weight_buf[...])
    top_ref[...] = signed_ref[0:RAD, :]
    bottom_ref[...] = signed_ref[rows - RAD : rows, :]
    left_ref[...] = signed_ref[:, 0:RAD]
    right_ref[...] = signed_ref[:, cols - RAD : cols]


SMALL = pl.BlockSpec(memory_space=pltpu.SMEM)
WHOLE = pl.BlockSpec(memory_space=pltpu.VMEM)
ANYWHERE = pl.BlockSpec(memory_space=pl.ANY)


def make_outbox(rects, owner, counts, target, weight, tiles, tile_cols):
    slots = owner.shape[0]
    rows, cols = target.shape
    return pl.pallas_call(
        lambda *refs: outbox_kernel(tile_cols, *refs),
        out_shape=(
            pltpu.VMEM((tiles, 2, 128), jnp.int32),
            pltpu.VMEM((rows, cols), F32),
            pltpu.VMEM((RAD, cols), F32),
            pltpu.VMEM((RAD, cols), F32),
            pltpu.VMEM((rows, RAD), F32),
            pltpu.VMEM((rows, RAD), F32),
        ),
        in_specs=[SMALL, WHOLE, WHOLE, ANYWHERE, ANYWHERE],
        scratch_shapes=[
            pltpu.VMEM((tiles + 48, 128), jnp.int32),
            pltpu.VMEM((rows, cols), jnp.int32),
            pltpu.VMEM((rows, cols), F32),
            pltpu.SemaphoreType.DMA((2,)),
        ],
        cost_estimate=pl.CostEstimate(flops=10**8, bytes_accessed=10**6, transcendentals=0),
    )(counts, rects, owner.reshape(1, slots), target, weight)


def tables_kernel(kernel_ref, table_ref, wide_ref):
    channels = kernel_ref.shape[0]
    lanes = channels * BLK
    tap, lane = iota((KS, lanes), 0), iota((KS, lanes), 1)
    taps = jnp.zeros((KS, lanes), F32)
    edge = jnp.zeros((KS, lanes), F32)
    for c in range(channels):
        mine = lane // BLK == c
        reverse = jnp.where(mine & (tap == KS - 1 - lane % BLK), 1.0, 0.0).astype(BF16)
        first = jnp.where(mine & (tap == 0), 1.0, 0.0).astype(BF16)
        taps = taps + jnp.dot(kernel_ref[c], reverse, preferred_element_type=F32)
        edge = edge + jnp.dot(kernel_ref[c], first, preferred_element_type=F32)
    co = iota((KS, 128), 1) % BLK
    for p in range(BLK):
        for h in range(lanes // 128):
            mine = taps[:, 128 * h : 128 * h + 128]
            ends = edge[:, 128 * h : 128 * h + 128]
            near = pltpu.roll(mine, p, 1) if p else mine
            far = pltpu.roll(mine, p + 128 - BLK, 1)
            far = jnp.where(co < p, far, jnp.where(co == p, ends, 0.0))
            wide_ref[h, pl.ds(p, KS, stride=WIDE), :] = far
            wide_ref[h, pl.ds(BLK + p, KS, stride=WIDE), :] = jnp.where(co >= p, near, 0.0)
    zero = jnp.zeros((2 * BLK, lanes), BF16)
    for a in range(TABLE):
        if a < LEAD or a >= LEAD + KS:
            table_ref[a] = zero
            continue
        at = (a - LEAD) * WIDE
        for h in range(lanes // 128):
            table_ref[a, :, 128 * h : 128 * h + 128] = wide_ref[h, at : at + 2 * BLK, :].astype(BF16)


def make_tables(kernel):
    lanes = kernel.shape[0] * BLK
    return pl.pallas_call(
        tables_kernel,
        out_shape=pltpu.VMEM((TABLE, 2 * BLK, lanes), BF16),
        in_specs=[WHOLE],
        scratch_shapes=[pltpu.VMEM((lanes // 128, KS * WIDE + 8, 128), F32)],
        compiler_params=pltpu.CompilerParams(vmem_limit_bytes=VMEM_LIMIT // 2),
        cost_estimate=pl.CostEstimate(flops=10**8, bytes_accessed=10**6, transcendentals=0),
    )(kernel)


def weight_strips(top_rows, bottom_rows, left_cols, right_cols):
    def beside(first, last, axis):
        count = lax.axis_size(axis)
        up = [(i, (i + 1) % count) for i in range(count)]
        down = [(j, i) for i, j in up]
        return lax.ppermute(last, axis, up), lax.ppermute(first, axis, down)

    left, right = beside(left_cols, right_cols, "col")
    last = right.shape[0] - RAD
    top, bottom = beside(
        jnp.concatenate([top_rows, right[:RAD], left[:RAD]], axis=1),
        jnp.concatenate([bottom_rows, right[last:], left[last:]], axis=1),
        "row",
    )
    r, c = lax.axis_index("row"), lax.axis_index("col")
    inside = jnp.stack([r > 0, r < lax.axis_size("row") - 1, c > 0, c < lax.axis_size("col") - 1])
    return top, bottom, left, right, inside.astype(jnp.int32)


def spread(x_ref, left, right, out_ref, rows, cols):
    for b in range(cols // BLK + 1):
        if b == 0:
            piece = jnp.concatenate([left, x_ref[:, 0:RAD]], axis=1)
        elif b == cols // BLK:
            piece = jnp.concatenate([x_ref[:, cols - RAD : cols], right], axis=1)
        else:
            piece = x_ref[:, BLK * b - RAD : BLK * b + RAD]
        out_ref[pl.ds(b, rows, stride=PITCH), :] = jnp.concatenate([piece] * 4, axis=1)
    for b in range(cols // BLK + 1, PITCH):
        out_ref[pl.ds(b, rows, stride=PITCH), :] = jnp.zeros((rows, 128), F32)


def channel_weights(socs_ref):
    k = iota((1, 256), 1) // (2 * BLK)
    wv = jnp.zeros((1, 256), F32)
    for i in range(4):
        wv = jnp.where(k == i, socs_ref[i], wv)
    return wv


def windows(mask, s_ref, first, cols):
    count = mask.shape[0]
    for b in range(cols // BLK + 1):
        if b == 0:
            window = jnp.concatenate([mask[:, cols + BLK : cols + 2 * BLK], mask[:, 0:BLK]], axis=1)
        else:
            window = mask[:, BLK * (b - 1) : BLK * (b + 1)]
        s_ref[pl.ds(first * PITCH + b, count, stride=PITCH), :] = jnp.concatenate([window, window], axis=1)


def four_rows(s_ref, a_ref, start, end, step):
    first_half = iota((step, 128), 1) < 64
    for m in range(start, end, step):
        for h in range(2):
            even = s_ref[m + 2 * h * PITCH : m + 2 * h * PITCH + step, :]
            odd = s_ref[m + (2 * h + 1) * PITCH : m + (2 * h + 1) * PITCH + step, :]
            a_ref[m : m + step, 128 * h : 128 * h + 128] = jnp.where(first_half, even, odd).astype(BF16)


def correlate(a_ref, starts, count, table_ref):
    fields = None
    for g in range(AROWS // 4):
        parts = [a_ref[m + 4 * PITCH * g : m + 4 * PITCH * g + count, :] for m in starts]
        left = parts[0] if len(parts) == 1 else jnp.concatenate(parts, axis=0)
        right = table_ref[LEAD + 4 * g : LEAD + 4 * g + 4].reshape(8 * BLK, 256)
        term = jnp.dot(left, right, preferred_element_type=F32)
        fields = term if fields is None else fields + term
    return fields


def resist_and_gradient(fields, signed, wv, gs_ref, at):
    square = fields * fields * wv
    intensity = square[:, :128] + square[:, 128:]
    intensity = intensity + pltpu.roll(intensity, 64, 1)
    intensity = intensity + pltpu.roll(intensity, 32, 1)
    resist = 1.0 / (1.0 + jnp.exp(3.0 - intensity))
    slope = 2.0 * (jnp.abs(signed) * resist - jnp.maximum(signed, 0.0)) * resist * (1.0 - resist)
    for h in range(2):
        lanes = slice(128 * h, 128 * h + 128)
        value = (2.0 * wv[:, lanes]) * fields[:, lanes] * slope
        gs_ref[at : at + fields.shape[0], lanes] = value.astype(gs_ref.dtype)
    return resist


def imaging_kernel(
    inbox_ref, table_ref, signed_ref, left_ref, right_ref, socs_ref, inside_ref,
    loss_ref, edges_ref, gs_ref, mask_ref, s_ref, a_ref, sw_ref,
):
    rows, cols = signed_ref.shape
    halo = 2 * RAD
    tall = rows + 2 * halo
    words = [inbox_ref[:, 0, :].T, inbox_ref[:, 1, :].T]
    lower = [(x & 0xFFFF).astype(F32) * 0.25 for x in words]
    upper = [(x >> 16).astype(F32) * 0.25 for x in words]
    cell = iota((BLK, 128), 0).astype(F32).astype(BF16)
    cell_end = (iota((BLK, 128), 0) + 1).astype(F32).astype(BF16)

    def covers(group, at, first, count):
        low8, high8 = lower[group][at : at + CAP, :], upper[group][at : at + CAP, :]
        stacked = []
        for base in range(first, first + count, BLK):
            low = jnp.clip(low8 - float(base), 0.0, float(BLK))
            high = jnp.clip(high8 - float(base), 0.0, float(BLK))
            parts = []
            for rank in range(CAP):
                lo = jnp.broadcast_to(low[rank : rank + 1, :], (BLK, 128)).astype(BF16)
                hi = jnp.broadcast_to(high[rank : rank + 1, :], (BLK, 128)).astype(BF16)
                parts.append(jnp.maximum(jnp.minimum(hi, cell_end) - jnp.maximum(lo, cell), 0.0))
            stacked.append(jnp.concatenate(parts, axis=1))
        return stacked[0] if len(stacked) == 1 else jnp.concatenate(stacked, axis=0)

    row_span = {-1: (rows - halo, halo, 0), 0: (0, rows, halo), 1: (0, halo, halo + rows)}
    col_span = {-1: (cols - halo, halo, cols + halo), 0: (0, cols, 0), 1: (0, halo, cols)}
    for n, (dr, dc) in enumerate(NEIGHBOURS + [(0, 0)]):
        group, at = (1, 0) if n == 8 else (0, 16 * n)
        r_first, r_count, r_at = row_span[dr]
        c_first, c_count, c_at = col_span[dc]
        row_cover = covers(group, at + 8, r_first, r_count)
        col_cover = covers(group, at, c_first, c_count)
        part = dot_nt(row_cover, col_cover).astype(BF16).astype(F32)
        mask_ref[r_at : r_at + r_count, c_at : c_at + c_count] = part

    edges_ref[0:64, :] = mask_ref[0:64, :].astype(BF16)
    edges_ref[64:112, :] = mask_ref[tall - 48 : tall, :].astype(BF16)
    s_ref[...] = jnp.zeros(s_ref.shape, F32)
    windows(mask_ref[...], s_ref, 0, cols)
    four_rows(s_ref, a_ref, RAD * PITCH, (tall - RAD) * PITCH, 16 * PITCH)
    left = jnp.where(inside_ref[2] > 0, left_ref[...], 0.0)
    right = jnp.where(inside_ref[3] > 0, right_ref[...], 0.0)
    spread(signed_ref, left, right, sw_ref, rows, cols)

    wv = channel_weights(socs_ref)
    chunk = rows // 4 * PITCH
    block = iota((chunk, 128), 0) % PITCH
    co = iota((chunk, 128), 1) & (BLK - 1)
    own = ((block > 0) | (co >= RAD)) & ((block < cols // BLK) | (co < RAD)) & (block <= cols // BLK)
    total = jnp.zeros((1, 128), F32)
    for k in range(4):
        m = k * chunk
        fields = correlate(a_ref, [RAD * PITCH + m], chunk, table_ref)
        signed = sw_ref[m : m + chunk, :]
        resist = resist_and_gradient(fields, signed, wv, gs_ref, m)
        miss = resist - jnp.where(signed > 0.0, 1.0, 0.0)
        part = jnp.where(own, jnp.abs(signed), 0.0) * miss * miss
        total = total + jnp.sum(part, axis=0, keepdims=True)
    total = 0.25 * jnp.sum(total, axis=1, keepdims=True)
    loss_ref[...] = jnp.broadcast_to(total, loss_ref.shape)


def imaging(inbox, table, signed, left, right, socs_weight, inside, devices):
    rows, cols = signed.shape
    tall = rows + 4 * RAD
    return pl.pallas_call(
        imaging_kernel,
        out_shape=(
            pltpu.VMEM((devices, 1, 128), F32),
            pltpu.VMEM((112, cols + 128), BF16),
            pltpu.VMEM((rows * PITCH, 256), BF16),
        ),
        in_specs=[WHOLE] * 5 + [SMALL] * 2,
        scratch_shapes=[
            pltpu.VMEM((tall, cols + 128), F32),
            pltpu.VMEM(((tall + 4) * PITCH, 128), F32),
            pltpu.VMEM((tall * PITCH, 256), BF16),
            pltpu.VMEM((rows * PITCH, 128), F32),
        ],
        compiler_params=pltpu.CompilerParams(vmem_limit_bytes=VMEM_LIMIT),
        cost_estimate=pl.CostEstimate(flops=4 * 10**9, bytes_accessed=8 * 10**6, transcendentals=10**6),
    )(inbox, table, signed, left, right, socs_weight, inside)


def adjoint_kernel(
    edges_ref, table_ref, gs_ref, top_ref, bottom_ref, socs_ref, inside_ref,
    out_ref, s_ref, a_ref, x_ref, sw_ref, gw_ref, g_ref, acc_ref, tile_ref,
):
    rows, cols = out_ref.shape
    ext = rows + 2 * RAD
    x_ref[0:RAD, :] = jnp.where(inside_ref[0] > 0, top_ref[...], 0.0)
    x_ref[RAD : 2 * RAD, :] = jnp.where(inside_ref[1] > 0, bottom_ref[...], 0.0)
    left = jnp.where(inside_ref[2] > 0, x_ref[:, cols + RAD : cols + 2 * RAD], 0.0)
    right = jnp.where(inside_ref[3] > 0, x_ref[:, cols : cols + RAD], 0.0)
    spread(x_ref, left, right, sw_ref, 2 * RAD, cols)
    s_ref[...] = jnp.zeros(s_ref.shape, F32)
    windows(edges_ref[0:64, :].astype(F32), s_ref, 0, cols)
    windows(edges_ref[64:112, :].astype(F32), s_ref, 64, cols)
    four_rows(s_ref, a_ref, 0, 48 * PITCH, 16 * PITCH)
    four_rows(s_ref, a_ref, 64 * PITCH, 112 * PITCH, 16 * PITCH)
    fields = correlate(a_ref, [0, 64 * PITCH], RAD * PITCH, table_ref)
    resist_and_gradient(fields, sw_ref[...], channel_weights(socs_ref), gw_ref, 0)
    gw_ref[2 * RAD * PITCH :, :] = gs_ref[...].astype(F32)

    for r in range(ext):
        for s in range(2):
            if r < RAD:
                row = r
            elif r >= RAD + rows:
                row = r - rows
            else:
                row = r + RAD
            at = row * PITCH + s
            g_ref[s, r % 8, r // 8] = gw_ref[at : at + 16, :].astype(BF16)

    total = jnp.zeros((256, 256), F32)
    for i in range(40):
        for s in range(2):
            fields = g_ref[s, i % 8, i // 8 : i // 8 + 16].reshape(256, 256)
            taps = table_ref[39 - i : 47 - i, BLK * (1 - s) : BLK * (2 - s), :].reshape(256, 256)
            total = total + dot_nt(fields, taps)
    for h in range(2):
        acc_ref[h] = total[:, 128 * h : 128 * h + 128]
    for q in range(cols // 128):
        for h in range(2):
            per_block = [acc_ref[h, pl.ds(4 * q + j, 16, stride=16), :] for j in range(4)]
            for j in range(4):
                pieces = [x[:, BLK * j : BLK * j + BLK] for x in per_block]
                tile_ref[q, pl.ds(4 * h + j, 16, stride=8), :] = jnp.concatenate(pieces, axis=1)
        out_ref[:, 128 * q : 128 * q + 128] = tile_ref[q]


def adjoint(edges, table, gs, top, bottom, socs_weight, inside, rows, cols):
    ext = rows + 2 * RAD
    return pl.pallas_call(
        adjoint_kernel,
        out_shape=jax.ShapeDtypeStruct((rows, cols), F32),
        in_specs=[WHOLE] * 5 + [SMALL] * 2,
        scratch_shapes=[
            pltpu.VMEM((116 * PITCH, 128), F32),
            pltpu.VMEM((112 * PITCH, 256), BF16),
            pltpu.VMEM((2 * RAD, cols + 2 * RAD), F32),
            pltpu.VMEM((2 * RAD * PITCH, 128), F32),
            pltpu.VMEM((ext * PITCH, 256), F32),
            pltpu.VMEM((2, 8, ext // 8, 16, 256), BF16),
            pltpu.VMEM((2, 256, 128), F32),
            pltpu.VMEM((cols // 128, rows, 128), F32),
        ],
        compiler_params=pltpu.CompilerParams(vmem_limit_bytes=VMEM_LIMIT),
        cost_estimate=pl.CostEstimate(flops=4 * 10**9, bytes_accessed=10**7, transcendentals=0),
    )(edges, table, gs, top, bottom, socs_weight, inside)


def shards(rects, owner, counts, target, loss_weight, kernel, socs_weight):
    row_devices = lax.axis_size("row")
    col_devices = lax.axis_size("col")
    devices = row_devices * col_devices
    rows, cols = target.shape
    outbox, signed, *strips = make_outbox(rects, owner, counts, target, loss_weight, devices, col_devices)
    inbox = lax.all_to_all(outbox, ("row", "col"), split_axis=0, concat_axis=0, tiled=True)
    table = make_tables(kernel)
    top, bottom, left, right, inside = weight_strips(*strips)
    local, edges, gs = imaging(inbox, table, signed, left, right, socs_weight, inside, devices)
    losses = lax.all_to_all(local, ("row", "col"), split_axis=0, concat_axis=0, tiled=True)
    mask_grad = adjoint(edges, table, gs, top, bottom, socs_weight, inside, rows, cols)
    window_area = rows * row_devices * cols * col_devices
    return (mask_grad, (jnp.sum(losses[:, 0, 0]) / window_area).reshape(1))


def solution(mesh):
    placed = (
        P(None, ("row", "col")),
        P(("row", "col")),
        P(("row", "col")),
        P("row", "col"),
        P("row", "col"),
        P(),
        P(),
    )
    return jax.shard_map(
        shards, mesh=mesh, in_specs=placed, out_specs=(P("row", "col"), P()), check_vma=False
    )
```

time: 61.7 us -> 53.7 us (0.87)
  local copies, waits for them, and re-layouts: 8.73 us -> 3.3 us
  waiting for transfers between devices: 1.12 us -> 3.02 us
  other arithmetic: 2.76 us -> 0.97 us
  Pallas kernels: 19.7 us -> 18.2 us
  starting transfers between devices: 25.7 us -> 24.7 us
    unnamed x15 -> x7, local copies, waits for them, and re-layouts: 7.14 us -> 3.3 us
    all_to_all x1, starting transfers between devices: 8.78 us -> 5.67 us  [shards(): lax.all_to_all(local, ('row', 'col'), split_axis=0, concat_axis=0, tiled=...]
    all_to_all x1, starting transfers between devices: 7.9 us -> 10.6 us  [shards(): lax.all_to_all(outbox, ('row', 'col'), split_axis=0, concat_axis=0, tiled...]
    select_n x2 -> x0, other arithmetic: 1.92 us -> none  [signed(): return jnp.where(target[at] > 0, loss_weight[at], -loss_weight[at])]
    pallas_call x3, Pallas kernels: 12.6 us -> 11 us  [the longest x1 7.37 us: imaging(): pl.pallas_call(imaging_kernel, out_shape=(pltpu.VMEM((devices, 1, 128), F...]
    all_to_all x1, waiting for transfers between devices: 0.01 us -> 1.09 us  [shards(): lax.all_to_all(local, ('row', 'col'), split_axis=0, concat_axis=0, tiled=...]
    all_to_all x1, waiting for transfers between devices: 1.11 us -> 1.91 us  [shards(): lax.all_to_all(outbox, ('row', 'col'), split_axis=0, concat_axis=0, tiled...]
    all_to_all x1 -> x0, local copies, waits for them, and re-layouts: 0.73 us -> none  [shards(): lax.all_to_all(local.reshape(devices), ('row', 'col'), split_axis=0, conc...]
  transfers between devices with their start and end apart: 6 -> 6, of which waited for: 1 -> 2; matrix products, arithmetic and copies ran while one was open for 5% -> 2% of each run, Pallas kernels for 21% -> 29%
where the time goes in v3:
time: 53.7 us; the launch traced here: 53.4 us
  starting transfers between devices  24.7 us (46%)
  Pallas kernels  18.2 us (34%)
  local copies, waits for them, and re-layouts  3.3 us (6%)
  between operations  3.19 us (6%)
  waiting for transfers between devices  3.02 us (6%)
  other arithmetic  0.97 us (2%)
    all_to_all x1, starting transfers between devices, shards(): lax.all_to_all(outbox, ('row', 'col'), split_axis=0, concat_axis=0, tiled...  10.6 us
    ppermute x4, starting transfers between devices, beside(): return (lax.ppermute(last, axis, up), lax.ppermute(first, axis, down))  8.48 us
    pallas_call x1, Pallas kernels, imaging(): pl.pallas_call(imaging_kernel, out_shape=(pltpu.VMEM((devices, 1, 128), F...  7.37 us
    pallas_call x1, Pallas kernels, adjoint(): pl.pallas_call(adjoint_kernel, out_shape=jax.ShapeDtypeStruct((rows, cols...  7.17 us
    all_to_all x1, starting transfers between devices, shards(): lax.all_to_all(local, ('row', 'col'), split_axis=0, concat_axis=0, tiled=...  5.67 us
    unnamed x7, local copies, waits for them, and re-layouts  3.3 us
    pallas_call x1, Pallas kernels, make_outbox(): pl.pallas_call(lambda *refs: outbox_kernel(tile_cols, *refs), out_shape=(...  2.45 us
    all_to_all x1, waiting for transfers between devices, shards(): lax.all_to_all(outbox, ('row', 'col'), split_axis=0, concat_axis=0, tiled...  1.91 us
  transfers between devices with their start and end apart: 6, of which 2 were waited for; matrix products, arithmetic and copies ran while one was open for 2% of the time, Pallas kernels for 29%

profile of v3, /device:TPU:1, one launch (start us, length us, event | category | flops | bytes accessed | tf_op | source)
XLA Modules:
  0.0 53.4 jit_solution(795710833113319149)
XLA Ops:
  0.6 0.0 copy-start
  1.3 2.4 %shard_map.86 = (s32[128,2,128]{2,1,0:T(2,128)}, f32[128,512]{1,0:T(8,128)S(1)}, f32[16,512]{1,0:T(8,128)S(1)}, f32[16,512]{1,0:T(8,128)S(1)}, f32[128,16]{1,0:T(8,128)S(1)}, /*index=5*/f32[128,16]{1,0:T(8,128)S(1)}) custom-call(s32[1]{0:T(128)S(6)} %copy.10.refs_0_, s32[4,512]{1,0:T(4,128)} %refs_1_.1, s32[1,512]{1,0:T(1,128)} %bitcast.6, ...), custom_call_target="tpu_custom_call" | custom-call | flops 100000000 | bytes 1000000 | tf_op jit(solution)/shard_map/pallas_call | solution.py:93
  3.8 2.8 %collective-permute-start = (f32[128,16]{1,0:T(8,128)S(1)}, f32[128,16]{1,0:T(8,128)S(1)}, u32[]{:S(2)}, u32[]{:S(2)}) collective-permute-start(f32[128,16]{1,0:T(8,128)S(1)} %get-tuple-element.13), channel_id=1, source_target_pairs={{0,1},{1,2},{2,3},{3,4},{4,5},{5,6},{6,7},{7,8},{8,9},{9,10},{10,1... | collective-permute-start | bytes 24584 | tf_op jit(solution)/shard_map/ppermute | solution.py:163
  6.5 0.0 collective-permute-start.1
  6.5 10.6 %all-to-all-start = ((s32[128,2,128]{2,1,0:T(2,128)}), s32[128,2,128]{2,1,0:T(2,128)S(1)}, u32[]{:S(2)}, u32[]{:S(2)}) async-start(s32[128,2,128]{2,1,0:T(2,128)} %get-tuple-element.11), calls=%async_computation | async-start | bytes 262144 | tf_op jit(solution)/shard_map/all_to_all | solution.py:404
  17.1 0.9 %copy.9.kernel_ref = bf16[8,33,33]{2,1,0:T(8,128)(2,1)S(1)} copy(bf16[8,33,33]{2,0,1:T(8,128)(2,1)} %param.12) | data formatting | bytes 34848 | tf_op args[5]
  18.0 0.1 add_convert_fusion.inside_ref
  18.1 1.2 %shard_map.87.table_ref = bf16[47,64,256]{2,1,0:T(8,128)(2,1)S(1)} custom-call(bf16[8,33,33]{2,1,0:T(8,128)(2,1)S(1)} %copy.9.kernel_ref), custom_call_target="tpu_custom_call" | custom-call | flops 100000000 | bytes 1000000 | tf_op jit(solution)/shard_map/pallas_call | solution.py:148
  19.3 0.0 collective-permute-done.1.right_ref
  19.3 0.0 collective-permute-done.left_ref
  19.3 0.1 pad_maximum_fusion
  19.4 2.9 %collective-permute-start.2 = (f32[16,544]{1,0:T(8,128)S(1)}, f32[16,544]{1,0:T(8,128)S(1)}, u32[]{:S(2)}, u32[]{:S(2)}) collective-permute-start(f32[16,544]{1,0:T(8,128)S(1)} %pad_maximum_fusion), channel_id=1, source_target_pairs={{0,16},{16,32},{32,48},{48,64},{64,80},{80,96},{96,112},{112,0},{1... | collective-permute-start | bytes 104456 | tf_op jit(solution)/shard_map/ppermute | solution.py:163
  22.3 0.1 pad_maximum_fusion.1
  22.4 2.8 %collective-permute-start.3 = (f32[16,544]{1,0:T(8,128)S(1)}, f32[16,544]{1,0:T(8,128)S(1)}, u32[]{:S(2)}, u32[]{:S(2)}) collective-permute-start(f32[16,544]{1,0:T(8,128)S(1)} %pad_maximum_fusion.1), channel_id=1, source_target_pairs={{16,0},{32,16},{48,32},{64,48},{80,64},{96,80},{112,96},{0,112},{1... | collective-permute-start | bytes 104456 | tf_op jit(solution)/shard_map/ppermute | solution.py:163
  25.2 1.9 %all-to-all-done.inbox_ref = s32[128,2,128]{2,1,0:T(2,128)S(1)} async-done(((s32[128,2,128]{2,1,0:T(2,128)}), s32[128,2,128]{2,1,0:T(2,128)S(1)}, u32[]{:S(2)}, u32[]{:S(2)}) %all-to-all-start) | async-done | bytes 131104 | tf_op jit(solution)/shard_map/all_to_all | solution.py:404
  27.1 7.4 %shard_map.88 = (f32[128,1,128]{2,1,0:T(1,128)}, bf16[112,640]{1,0:T(8,128)(2,1)S(1)}, bf16[2560,256]{1,0:T(8,128)(2,1)S(1)}) custom-call(s32[128,2,128]{2,1,0:T(2,128)S(1)} %all-to-all-done.inbox_ref, bf16[47,64,256]{2,1,0:T(8,128)(2,1)S(1)} %shard_map.87.table_ref, f32[128,512]{1,0:T(8,128)S(1)} %get-tuple-element.12.signed_ref, ...), custom_call_target="tpu_custom_call" | custom-call | flops 4000000000 | bytes 8000000 | tf_op jit(solution)/shard_map/pallas_call | solution.py:310
  34.5 1.1 %copy-done.1 = bf16[2560,256]{1,0:T(8,128)(2,1)} copy-done((bf16[2560,256]{1,0:T(8,128)(2,1)}, bf16[2560,256]{1,0:T(8,128)(2,1)S(1)}, u32[]{:S(2)}) %copy-start.1) | copy-done | bytes 1310744
  35.6 5.7 %all-to-all-start.1 = ((f32[128,1,128]{2,1,0:T(1,128)}), f32[128,1,128]{2,1,0:T(1,128)S(1)}, u32[]{:S(2)}, u32[]{:S(2)}) async-start(f32[128,1,128]{2,1,0:T(1,128)} %get-tuple-element.19), calls=%async_computation.1 | async-start | bytes 131072 | tf_op jit(solution)/shard_map/all_to_all | solution.py:408
  41.2 0.0 collective-permute-done.2.top_ref
  41.2 0.0 collective-permute-done.3.bottom_ref
  41.3 1.3 %copy-done.2 = bf16[2560,256]{1,0:T(8,128)(2,1)S(1)} copy-done((bf16[2560,256]{1,0:T(8,128)(2,1)S(1)}, bf16[2560,256]{1,0:T(8,128)(2,1)}, u32[]{:S(2)}) %copy-start.2) | copy-done | bytes 1310744
  42.6 7.2 %shard_map.89 = f32[128,512]{1,0:T(8,128)} custom-call(bf16[112,640]{1,0:T(8,128)(2,1)S(1)} %get-tuple-element.15.edges_ref, bf16[47,64,256]{2,1,0:T(8,128)(2,1)S(1)} %shard_map.87.table_ref, bf16[2560,256]{1,0:T(8,128)(2,1)S(1)} %copy-done.2, f32[16,544]{1,0:T(8,128)S(1)} %collective-permute-done.2.top_ref, ...), custom_call_target="tpu_custom_call" | custom-call | flops 4000000000 | bytes 10000000 | tf_op jit(solution)/shard_map/pallas_call | solution.py:379
  49.7 1.1 %all-to-all-done.1 = f32[128,1,128]{2,1,0:T(1,128)S(1)} async-done(((f32[128,1,128]{2,1,0:T(1,128)}), f32[128,1,128]{2,1,0:T(1,128)S(1)}, u32[]{:S(2)}, u32[]{:S(2)}) %all-to-all-start.1) | async-done | bytes 65568 | tf_op jit(solution)/shard_map/all_to_all | solution.py:408
  50.8 0.7 %slice_reduce_fusion = f32[]{:T(128)} fusion(f32[128,1,128]{2,1,0:T(1,128)S(1)} %all-to-all-done.1), kind=kLoop, calls=%fused_computation | loop fusion | flops 127 | bytes 516 | tf_op jit(solution)/shard_map/reduce_sum | solution.py:411
  (5 shorter events, 0.0 us)
Async XLA Ops:
  0.6 26.5 %copy-start = (f32[4]{0:T(128)S(1)}, f32[4]{0:T(128)}, u32[]{:S(2)}) copy-start(f32[4]{0:T(128)} %socs_ref.3) | copy-start | bytes 52
  3.8 15.5 %collective-permute-start = (f32[128,16]{1,0:T(8,128)S(1)}, f32[128,16]{1,0:T(8,128)S(1)}, u32[]{:S(2)}, u32[]{:S(2)}) collective-permute-start(f32[128,16]{1,0:T(8,128)S(1)} %get-tuple-element.13), channel_id=1, source_target_pairs={{0,1},{1,2},{2,3},{3,4},{4,5},{5,6},{6,7},{7,8},{8,9},{9,10},{10,1... | collective-permute-start | bytes 24584 | tf_op jit(solution)/shard_map/ppermute | solution.py:163
  6.5 12.8 %collective-permute-start.1 = (f32[128,16]{1,0:T(8,128)S(1)}, f32[128,16]{1,0:T(8,128)S(1)}, u32[]{:S(2)}, u32[]{:S(2)}) collective-permute-start(f32[128,16]{1,0:T(8,128)S(1)} %get-tuple-element.14), channel_id=1, source_target_pairs={{1,0},{2,1},{3,2},{4,3},{5,4},{6,5},{7,6},{8,7},{9,8},{10,9},{11,1... | collective-permute-start | bytes 24584 | tf_op jit(solution)/shard_map/ppermute | solution.py:163
  6.5 20.6 %all-to-all-start = ((s32[128,2,128]{2,1,0:T(2,128)}), s32[128,2,128]{2,1,0:T(2,128)S(1)}, u32[]{:S(2)}, u32[]{:S(2)}) async-start(s32[128,2,128]{2,1,0:T(2,128)} %get-tuple-element.11), calls=%async_computation | async-start | bytes 262144 | tf_op jit(solution)/shard_map/all_to_all | solution.py:404
  19.4 21.9 %collective-permute-start.2 = (f32[16,544]{1,0:T(8,128)S(1)}, f32[16,544]{1,0:T(8,128)S(1)}, u32[]{:S(2)}, u32[]{:S(2)}) collective-permute-start(f32[16,544]{1,0:T(8,128)S(1)} %pad_maximum_fusion), channel_id=1, source_target_pairs={{0,16},{16,32},{32,48},{48,64},{64,80},{80,96},{96,112},{112,0},{1... | collective-permute-start | bytes 104456 | tf_op jit(solution)/shard_map/ppermute | solution.py:163
  22.4 18.9 %collective-permute-start.3 = (f32[16,544]{1,0:T(8,128)S(1)}, f32[16,544]{1,0:T(8,128)S(1)}, u32[]{:S(2)}, u32[]{:S(2)}) collective-permute-start(f32[16,544]{1,0:T(8,128)S(1)} %pad_maximum_fusion.1), channel_id=1, source_target_pairs={{16,0},{32,16},{48,32},{64,48},{80,64},{96,80},{112,96},{0,112},{1... | collective-permute-start | bytes 104456 | tf_op jit(solution)/shard_map/ppermute | solution.py:163
  34.5 1.1 %copy-start.1 = (bf16[2560,256]{1,0:T(8,128)(2,1)}, bf16[2560,256]{1,0:T(8,128)(2,1)S(1)}, u32[]{:S(2)}) copy-start(bf16[2560,256]{1,0:T(8,128)(2,1)S(1)} %get-tuple-element.16.gs_ref) | copy-start | bytes 3932164
  35.6 15.3 %all-to-all-start.1 = ((f32[128,1,128]{2,1,0:T(1,128)}), f32[128,1,128]{2,1,0:T(1,128)S(1)}, u32[]{:S(2)}, u32[]{:S(2)}) async-start(f32[128,1,128]{2,1,0:T(1,128)} %get-tuple-element.19), calls=%async_computation.1 | async-start | bytes 131072 | tf_op jit(solution)/shard_map/all_to_all | solution.py:408
  41.3 1.3 %copy-start.2 = (bf16[2560,256]{1,0:T(8,128)(2,1)S(1)}, bf16[2560,256]{1,0:T(8,128)(2,1)}, u32[]{:S(2)}) copy-start(bf16[2560,256]{1,0:T(8,128)(2,1)} %copy-done.1) | copy-start | bytes 3932164

commit v4 on v3

--- a/solution.py
+++ b/solution.py
@@ -9,11 +9,9 @@
 CAP = 8
 KS = 33
 BLK = 32
-AROWS = 36
-LEAD = 7
-TABLE = 47
+GROUP = 8
 WIDE = 2 * BLK + 1
-PITCH = 20
+PITCH = 18
 NEIGHBOURS = [(dr, dc) for dr in (-1, 0, 1) for dc in (-1, 0, 1) if (dr, dc) != (0, 0)]
 F32 = jnp.float32
 BF16 = jnp.bfloat16
@@ -112,17 +110,18 @@
 
 
 def tables_kernel(kernel_ref, table_ref, wide_ref):
-    channels = kernel_ref.shape[0]
+    channels = kernel_ref.shape[1]
     lanes = channels * BLK
-    tap, lane = iota((KS, lanes), 0), iota((KS, lanes), 1)
-    taps = jnp.zeros((KS, lanes), F32)
-    edge = jnp.zeros((KS, lanes), F32)
-    for c in range(channels):
-        mine = lane // BLK == c
-        reverse = jnp.where(mine & (tap == KS - 1 - lane % BLK), 1.0, 0.0).astype(BF16)
-        first = jnp.where(mine & (tap == 0), 1.0, 0.0).astype(BF16)
-        taps = taps + jnp.dot(kernel_ref[c], reverse, preferred_element_type=F32)
-        edge = edge + jnp.dot(kernel_ref[c], first, preferred_element_type=F32)
+    tap, lane = iota((KS, lanes), 0), iota((KS, lanes), 1) % BLK
+    flat = kernel_ref[...].astype(F32).reshape(KS * channels, KS).astype(BF16)
+    mine = iota((KS, channels, lanes), 1) == iota((KS, channels, lanes), 2) // BLK
+
+    def by_lane(picked):
+        every = jnp.dot(flat, jnp.where(picked, 1.0, 0.0).astype(BF16), preferred_element_type=F32)
+        return jnp.sum(jnp.where(mine, every.reshape(KS, channels, lanes), 0.0), axis=1)
+
+    taps = by_lane(tap == KS - 1 - lane)
+    edge = by_lane(tap == 0)
     co = iota((KS, 128), 1) % BLK
     for p in range(BLK):
         for h in range(lanes // 128):
@@ -133,26 +132,21 @@
             far = jnp.where(co < p, far, jnp.where(co == p, ends, 0.0))
             wide_ref[h, pl.ds(p, KS, stride=WIDE), :] = far
             wide_ref[h, pl.ds(BLK + p, KS, stride=WIDE), :] = jnp.where(co >= p, near, 0.0)
-    zero = jnp.zeros((2 * BLK, lanes), BF16)
-    for a in range(TABLE):
-        if a < LEAD or a >= LEAD + KS:
-            table_ref[a] = zero
-            continue
-        at = (a - LEAD) * WIDE
+    for a in range(KS):
         for h in range(lanes // 128):
-            table_ref[a, :, 128 * h : 128 * h + 128] = wide_ref[h, at : at + 2 * BLK, :].astype(BF16)
+            table_ref[a, :, 128 * h : 128 * h + 128] = wide_ref[h, a * WIDE : a * WIDE + 2 * BLK, :].astype(BF16)
 
 
 def make_tables(kernel):
     lanes = kernel.shape[0] * BLK
     return pl.pallas_call(
         tables_kernel,
-        out_shape=pltpu.VMEM((TABLE, 2 * BLK, lanes), BF16),
+        out_shape=pltpu.VMEM((KS, 2 * BLK, lanes), BF16),
         in_specs=[WHOLE],
         scratch_shapes=[pltpu.VMEM((lanes // 128, KS * WIDE + 8, 128), F32)],
         compiler_params=pltpu.CompilerParams(vmem_limit_bytes=VMEM_LIMIT // 2),
-        cost_estimate=pl.CostEstimate(flops=10**8, bytes_accessed=10**6, transcendentals=0),
-    )(kernel)
+        cost_estimate=pl.CostEstimate(flops=10**10, bytes_accessed=10**6, transcendentals=0),
+    )(kernel.transpose(1, 0, 2))
 
 
 def weight_strips(top_rows, bottom_rows, left_cols, right_cols):
@@ -203,12 +197,14 @@
         else:
             window = mask[:, BLK * (b - 1) : BLK * (b + 1)]
         s_ref[pl.ds(first * PITCH + b, count, stride=PITCH), :] = jnp.concatenate([window, window], axis=1)
-
-
-def four_rows(s_ref, a_ref, start, end, step):
+    for b in range(cols // BLK + 1, PITCH):
+        s_ref[pl.ds(first * PITCH + b, count, stride=PITCH), :] = jnp.zeros((count, 128), F32)
+
+
+def group_rows(s_ref, a_ref, start, end, step):
     first_half = iota((step, 128), 1) < 64
     for m in range(start, end, step):
-        for h in range(2):
+        for h in range(GROUP // 2):
             even = s_ref[m + 2 * h * PITCH : m + 2 * h * PITCH + step, :]
             odd = s_ref[m + (2 * h + 1) * PITCH : m + (2 * h + 1) * PITCH + step, :]
             a_ref[m : m + step, 128 * h : 128 * h + 128] = jnp.where(first_half, even, odd).astype(BF16)
@@ -216,10 +212,14 @@
 
 def correlate(a_ref, starts, count, table_ref):
     fields = None
-    for g in range(AROWS // 4):
-        parts = [a_ref[m + 4 * PITCH * g : m + 4 * PITCH * g + count, :] for m in starts]
+    for g in range(0, KS, GROUP):
+        taken = min(GROUP, KS - g)
+        right = table_ref[g : g + taken].reshape(taken * 2 * BLK, 256)
+        if taken % 2:
+            right = jnp.concatenate([right, jnp.zeros((2 * BLK, 256), BF16)], axis=0)
+        lanes = slice(0, right.shape[0])
+        parts = [a_ref[m + PITCH * g : m + PITCH * g + count, lanes] for m in starts]
         left = parts[0] if len(parts) == 1 else jnp.concatenate(parts, axis=0)
-        right = table_ref[LEAD + 4 * g : LEAD + 4 * g + 4].reshape(8 * BLK, 256)
         term = jnp.dot(left, right, preferred_element_type=F32)
         fields = term if fields is None else fields + term
     return fields
@@ -279,9 +279,9 @@
 
     edges_ref[0:64, :] = mask_ref[0:64, :].astype(BF16)
     edges_ref[64:112, :] = mask_ref[tall - 48 : tall, :].astype(BF16)
-    s_ref[...] = jnp.zeros(s_ref.shape, F32)
+    s_ref[tall * PITCH :, :] = jnp.zeros((8 * PITCH, 128), F32)
     windows(mask_ref[...], s_ref, 0, cols)
-    four_rows(s_ref, a_ref, RAD * PITCH, (tall - RAD) * PITCH, 16 * PITCH)
+    group_rows(s_ref, a_ref, RAD * PITCH, (tall - RAD) * PITCH, 16 * PITCH)
     left = jnp.where(inside_ref[2] > 0, left_ref[...], 0.0)
     right = jnp.where(inside_ref[3] > 0, right_ref[...], 0.0)
     spread(signed_ref, left, right, sw_ref, rows, cols)
@@ -317,13 +317,23 @@
         in_specs=[WHOLE] * 5 + [SMALL] * 2,
         scratch_shapes=[
             pltpu.VMEM((tall, cols + 128), F32),
-            pltpu.VMEM(((tall + 4) * PITCH, 128), F32),
-            pltpu.VMEM((tall * PITCH, 256), BF16),
+            pltpu.VMEM(((tall + 8) * PITCH, 128), F32),
+            pltpu.VMEM((tall * PITCH, 64 * GROUP), BF16),
             pltpu.VMEM((rows * PITCH, 128), F32),
         ],
         compiler_params=pltpu.CompilerParams(vmem_limit_bytes=VMEM_LIMIT),
         cost_estimate=pl.CostEstimate(flops=4 * 10**9, bytes_accessed=8 * 10**6, transcendentals=10**6),
     )(inbox, table, signed, left, right, socs_weight, inside)
+
+
+def adjoint_taps(table_ref, start, at):
+    first, last = max(start, 0), min(start + 8, KS)
+    pieces = [table_ref[first:last, at : at + BLK, :].reshape((last - first) * BLK, 256)]
+    if first > start:
+        pieces.insert(0, jnp.zeros(((first - start) * BLK, 256), BF16))
+    if last < start + 8:
+        pieces.append(jnp.zeros(((start + 8 - last) * BLK, 256), BF16))
+    return pieces[0] if len(pieces) == 1 else jnp.concatenate(pieces, axis=0)
 
 
 def adjoint_kernel(
@@ -337,11 +347,11 @@
     left = jnp.where(inside_ref[2] > 0, x_ref[:, cols + RAD : cols + 2 * RAD], 0.0)
     right = jnp.where(inside_ref[3] > 0, x_ref[:, cols : cols + RAD], 0.0)
     spread(x_ref, left, right, sw_ref, 2 * RAD, cols)
-    s_ref[...] = jnp.zeros(s_ref.shape, F32)
+    s_ref[112 * PITCH :, :] = jnp.zeros((8 * PITCH, 128), F32)
     windows(edges_ref[0:64, :].astype(F32), s_ref, 0, cols)
     windows(edges_ref[64:112, :].astype(F32), s_ref, 64, cols)
-    four_rows(s_ref, a_ref, 0, 48 * PITCH, 16 * PITCH)
-    four_rows(s_ref, a_ref, 64 * PITCH, 112 * PITCH, 16 * PITCH)
+    group_rows(s_ref, a_ref, 0, 48 * PITCH, 16 * PITCH)
+    group_rows(s_ref, a_ref, 64 * PITCH, 112 * PITCH, 16 * PITCH)
     fields = correlate(a_ref, [0, 64 * PITCH], RAD * PITCH, table_ref)
     resist_and_gradient(fields, sw_ref[...], channel_weights(socs_ref), gw_ref, 0)
     gw_ref[2 * RAD * PITCH :, :] = gs_ref[...].astype(F32)
@@ -361,8 +371,7 @@
     for i in range(40):
         for s in range(2):
             fields = g_ref[s, i % 8, i // 8 : i // 8 + 16].reshape(256, 256)
-            taps = table_ref[39 - i : 47 - i, BLK * (1 - s) : BLK * (2 - s), :].reshape(256, 256)
-            total = total + dot_nt(fields, taps)
+            total = total + dot_nt(fields, adjoint_taps(table_ref, KS - 1 - i, BLK * (1 - s)))
     for h in range(2):
         acc_ref[h] = total[:, 128 * h : 128 * h + 128]
     for q in range(cols // 128):
@@ -381,8 +390,8 @@
         out_shape=jax.ShapeDtypeStruct((rows, cols), F32),
         in_specs=[WHOLE] * 5 + [SMALL] * 2,
         scratch_shapes=[
-            pltpu.VMEM((116 * PITCH, 128), F32),
-            pltpu.VMEM((112 * PITCH, 256), BF16),
+            pltpu.VMEM((120 * PITCH, 128), F32),
+            pltpu.VMEM((112 * PITCH, 64 * GROUP), BF16),
             pltpu.VMEM((2 * RAD, cols + 2 * RAD), F32),
             pltpu.VMEM((2 * RAD * PITCH, 128), F32),
             pltpu.VMEM((ext * PITCH, 256), F32),

time: 53.7 us -> 51.9 us (0.966)
  local copies, waits for them, and re-layouts: 3.3 us -> 0.89 us
  waiting for transfers between devices: 3.02 us -> 4.74 us
  Pallas kernels: 18.2 us -> 17.2 us
    unnamed x7 -> x4, local copies, waits for them, and re-layouts: 3.3 us -> 0.88 us
    all_to_all x1, waiting for transfers between devices: 1.09 us -> 2.7 us  [shards(): lax.all_to_all(local, ('row', 'col'), split_axis=0, concat_axis=0, tiled=...]
    pallas_call x1, Pallas kernels: 7.37 us -> 6.78 us  [imaging(): pl.pallas_call(imaging_kernel, out_shape=(pltpu.VMEM((devices, 1, 128), F...]
  transfers between devices with their start and end apart: 6 -> 6, of which waited for: 2 -> 2; matrix products, arithmetic and copies ran while one was open for 2% -> 0% of each run, Pallas kernels for 29% -> 29%
where the time goes in v4:
time: 51.9 us; the launch traced here: 51.5 us
  starting transfers between devices  24.6 us (47%)
  Pallas kernels  17.2 us (33%)
  waiting for transfers between devices  4.74 us (9%)
  between operations  3.15 us (6%)
  other arithmetic  0.97 us (2%)
  local copies, waits for them, and re-layouts  0.89 us (2%)
    all_to_all x1, starting transfers between devices, shards(): lax.all_to_all(outbox, ('row', 'col'), split_axis=0, concat_axis=0, tiled...  10.6 us
    ppermute x4, starting transfers between devices, beside(): return (lax.ppermute(last, axis, up), lax.ppermute(first, axis, down))  8.49 us
    pallas_call x1, Pallas kernels, adjoint(): pl.pallas_call(adjoint_kernel, out_shape=jax.ShapeDtypeStruct((rows, cols...  6.89 us
    pallas_call x1, Pallas kernels, imaging(): pl.pallas_call(imaging_kernel, out_shape=(pltpu.VMEM((devices, 1, 128), F...  6.78 us
    all_to_all x1, starting transfers between devices, shards(): lax.all_to_all(local, ('row', 'col'), split_axis=0, concat_axis=0, tiled=...  5.55 us
    all_to_all x1, waiting for transfers between devices, shards(): lax.all_to_all(local, ('row', 'col'), split_axis=0, concat_axis=0, tiled=...  2.7 us
    pallas_call x1, Pallas kernels, make_outbox(): pl.pallas_call(lambda *refs: outbox_kernel(tile_cols, *refs), out_shape=(...  2.45 us
    all_to_all x1, waiting for transfers between devices, shards(): lax.all_to_all(outbox, ('row', 'col'), split_axis=0, concat_axis=0, tiled...  2.03 us
  transfers between devices with their start and end apart: 6, of which 2 were waited for; matrix products, arithmetic and copies ran while one was open for 0% of the time, Pallas kernels for 29%

profile of v4, /device:TPU:1, one launch (start us, length us, event | category | flops | bytes accessed | tf_op | source)
XLA Modules:
  0.0 51.5 jit_solution(8187540644148428375)
XLA Ops:
  1.3 2.4 %shard_map.86 = (s32[128,2,128]{2,1,0:T(2,128)}, f32[128,512]{1,0:T(8,128)S(1)}, f32[16,512]{1,0:T(8,128)S(1)}, f32[16,512]{1,0:T(8,128)S(1)}, f32[128,16]{1,0:T(8,128)S(1)}, /*index=5*/f32[128,16]{1,0:T(8,128)S(1)}) custom-call(s32[1]{0:T(128)S(6)} %copy.9.refs_0_, s32[4,512]{1,0:T(4,128)} %refs_1_.1, s32[1,512]{1,0:T(1,128)} %bitcast.8, ...), custom_call_target="tpu_custom_call" | custom-call | flops 100000000 | bytes 1000000 | tf_op jit(solution)/shard_map/pallas_call | solution.py:91
  3.7 2.8 %collective-permute-start = (f32[128,16]{1,0:T(8,128)S(1)}, f32[128,16]{1,0:T(8,128)S(1)}, u32[]{:S(2)}, u32[]{:S(2)}) collective-permute-start(f32[128,16]{1,0:T(8,128)S(1)} %get-tuple-element.13), channel_id=1, source_target_pairs={{0,1},{1,2},{2,3},{3,4},{4,5},{5,6},{6,7},{7,8},{8,9},{9,10},{10,1... | collective-permute-start | bytes 24584 | tf_op jit(solution)/shard_map/ppermute | solution.py:157
  6.5 0.0 collective-permute-start.1
  6.5 10.6 %all-to-all-start = ((s32[128,2,128]{2,1,0:T(2,128)}), s32[128,2,128]{2,1,0:T(2,128)S(1)}, u32[]{:S(2)}, u32[]{:S(2)}) async-start(s32[128,2,128]{2,1,0:T(2,128)} %get-tuple-element.11), calls=%async_computation | async-start | bytes 262144 | tf_op jit(solution)/shard_map/all_to_all | solution.py:413
  17.1 0.0 copy-start
  17.1 0.9 %copy-done = bf16[8,33,33]{2,0,1:T(8,128)(2,1)S(1)} copy-done((bf16[8,33,33]{2,0,1:T(8,128)(2,1)S(1)}, bf16[8,33,33]{2,0,1:T(8,128)(2,1)}, u32[]{:S(2)}) %copy-start) | copy-done | bytes 17448
  17.9 0.0 copy-start.1
  18.0 1.1 %shard_map.87.table_ref = bf16[33,64,256]{2,1,0:T(8,128)(2,1)S(1)} custom-call(bf16[33,8,33]{2,1,0:T(8,128)(2,1)S(1)} %bitcast.7), custom_call_target="tpu_custom_call" | custom-call | flops 10000000000 | bytes 1000000 | tf_op jit(solution)/shard_map/pallas_call | solution.py:142
  19.1 0.1 add_convert_fusion.inside_ref
  19.1 0.0 collective-permute-done.1.right_ref
  19.1 0.0 collective-permute-done.left_ref
  19.2 0.1 pad_maximum_fusion
  19.2 2.9 %collective-permute-start.2 = (f32[16,544]{1,0:T(8,128)S(1)}, f32[16,544]{1,0:T(8,128)S(1)}, u32[]{:S(2)}, u32[]{:S(2)}) collective-permute-start(f32[16,544]{1,0:T(8,128)S(1)} %pad_maximum_fusion), channel_id=1, source_target_pairs={{0,16},{16,32},{32,48},{48,64},{64,80},{80,96},{96,112},{112,0},{1... | collective-permute-start | bytes 104456 | tf_op jit(solution)/shard_map/ppermute | solution.py:157
  22.1 0.1 pad_maximum_fusion.1
  22.2 2.8 %collective-permute-start.3 = (f32[16,544]{1,0:T(8,128)S(1)}, f32[16,544]{1,0:T(8,128)S(1)}, u32[]{:S(2)}, u32[]{:S(2)}) collective-permute-start(f32[16,544]{1,0:T(8,128)S(1)} %pad_maximum_fusion.1), channel_id=1, source_target_pairs={{16,0},{32,16},{48,32},{64,48},{80,64},{96,80},{112,96},{0,112},{1... | collective-permute-start | bytes 104456 | tf_op jit(solution)/shard_map/ppermute | solution.py:157
  25.0 2.0 %all-to-all-done.inbox_ref = s32[128,2,128]{2,1,0:T(2,128)S(1)} async-done(((s32[128,2,128]{2,1,0:T(2,128)}), s32[128,2,128]{2,1,0:T(2,128)S(1)}, u32[]{:S(2)}, u32[]{:S(2)}) %all-to-all-start) | async-done | bytes 131104 | tf_op jit(solution)/shard_map/all_to_all | solution.py:413
  27.1 0.0 copy-done.1
  27.1 6.8 %shard_map.88 = (f32[128,1,128]{2,1,0:T(1,128)}, bf16[112,640]{1,0:T(8,128)(2,1)S(1)}, bf16[2304,256]{1,0:T(8,128)(2,1)S(1)}) custom-call(s32[128,2,128]{2,1,0:T(2,128)S(1)} %all-to-all-done.inbox_ref, bf16[33,64,256]{2,1,0:T(8,128)(2,1)S(1)} %shard_map.87.table_ref, f32[128,512]{1,0:T(8,128)S(1)} %get-tuple-element.12.signed_ref, ...), custom_call_target="tpu_custom_call" | custom-call | flops 4000000000 | bytes 8000000 | tf_op jit(solution)/shard_map/pallas_call | solution.py:310
  33.9 5.6 %all-to-all-start.1 = ((f32[128,1,128]{2,1,0:T(1,128)}), f32[128,1,128]{2,1,0:T(1,128)S(1)}, u32[]{:S(2)}, u32[]{:S(2)}) async-start(f32[128,1,128]{2,1,0:T(1,128)} %get-tuple-element.19), calls=%async_computation.1 | async-start | bytes 131072 | tf_op jit(solution)/shard_map/all_to_all | solution.py:417
  39.4 0.0 collective-permute-done.2.top_ref
  39.4 0.0 collective-permute-done.3.bottom_ref
  39.4 6.9 %shard_map.89 = f32[128,512]{1,0:T(8,128)} custom-call(bf16[112,640]{1,0:T(8,128)(2,1)S(1)} %get-tuple-element.15.edges_ref, bf16[33,64,256]{2,1,0:T(8,128)(2,1)S(1)} %shard_map.87.table_ref, bf16[2304,256]{1,0:T(8,128)(2,1)S(1)} %get-tuple-element.16.gs_ref, f32[16,544]{1,0:T(8,128)S(1)} %collective-permute-done.2.top_ref, ...), custom_call_target="tpu_custom_call" | custom-call | flops 4000000000 | bytes 10000000 | tf_op jit(solution)/shard_map/pallas_call | solution.py:388
  46.3 2.7 %all-to-all-done.1 = f32[128,1,128]{2,1,0:T(1,128)S(1)} async-done(((f32[128,1,128]{2,1,0:T(1,128)}), f32[128,1,128]{2,1,0:T(1,128)S(1)}, u32[]{:S(2)}, u32[]{:S(2)}) %all-to-all-start.1) | async-done | bytes 65568 | tf_op jit(solution)/shard_map/all_to_all | solution.py:417
  49.0 0.7 %slice_reduce_fusion = f32[]{:T(128)} fusion(f32[128,1,128]{2,1,0:T(1,128)S(1)} %all-to-all-done.1), kind=kLoop, calls=%fused_computation | loop fusion | flops 127 | bytes 516 | tf_op jit(solution)/shard_map/reduce_sum | solution.py:420
  (2 shorter events, 0.0 us)
Async XLA Ops:
  3.7 15.4 %collective-permute-start = (f32[128,16]{1,0:T(8,128)S(1)}, f32[128,16]{1,0:T(8,128)S(1)}, u32[]{:S(2)}, u32[]{:S(2)}) collective-permute-start(f32[128,16]{1,0:T(8,128)S(1)} %get-tuple-element.13), channel_id=1, source_target_pairs={{0,1},{1,2},{2,3},{3,4},{4,5},{5,6},{6,7},{7,8},{8,9},{9,10},{10,1... | collective-permute-start | bytes 24584 | tf_op jit(solution)/shard_map/ppermute | solution.py:157
  6.5 12.6 %collective-permute-start.1 = (f32[128,16]{1,0:T(8,128)S(1)}, f32[128,16]{1,0:T(8,128)S(1)}, u32[]{:S(2)}, u32[]{:S(2)}) collective-permute-start(f32[128,16]{1,0:T(8,128)S(1)} %get-tuple-element.14), channel_id=1, source_target_pairs={{1,0},{2,1},{3,2},{4,3},{5,4},{6,5},{7,6},{8,7},{9,8},{10,9},{11,1... | collective-permute-start | bytes 24584 | tf_op jit(solution)/shard_map/ppermute | solution.py:157
  6.5 20.6 %all-to-all-start = ((s32[128,2,128]{2,1,0:T(2,128)}), s32[128,2,128]{2,1,0:T(2,128)S(1)}, u32[]{:S(2)}, u32[]{:S(2)}) async-start(s32[128,2,128]{2,1,0:T(2,128)} %get-tuple-element.11), calls=%async_computation | async-start | bytes 262144 | tf_op jit(solution)/shard_map/all_to_all | solution.py:413
  17.1 0.9 %copy-start = (bf16[8,33,33]{2,0,1:T(8,128)(2,1)S(1)}, bf16[8,33,33]{2,0,1:T(8,128)(2,1)}, u32[]{:S(2)}) copy-start(bf16[8,33,33]{2,0,1:T(8,128)(2,1)} %param.12) | copy-start | bytes 52276
  17.9 9.1 %copy-start.1 = (f32[4]{0:T(128)S(1)}, f32[4]{0:T(128)}, u32[]{:S(2)}) copy-start(f32[4]{0:T(128)} %socs_ref.3) | copy-start | bytes 52
  19.2 20.2 %collective-permute-start.2 = (f32[16,544]{1,0:T(8,128)S(1)}, f32[16,544]{1,0:T(8,128)S(1)}, u32[]{:S(2)}, u32[]{:S(2)}) collective-permute-start(f32[16,544]{1,0:T(8,128)S(1)} %pad_maximum_fusion), channel_id=1, source_target_pairs={{0,16},{16,32},{32,48},{48,64},{64,80},{80,96},{96,112},{112,0},{1... | collective-permute-start | bytes 104456 | tf_op jit(solution)/shard_map/ppermute | solution.py:157
  22.2 17.2 %collective-permute-start.3 = (f32[16,544]{1,0:T(8,128)S(1)}, f32[16,544]{1,0:T(8,128)S(1)}, u32[]{:S(2)}, u32[]{:S(2)}) collective-permute-start(f32[16,544]{1,0:T(8,128)S(1)} %pad_maximum_fusion.1), channel_id=1, source_target_pairs={{16,0},{32,16},{48,32},{64,48},{80,64},{96,80},{112,96},{0,112},{1... | collective-permute-start | bytes 104456 | tf_op jit(solution)/shard_map/ppermute | solution.py:157
  33.9 15.2 %all-to-all-start.1 = ((f32[128,1,128]{2,1,0:T(1,128)}), f32[128,1,128]{2,1,0:T(1,128)S(1)}, u32[]{:S(2)}, u32[]{:S(2)}) async-start(f32[128,1,128]{2,1,0:T(1,128)} %get-tuple-element.19), calls=%async_computation.1 | async-start | bytes 131072 | tf_op jit(solution)/shard_map/all_to_all | solution.py:417

commit v5 on v4

--- a/solution.py
+++ b/solution.py
@@ -165,7 +165,7 @@
     )
     r, c = lax.axis_index("row"), lax.axis_index("col")
     inside = jnp.stack([r > 0, r < lax.axis_size("row") - 1, c > 0, c < lax.axis_size("col") - 1])
-    return top, bottom, left, right, inside.astype(jnp.int32)
+    return top, bottom, left, right, jnp.broadcast_to(inside.astype(F32)[:, None], (4, 128))
 
 
 def spread(x_ref, left, right, out_ref, rows, cols):
@@ -181,22 +181,26 @@
         out_ref[pl.ds(b, rows, stride=PITCH), :] = jnp.zeros((rows, 128), F32)
 
 
-def channel_weights(socs_ref):
-    k = iota((1, 256), 1) // (2 * BLK)
-    wv = jnp.zeros((1, 256), F32)
-    for i in range(4):
-        wv = jnp.where(k == i, socs_ref[i], wv)
-    return wv
-
-
 def windows(mask, s_ref, first, cols):
     count = mask.shape[0]
+    lane = iota((count, 128), 1)
+    tiles = [mask[:, 128 * q : 128 * q + 128] for q in range(cols // 128 + 1)]
+    turned = [[x] + [pltpu.roll(x, 128 - BLK * j, 1) for j in (1, 2, 3)] for x in tiles]
     for b in range(cols // BLK + 1):
         if b == 0:
-            window = jnp.concatenate([mask[:, cols + BLK : cols + 2 * BLK], mask[:, 0:BLK]], axis=1)
+            low = jnp.where(lane < 32, turned[-1][1], turned[0][3])
+            high = jnp.where(lane < 96, turned[-1][3], turned[0][1])
         else:
-            window = mask[:, BLK * (b - 1) : BLK * (b + 1)]
-        s_ref[pl.ds(first * PITCH + b, count, stride=PITCH), :] = jnp.concatenate([window, window], axis=1)
+            q, j = divmod(b - 1, 4)
+            x = turned[q]
+            if j < 3:
+                low, high = x[j], x[(j + 2) % 4]
+            else:
+                y = turned[q + 1]
+                low = jnp.where(lane < 32, x[3], y[3])
+                high = jnp.where(lane < 96, x[1], y[1])
+        value = jnp.where(lane < 64, low, high)
+        s_ref[pl.ds(first * PITCH + b, count, stride=PITCH), :] = value
     for b in range(cols // BLK + 1, PITCH):
         s_ref[pl.ds(first * PITCH + b, count, stride=PITCH), :] = jnp.zeros((count, 128), F32)
 
@@ -226,21 +230,23 @@
 
 
 def resist_and_gradient(fields, signed, wv, gs_ref, at):
-    square = fields * fields * wv
+    weighted = fields * wv
+    square = fields * weighted
     intensity = square[:, :128] + square[:, 128:]
     intensity = intensity + pltpu.roll(intensity, 64, 1)
     intensity = intensity + pltpu.roll(intensity, 32, 1)
     resist = 1.0 / (1.0 + jnp.exp(3.0 - intensity))
-    slope = 2.0 * (jnp.abs(signed) * resist - jnp.maximum(signed, 0.0)) * resist * (1.0 - resist)
+    miss = resist - jnp.where(signed > 0.0, 1.0, 0.0)
+    pull = jnp.abs(signed) * miss
+    slope = 4.0 * pull * (resist * (1.0 - resist))
     for h in range(2):
         lanes = slice(128 * h, 128 * h + 128)
-        value = (2.0 * wv[:, lanes]) * fields[:, lanes] * slope
-        gs_ref[at : at + fields.shape[0], lanes] = value.astype(gs_ref.dtype)
-    return resist
+        gs_ref[at : at + fields.shape[0], lanes] = (weighted[:, lanes] * slope).astype(gs_ref.dtype)
+    return miss, pull
 
 
 def imaging_kernel(
-    inbox_ref, table_ref, signed_ref, left_ref, right_ref, socs_ref, inside_ref,
+    inbox_ref, table_ref, signed_ref, left_ref, right_ref, inside_ref, wv_ref,
     loss_ref, edges_ref, gs_ref, mask_ref, s_ref, a_ref, sw_ref,
 ):
     rows, cols = signed_ref.shape
@@ -279,32 +285,33 @@
 
     edges_ref[0:64, :] = mask_ref[0:64, :].astype(BF16)
     edges_ref[64:112, :] = mask_ref[tall - 48 : tall, :].astype(BF16)
-    s_ref[tall * PITCH :, :] = jnp.zeros((8 * PITCH, 128), F32)
-    windows(mask_ref[...], s_ref, 0, cols)
+    windows(mask_ref[RAD : tall - RAD + 8, :], s_ref, RAD, cols)
     group_rows(s_ref, a_ref, RAD * PITCH, (tall - RAD) * PITCH, 16 * PITCH)
-    left = jnp.where(inside_ref[2] > 0, left_ref[...], 0.0)
-    right = jnp.where(inside_ref[3] > 0, right_ref[...], 0.0)
+    left = jnp.where(inside_ref[2:3, 0:1] > 0.0, left_ref[...], 0.0)
+    right = jnp.where(inside_ref[3:4, 0:1] > 0.0, right_ref[...], 0.0)
     spread(signed_ref, left, right, sw_ref, rows, cols)
 
-    wv = channel_weights(socs_ref)
-    chunk = rows // 4 * PITCH
+    wv = wv_ref[...]
+    chunk = rows // 8 * PITCH
     block = iota((chunk, 128), 0) % PITCH
     co = iota((chunk, 128), 1) & (BLK - 1)
     own = ((block > 0) | (co >= RAD)) & ((block < cols // BLK) | (co < RAD)) & (block <= cols // BLK)
     total = jnp.zeros((1, 128), F32)
-    for k in range(4):
+    ahead = correlate(a_ref, [RAD * PITCH], chunk, table_ref)
+    for k in range(8):
         m = k * chunk
-        fields = correlate(a_ref, [RAD * PITCH + m], chunk, table_ref)
+        fields = ahead
+        if k < 7:
+            ahead = correlate(a_ref, [RAD * PITCH + m + chunk], chunk, table_ref)
         signed = sw_ref[m : m + chunk, :]
-        resist = resist_and_gradient(fields, signed, wv, gs_ref, m)
-        miss = resist - jnp.where(signed > 0.0, 1.0, 0.0)
-        part = jnp.where(own, jnp.abs(signed), 0.0) * miss * miss
+        miss, pull = resist_and_gradient(fields, signed, wv, gs_ref, m)
+        part = jnp.where(own, pull * miss, 0.0)
         total = total + jnp.sum(part, axis=0, keepdims=True)
     total = 0.25 * jnp.sum(total, axis=1, keepdims=True)
     loss_ref[...] = jnp.broadcast_to(total, loss_ref.shape)
 
 
-def imaging(inbox, table, signed, left, right, socs_weight, inside, devices):
+def imaging(inbox, table, signed, left, right, inside, wv, devices):
     rows, cols = signed.shape
     tall = rows + 4 * RAD
     return pl.pallas_call(
@@ -314,7 +321,7 @@
             pltpu.VMEM((112, cols + 128), BF16),
             pltpu.VMEM((rows * PITCH, 256), BF16),
         ),
-        in_specs=[WHOLE] * 5 + [SMALL] * 2,
+        in_specs=[WHOLE] * 7,
         scratch_shapes=[
             pltpu.VMEM((tall, cols + 128), F32),
             pltpu.VMEM(((tall + 8) * PITCH, 128), F32),
@@ -323,7 +330,7 @@
         ],
         compiler_params=pltpu.CompilerParams(vmem_limit_bytes=VMEM_LIMIT),
         cost_estimate=pl.CostEstimate(flops=4 * 10**9, bytes_accessed=8 * 10**6, transcendentals=10**6),
-    )(inbox, table, signed, left, right, socs_weight, inside)
+    )(inbox, table, signed, left, right, inside, wv)
 
 
 def adjoint_taps(table_ref, start, at):
@@ -337,15 +344,15 @@
 
 
 def adjoint_kernel(
-    edges_ref, table_ref, gs_ref, top_ref, bottom_ref, socs_ref, inside_ref,
+    edges_ref, table_ref, gs_ref, top_ref, bottom_ref, inside_ref, wv_ref,
     out_ref, s_ref, a_ref, x_ref, sw_ref, gw_ref, g_ref, acc_ref, tile_ref,
 ):
     rows, cols = out_ref.shape
     ext = rows + 2 * RAD
-    x_ref[0:RAD, :] = jnp.where(inside_ref[0] > 0, top_ref[...], 0.0)
-    x_ref[RAD : 2 * RAD, :] = jnp.where(inside_ref[1] > 0, bottom_ref[...], 0.0)
-    left = jnp.where(inside_ref[2] > 0, x_ref[:, cols + RAD : cols + 2 * RAD], 0.0)
-    right = jnp.where(inside_ref[3] > 0, x_ref[:, cols : cols + RAD], 0.0)
+    x_ref[0:RAD, :] = jnp.where(inside_ref[0:1, 0:1] > 0.0, top_ref[...], 0.0)
+    x_ref[RAD : 2 * RAD, :] = jnp.where(inside_ref[1:2, 0:1] > 0.0, bottom_ref[...], 0.0)
+    left = jnp.where(inside_ref[2:3, 0:1] > 0.0, x_ref[:, cols + RAD : cols + 2 * RAD], 0.0)
+    right = jnp.where(inside_ref[3:4, 0:1] > 0.0, x_ref[:, cols : cols + RAD], 0.0)
     spread(x_ref, left, right, sw_ref, 2 * RAD, cols)
     s_ref[112 * PITCH :, :] = jnp.zeros((8 * PITCH, 128), F32)
     windows(edges_ref[0:64, :].astype(F32), s_ref, 0, cols)
@@ -353,7 +360,7 @@
     group_rows(s_ref, a_ref, 0, 48 * PITCH, 16 * PITCH)
     group_rows(s_ref, a_ref, 64 * PITCH, 112 * PITCH, 16 * PITCH)
     fields = correlate(a_ref, [0, 64 * PITCH], RAD * PITCH, table_ref)
-    resist_and_gradient(fields, sw_ref[...], channel_weights(socs_ref), gw_ref, 0)
+    resist_and_gradient(fields, sw_ref[...], wv_ref[...], gw_ref, 0)
     gw_ref[2 * RAD * PITCH :, :] = gs_ref[...].astype(F32)
 
     for r in range(ext):
@@ -383,12 +390,12 @@
         out_ref[:, 128 * q : 128 * q + 128] = tile_ref[q]
 
 
-def adjoint(edges, table, gs, top, bottom, socs_weight, inside, rows, cols):
+def adjoint(edges, table, gs, top, bottom, inside, wv, rows, cols):
     ext = rows + 2 * RAD
     return pl.pallas_call(
         adjoint_kernel,
         out_shape=jax.ShapeDtypeStruct((rows, cols), F32),
-        in_specs=[WHOLE] * 5 + [SMALL] * 2,
+        in_specs=[WHOLE] * 7,
         scratch_shapes=[
             pltpu.VMEM((120 * PITCH, 128), F32),
             pltpu.VMEM((112 * PITCH, 64 * GROUP), BF16),
@@ -401,7 +408,7 @@
         ],
         compiler_params=pltpu.CompilerParams(vmem_limit_bytes=VMEM_LIMIT),
         cost_estimate=pl.CostEstimate(flops=4 * 10**9, bytes_accessed=10**7, transcendentals=0),
-    )(edges, table, gs, top, bottom, socs_weight, inside)
+    )(edges, table, gs, top, bottom, inside, wv)
 
 
 def shards(rects, owner, counts, target, loss_weight, kernel, socs_weight):
@@ -413,9 +420,10 @@
     inbox = lax.all_to_all(outbox, ("row", "col"), split_axis=0, concat_axis=0, tiled=True)
     table = make_tables(kernel)
     top, bottom, left, right, inside = weight_strips(*strips)
-    local, edges, gs = imaging(inbox, table, signed, left, right, socs_weight, inside, devices)
+    wv = jnp.repeat(socs_weight, 2 * BLK).reshape(1, kernel.shape[0] * BLK)
+    local, edges, gs = imaging(inbox, table, signed, left, right, inside, wv, devices)
     losses = lax.all_to_all(local, ("row", "col"), split_axis=0, concat_axis=0, tiled=True)
-    mask_grad = adjoint(edges, table, gs, top, bottom, socs_weight, inside, rows, cols)
+    mask_grad = adjoint(edges, table, gs, top, bottom, inside, wv, rows, cols)
     window_area = rows * row_devices * cols * col_devices
     return (mask_grad, (jnp.sum(losses[:, 0, 0]) / window_area).reshape(1))
 

time: 51.9 us -> 51.2 us (0.987)
  Pallas kernels: 17.2 us -> 15.8 us
    pallas_call x1, Pallas kernels: 6.78 us -> 5.95 us  [imaging(): pl.pallas_call(imaging_kernel, out_shape=(pltpu.VMEM((devices, 1, 128), F...]
    pallas_call x1, Pallas kernels: 6.89 us -> 6.28 us  [adjoint(): pl.pallas_call(adjoint_kernel, out_shape=jax.ShapeDtypeStruct((rows, cols...]
    all_to_all x1, waiting for transfers between devices: 2.7 us -> 3.31 us  [shards(): lax.all_to_all(local, ('row', 'col'), split_axis=0, concat_axis=0, tiled=...]
  transfers between devices with their start and end apart: 6 -> 6, of which waited for: 2 -> 2; matrix products, arithmetic and copies ran while one was open for 0% -> 1% of each run, Pallas kernels for 29% -> 26%
where the time goes in v5:
time: 51.2 us; the launch traced here: 50.9 us
  starting transfers between devices  24.8 us (48%)
  Pallas kernels  15.8 us (31%)
  waiting for transfers between devices  5.19 us (10%)
  between operations  3.15 us (6%)
  local copies, waits for them, and re-layouts  1.11 us (2%)
  other arithmetic  0.97 us (2%)
    all_to_all x1, starting transfers between devices, shards(): lax.all_to_all(outbox, ('row', 'col'), split_axis=0, concat_axis=0, tiled...  10.6 us
    ppermute x4, starting transfers between devices, beside(): return (lax.ppermute(last, axis, up), lax.ppermute(first, axis, down))  8.49 us
    pallas_call x1, Pallas kernels, adjoint(): pl.pallas_call(adjoint_kernel, out_shape=jax.ShapeDtypeStruct((rows, cols...  6.28 us
    pallas_call x1, Pallas kernels, imaging(): pl.pallas_call(imaging_kernel, out_shape=(pltpu.VMEM((devices, 1, 128), F...  5.95 us
    all_to_all x1, starting transfers between devices, shards(): lax.all_to_all(local, ('row', 'col'), split_axis=0, concat_axis=0, tiled=...  5.72 us
    all_to_all x1, waiting for transfers between devices, shards(): lax.all_to_all(local, ('row', 'col'), split_axis=0, concat_axis=0, tiled=...  3.31 us
    pallas_call x1, Pallas kernels, make_outbox(): pl.pallas_call(lambda *refs: outbox_kernel(tile_cols, *refs), out_shape=(...  2.45 us
    all_to_all x1, waiting for transfers between devices, shards(): lax.all_to_all(outbox, ('row', 'col'), split_axis=0, concat_axis=0, tiled...  1.87 us
  transfers between devices with their start and end apart: 6, of which 2 were waited for; matrix products, arithmetic and copies ran while one was open for 1% of the time, Pallas kernels for 26%

profile of v5, /device:TPU:1, one launch (start us, length us, event | category | flops | bytes accessed | tf_op | source)
XLA Modules:
  0.0 50.9 jit_solution(11095530079141322556)
XLA Ops:
  1.3 2.4 %shard_map.86 = (s32[128,2,128]{2,1,0:T(2,128)}, f32[128,512]{1,0:T(8,128)S(1)}, f32[16,512]{1,0:T(8,128)S(1)}, f32[16,512]{1,0:T(8,128)S(1)}, f32[128,16]{1,0:T(8,128)S(1)}, /*index=5*/f32[128,16]{1,0:T(8,128)S(1)}) custom-call(s32[1]{0:T(128)S(6)} %copy.9.refs_0_, s32[4,512]{1,0:T(4,128)} %refs_1_.1, s32[1,512]{1,0:T(1,128)} %bitcast.8, ...), custom_call_target="tpu_custom_call" | custom-call | flops 100000000 | bytes 1000000 | tf_op jit(solution)/shard_map/pallas_call | solution.py:91
  3.7 2.8 %collective-permute-start = (f32[128,16]{1,0:T(8,128)S(1)}, f32[128,16]{1,0:T(8,128)S(1)}, u32[]{:S(2)}, u32[]{:S(2)}) collective-permute-start(f32[128,16]{1,0:T(8,128)S(1)} %get-tuple-element.13), channel_id=1, source_target_pairs={{0,1},{1,2},{2,3},{3,4},{4,5},{5,6},{6,7},{7,8},{8,9},{9,10},{10,1... | collective-permute-start | bytes 24584 | tf_op jit(solution)/shard_map/ppermute | solution.py:157
  6.5 0.0 collective-permute-start.1
  6.5 10.6 %all-to-all-start = ((s32[128,2,128]{2,1,0:T(2,128)}), s32[128,2,128]{2,1,0:T(2,128)S(1)}, u32[]{:S(2)}, u32[]{:S(2)}) async-start(s32[128,2,128]{2,1,0:T(2,128)} %get-tuple-element.11), calls=%async_computation | async-start | bytes 262144 | tf_op jit(solution)/shard_map/all_to_all | solution.py:420
  17.1 0.0 copy-start
  17.1 0.9 %copy-done = bf16[8,33,33]{2,0,1:T(8,128)(2,1)S(1)} copy-done((bf16[8,33,33]{2,0,1:T(8,128)(2,1)S(1)}, bf16[8,33,33]{2,0,1:T(8,128)(2,1)}, u32[]{:S(2)}) %copy-start) | copy-done | bytes 17448
  18.0 1.1 %shard_map.87.table_ref = bf16[33,64,256]{2,1,0:T(8,128)(2,1)S(1)} custom-call(bf16[33,8,33]{2,1,0:T(8,128)(2,1)S(1)} %bitcast.7), custom_call_target="tpu_custom_call" | custom-call | flops 10000000000 | bytes 1000000 | tf_op jit(solution)/shard_map/pallas_call | solution.py:142
  19.1 0.1 add_convert_fusion
  19.1 0.1 broadcast_in_dim.10
  19.2 0.1 reshape_reshape.3.wv_ref
  19.3 0.0 collective-permute-done.1.right_ref
  19.3 0.0 collective-permute-done.left_ref
  19.3 0.1 pad_maximum_fusion
  19.4 2.9 %collective-permute-start.2 = (f32[16,544]{1,0:T(8,128)S(1)}, f32[16,544]{1,0:T(8,128)S(1)}, u32[]{:S(2)}, u32[]{:S(2)}) collective-permute-start(f32[16,544]{1,0:T(8,128)S(1)} %pad_maximum_fusion), channel_id=1, source_target_pairs={{0,16},{16,32},{32,48},{48,64},{64,80},{80,96},{96,112},{112,0},{1... | collective-permute-start | bytes 104456 | tf_op jit(solution)/shard_map/ppermute | solution.py:157
  22.3 0.1 pad_maximum_fusion.1
  22.4 2.8 %collective-permute-start.3 = (f32[16,544]{1,0:T(8,128)S(1)}, f32[16,544]{1,0:T(8,128)S(1)}, u32[]{:S(2)}, u32[]{:S(2)}) collective-permute-start(f32[16,544]{1,0:T(8,128)S(1)} %pad_maximum_fusion.1), channel_id=1, source_target_pairs={{16,0},{32,16},{48,32},{64,48},{80,64},{96,80},{112,96},{0,112},{1... | collective-permute-start | bytes 104456 | tf_op jit(solution)/shard_map/ppermute | solution.py:157
  25.2 1.9 %all-to-all-done.inbox_ref = s32[128,2,128]{2,1,0:T(2,128)S(1)} async-done(((s32[128,2,128]{2,1,0:T(2,128)}), s32[128,2,128]{2,1,0:T(2,128)S(1)}, u32[]{:S(2)}, u32[]{:S(2)}) %all-to-all-start) | async-done | bytes 131104 | tf_op jit(solution)/shard_map/all_to_all | solution.py:420
  27.1 0.1 broadcast_in_dim.4.inside_ref
  27.1 5.9 %shard_map.88 = (f32[128,1,128]{2,1,0:T(1,128)}, bf16[112,640]{1,0:T(8,128)(2,1)S(1)}, bf16[2304,256]{1,0:T(8,128)(2,1)S(1)}) custom-call(s32[128,2,128]{2,1,0:T(2,128)S(1)} %all-to-all-done.inbox_ref, bf16[33,64,256]{2,1,0:T(8,128)(2,1)S(1)} %shard_map.87.table_ref, f32[128,512]{1,0:T(8,128)S(1)} %get-tuple-element.12.signed_ref, ...), custom_call_target="tpu_custom_call" | custom-call | flops 4000000000 | bytes 8000000 | tf_op jit(solution)/shard_map/pallas_call | solution.py:317
  33.1 5.7 %all-to-all-start.1 = ((f32[128,1,128]{2,1,0:T(1,128)}), f32[128,1,128]{2,1,0:T(1,128)S(1)}, u32[]{:S(2)}, u32[]{:S(2)}) async-start(f32[128,1,128]{2,1,0:T(1,128)} %get-tuple-element.19), calls=%async_computation.1 | async-start | bytes 131072 | tf_op jit(solution)/shard_map/all_to_all | solution.py:425
  38.8 0.0 collective-permute-done.2.top_ref
  38.8 6.3 %shard_map.89 = f32[128,512]{1,0:T(8,128)} custom-call(bf16[112,640]{1,0:T(8,128)(2,1)S(1)} %get-tuple-element.15.edges_ref, bf16[33,64,256]{2,1,0:T(8,128)(2,1)S(1)} %shard_map.87.table_ref, bf16[2304,256]{1,0:T(8,128)(2,1)S(1)} %get-tuple-element.16.gs_ref, f32[16,544]{1,0:T(8,128)S(1)} %collective-permute-done.2.top_ref, ...), custom_call_target="tpu_custom_call" | custom-call | flops 4000000000 | bytes 10000000 | tf_op jit(solution)/shard_map/pallas_call | solution.py:395
  45.1 3.3 %all-to-all-done.1 = f32[128,1,128]{2,1,0:T(1,128)S(1)} async-done(((f32[128,1,128]{2,1,0:T(1,128)}), f32[128,1,128]{2,1,0:T(1,128)S(1)}, u32[]{:S(2)}, u32[]{:S(2)}) %all-to-all-start.1) | async-done | bytes 65568 | tf_op jit(solution)/shard_map/all_to_all | solution.py:425
  48.4 0.7 %slice_reduce_fusion = f32[]{:T(128)} fusion(f32[128,1,128]{2,1,0:T(1,128)S(1)} %all-to-all-done.1), kind=kLoop, calls=%fused_computation | loop fusion | flops 127 | bytes 516 | tf_op jit(solution)/shard_map/reduce_sum | solution.py:428
  (5 shorter events, 0.0 us)
Async XLA Ops:
  3.7 15.6 %collective-permute-start = (f32[128,16]{1,0:T(8,128)S(1)}, f32[128,16]{1,0:T(8,128)S(1)}, u32[]{:S(2)}, u32[]{:S(2)}) collective-permute-start(f32[128,16]{1,0:T(8,128)S(1)} %get-tuple-element.13), channel_id=1, source_target_pairs={{0,1},{1,2},{2,3},{3,4},{4,5},{5,6},{6,7},{7,8},{8,9},{9,10},{10,1... | collective-permute-start | bytes 24584 | tf_op jit(solution)/shard_map/ppermute | solution.py:157
  6.5 12.8 %collective-permute-start.1 = (f32[128,16]{1,0:T(8,128)S(1)}, f32[128,16]{1,0:T(8,128)S(1)}, u32[]{:S(2)}, u32[]{:S(2)}) collective-permute-start(f32[128,16]{1,0:T(8,128)S(1)} %get-tuple-element.14), channel_id=1, source_target_pairs={{1,0},{2,1},{3,2},{4,3},{5,4},{6,5},{7,6},{8,7},{9,8},{10,9},{11,1... | collective-permute-start | bytes 24584 | tf_op jit(solution)/shard_map/ppermute | solution.py:157
  6.5 20.6 %all-to-all-start = ((s32[128,2,128]{2,1,0:T(2,128)}), s32[128,2,128]{2,1,0:T(2,128)S(1)}, u32[]{:S(2)}, u32[]{:S(2)}) async-start(s32[128,2,128]{2,1,0:T(2,128)} %get-tuple-element.11), calls=%async_computation | async-start | bytes 262144 | tf_op jit(solution)/shard_map/all_to_all | solution.py:420
  17.1 0.9 %copy-start = (bf16[8,33,33]{2,0,1:T(8,128)(2,1)S(1)}, bf16[8,33,33]{2,0,1:T(8,128)(2,1)}, u32[]{:S(2)}) copy-start(bf16[8,33,33]{2,0,1:T(8,128)(2,1)} %param.12) | copy-start | bytes 52276
  17.9 1.2 %copy-start.1 = (f32[4]{0:T(128)S(1)}, f32[4]{0:T(128)}, u32[]{:S(2)}) copy-start(f32[4]{0:T(128)} %param.13) | copy-start | bytes 52
  19.4 19.4 %collective-permute-start.2 = (f32[16,544]{1,0:T(8,128)S(1)}, f32[16,544]{1,0:T(8,128)S(1)}, u32[]{:S(2)}, u32[]{:S(2)}) collective-permute-start(f32[16,544]{1,0:T(8,128)S(1)} %pad_maximum_fusion), channel_id=1, source_target_pairs={{0,16},{16,32},{32,48},{48,64},{64,80},{80,96},{96,112},{112,0},{1... | collective-permute-start | bytes 104456 | tf_op jit(solution)/shard_map/ppermute | solution.py:157
  22.4 16.5 %collective-permute-start.3 = (f32[16,544]{1,0:T(8,128)S(1)}, f32[16,544]{1,0:T(8,128)S(1)}, u32[]{:S(2)}, u32[]{:S(2)}) collective-permute-start(f32[16,544]{1,0:T(8,128)S(1)} %pad_maximum_fusion.1), channel_id=1, source_target_pairs={{16,0},{32,16},{48,32},{64,48},{80,64},{96,80},{112,96},{0,112},{1... | collective-permute-start | bytes 104456 | tf_op jit(solution)/shard_map/ppermute | solution.py:157
  33.1 15.3 %all-to-all-start.1 = ((f32[128,1,128]{2,1,0:T(1,128)}), f32[128,1,128]{2,1,0:T(1,128)S(1)}, u32[]{:S(2)}, u32[]{:S(2)}) async-start(f32[128,1,128]{2,1,0:T(1,128)} %get-tuple-element.19), calls=%async_computation.1 | async-start | bytes 131072 | tf_op jit(solution)/shard_map/all_to_all | solution.py:425

commit v6 on v5

--- a/solution.py
+++ b/solution.py
@@ -29,7 +29,7 @@
 def outbox_kernel(
     tile_cols, counts_ref, rects_ref, owner_ref, target_ref, weight_ref,
     out_ref, signed_ref, top_ref, bottom_ref, left_ref, right_ref,
-    pad_ref, target_buf, weight_buf, sems,
+    pad_ref, box_ref, target_buf, weight_buf, sems,
 ):
     rows, cols = signed_ref.shape
     load_target = pltpu.make_async_copy(target_ref, target_buf, sems.at[0])
@@ -69,8 +69,10 @@
         start = 24 + dr * tile_cols + dc
         inside = (column + dc >= 0) & (column + dc < tile_cols) & (group == n)
         result = jnp.where(inside, pad_ref[start : start + tiles, :], result)
-    out_ref[:, 0, :] = result
-    out_ref[:, 1, :] = word
+    box_ref[:, 0, :] = result
+    box_ref[:, 1, :] = word
+    store = pltpu.make_async_copy(box_ref, out_ref, sems.at[2])
+    store.start()
     load_target.wait()
     load_weight.wait()
     signed_ref[...] = jnp.where(target_buf[...] > 0, weight_buf[...], -weight_buf[...])
@@ -78,6 +80,7 @@
     bottom_ref[...] = signed_ref[rows - RAD : rows, :]
     left_ref[...] = signed_ref[:, 0:RAD]
     right_ref[...] = signed_ref[:, cols - RAD : cols]
+    store.wait()
 
 
 SMALL = pl.BlockSpec(memory_space=pltpu.SMEM)
@@ -91,7 +94,7 @@
     return pl.pallas_call(
         lambda *refs: outbox_kernel(tile_cols, *refs),
         out_shape=(
-            pltpu.VMEM((tiles, 2, 128), jnp.int32),
+            jax.ShapeDtypeStruct((tiles, 2, 128), jnp.int32),
             pltpu.VMEM((rows, cols), F32),
             pltpu.VMEM((RAD, cols), F32),
             pltpu.VMEM((RAD, cols), F32),
@@ -99,11 +102,13 @@
             pltpu.VMEM((rows, RAD), F32),
         ),
         in_specs=[SMALL, WHOLE, WHOLE, ANYWHERE, ANYWHERE],
+        out_specs=(ANYWHERE,) + (WHOLE,) * 5,
         scratch_shapes=[
             pltpu.VMEM((tiles + 48, 128), jnp.int32),
+            pltpu.VMEM((tiles, 2, 128), jnp.int32),
             pltpu.VMEM((rows, cols), jnp.int32),
             pltpu.VMEM((rows, cols), F32),
-            pltpu.SemaphoreType.DMA((2,)),
+            pltpu.SemaphoreType.DMA((3,)),
         ],
         cost_estimate=pl.CostEstimate(flops=10**8, bytes_accessed=10**6, transcendentals=0),
     )(counts, rects, owner.reshape(1, slots), target, weight)

time: 51.2 us -> 50.9 us (level)
  no operation moved by 1% of the time
where the time goes in v6:
time: 50.9 us; the launch traced here: 50.6 us
  starting transfers between devices  24.7 us (49%)
  Pallas kernels  15.5 us (30%)
  waiting for transfers between devices  5.17 us (10%)
  between operations  3.15 us (6%)
  local copies, waits for them, and re-layouts  1.11 us (2%)
  other arithmetic  0.97 us (2%)
    all_to_all x1, starting transfers between devices, shards(): lax.all_to_all(outbox, ('row', 'col'), split_axis=0, concat_axis=0, tiled...  10.5 us
    ppermute x4, starting transfers between devices, beside(): return (lax.ppermute(last, axis, up), lax.ppermute(first, axis, down))  8.49 us
    pallas_call x1, Pallas kernels, adjoint(): pl.pallas_call(adjoint_kernel, out_shape=jax.ShapeDtypeStruct((rows, cols...  6.32 us
    pallas_call x1, Pallas kernels, imaging(): pl.pallas_call(imaging_kernel, out_shape=(pltpu.VMEM((devices, 1, 128), F...  5.96 us
    all_to_all x1, starting transfers between devices, shards(): lax.all_to_all(local, ('row', 'col'), split_axis=0, concat_axis=0, tiled=...  5.7 us
    all_to_all x1, waiting for transfers between devices, shards(): lax.all_to_all(local, ('row', 'col'), split_axis=0, concat_axis=0, tiled=...  3.27 us
    pallas_call x1, Pallas kernels, make_outbox(): pl.pallas_call(lambda *refs: outbox_kernel(tile_cols, *refs), out_shape=(...  2.1 us
    all_to_all x1, waiting for transfers between devices, shards(): lax.all_to_all(outbox, ('row', 'col'), split_axis=0, concat_axis=0, tiled...  1.89 us
  transfers between devices with their start and end apart: 6, of which 2 were waited for; matrix products, arithmetic and copies ran while one was open for 1% of the time, Pallas kernels for 26%

profile of v6, /device:TPU:1, one launch (start us, length us, event | category | flops | bytes accessed | tf_op | source)
XLA Modules:
  0.0 50.6 jit_solution(7690095344401830081)
XLA Ops:
  1.3 2.1 %shard_map.86 = (s32[128,2,128]{2,1,0:T(2,128)}, f32[128,512]{1,0:T(8,128)S(1)}, f32[16,512]{1,0:T(8,128)S(1)}, f32[16,512]{1,0:T(8,128)S(1)}, f32[128,16]{1,0:T(8,128)S(1)}, /*index=5*/f32[128,16]{1,0:T(8,128)S(1)}) custom-call(s32[1]{0:T(128)S(6)} %copy.9.refs_0_, s32[4,512]{1,0:T(4,128)} %refs_1_.1, s32[1,512]{1,0:T(1,128)} %bitcast.8, ...), custom_call_target="tpu_custom_call" | custom-call | flops 100000000 | bytes 1000000 | tf_op jit(solution)/shard_map/pallas_call | solution.py:94
  3.4 2.8 %collective-permute-start = (f32[128,16]{1,0:T(8,128)S(1)}, f32[128,16]{1,0:T(8,128)S(1)}, u32[]{:S(2)}, u32[]{:S(2)}) collective-permute-start(f32[128,16]{1,0:T(8,128)S(1)} %get-tuple-element.13), channel_id=1, source_target_pairs={{0,1},{1,2},{2,3},{3,4},{4,5},{5,6},{6,7},{7,8},{8,9},{9,10},{10,1... | collective-permute-start | bytes 24584 | tf_op jit(solution)/shard_map/ppermute | solution.py:162
  6.1 0.0 collective-permute-start.1
  6.1 10.5 %all-to-all-start = ((s32[128,2,128]{2,1,0:T(2,128)}), s32[128,2,128]{2,1,0:T(2,128)S(1)}, u32[]{:S(2)}, u32[]{:S(2)}) async-start(s32[128,2,128]{2,1,0:T(2,128)} %get-tuple-element.11), calls=%async_computation | async-start | bytes 262144 | tf_op jit(solution)/shard_map/all_to_all | solution.py:425
  16.7 0.0 copy-start
  16.7 0.9 %copy-done = bf16[8,33,33]{2,0,1:T(8,128)(2,1)S(1)} copy-done((bf16[8,33,33]{2,0,1:T(8,128)(2,1)S(1)}, bf16[8,33,33]{2,0,1:T(8,128)(2,1)}, u32[]{:S(2)}) %copy-start) | copy-done | bytes 17448
  17.6 1.1 %shard_map.87.table_ref = bf16[33,64,256]{2,1,0:T(8,128)(2,1)S(1)} custom-call(bf16[33,8,33]{2,1,0:T(8,128)(2,1)S(1)} %bitcast.7), custom_call_target="tpu_custom_call" | custom-call | flops 10000000000 | bytes 1000000 | tf_op jit(solution)/shard_map/pallas_call | solution.py:147
  18.7 0.1 add_convert_fusion
  18.8 0.1 broadcast_in_dim.10
  18.8 0.1 reshape_reshape.3.wv_ref
  18.9 0.0 collective-permute-done.left_ref
  19.0 0.1 pad_maximum_fusion
  19.0 2.9 %collective-permute-start.2 = (f32[16,544]{1,0:T(8,128)S(1)}, f32[16,544]{1,0:T(8,128)S(1)}, u32[]{:S(2)}, u32[]{:S(2)}) collective-permute-start(f32[16,544]{1,0:T(8,128)S(1)} %pad_maximum_fusion), channel_id=1, source_target_pairs={{0,16},{16,32},{32,48},{48,64},{64,80},{80,96},{96,112},{112,0},{1... | collective-permute-start | bytes 104456 | tf_op jit(solution)/shard_map/ppermute | solution.py:162
  21.9 0.1 pad_maximum_fusion.1
  22.0 2.8 %collective-permute-start.3 = (f32[16,544]{1,0:T(8,128)S(1)}, f32[16,544]{1,0:T(8,128)S(1)}, u32[]{:S(2)}, u32[]{:S(2)}) collective-permute-start(f32[16,544]{1,0:T(8,128)S(1)} %pad_maximum_fusion.1), channel_id=1, source_target_pairs={{16,0},{32,16},{48,32},{64,48},{80,64},{96,80},{112,96},{0,112},{1... | collective-permute-start | bytes 104456 | tf_op jit(solution)/shard_map/ppermute | solution.py:162
  24.8 1.9 %all-to-all-done.inbox_ref = s32[128,2,128]{2,1,0:T(2,128)S(1)} async-done(((s32[128,2,128]{2,1,0:T(2,128)}), s32[128,2,128]{2,1,0:T(2,128)S(1)}, u32[]{:S(2)}, u32[]{:S(2)}) %all-to-all-start) | async-done | bytes 131104 | tf_op jit(solution)/shard_map/all_to_all | solution.py:425
  26.7 0.1 broadcast_in_dim.4.inside_ref
  26.8 6.0 %shard_map.88 = (f32[128,1,128]{2,1,0:T(1,128)}, bf16[112,640]{1,0:T(8,128)(2,1)S(1)}, bf16[2304,256]{1,0:T(8,128)(2,1)S(1)}) custom-call(s32[128,2,128]{2,1,0:T(2,128)S(1)} %all-to-all-done.inbox_ref, bf16[33,64,256]{2,1,0:T(8,128)(2,1)S(1)} %shard_map.87.table_ref, f32[128,512]{1,0:T(8,128)S(1)} %get-tuple-element.12.signed_ref, ...), custom_call_target="tpu_custom_call" | custom-call | flops 4000000000 | bytes 8000000 | tf_op jit(solution)/shard_map/pallas_call | solution.py:322
  32.8 5.7 %all-to-all-start.1 = ((f32[128,1,128]{2,1,0:T(1,128)}), f32[128,1,128]{2,1,0:T(1,128)S(1)}, u32[]{:S(2)}, u32[]{:S(2)}) async-start(f32[128,1,128]{2,1,0:T(1,128)} %get-tuple-element.19), calls=%async_computation.1 | async-start | bytes 131072 | tf_op jit(solution)/shard_map/all_to_all | solution.py:430
  38.5 0.0 collective-permute-done.2.top_ref
  38.5 0.0 collective-permute-done.3.bottom_ref
  38.5 6.3 %shard_map.89 = f32[128,512]{1,0:T(8,128)} custom-call(bf16[112,640]{1,0:T(8,128)(2,1)S(1)} %get-tuple-element.15.edges_ref, bf16[33,64,256]{2,1,0:T(8,128)(2,1)S(1)} %shard_map.87.table_ref, bf16[2304,256]{1,0:T(8,128)(2,1)S(1)} %get-tuple-element.16.gs_ref, f32[16,544]{1,0:T(8,128)S(1)} %collective-permute-done.2.top_ref, ...), custom_call_target="tpu_custom_call" | custom-call | flops 4000000000 | bytes 10000000 | tf_op jit(solution)/shard_map/pallas_call | solution.py:400
  44.8 3.3 %all-to-all-done.1 = f32[128,1,128]{2,1,0:T(1,128)S(1)} async-done(((f32[128,1,128]{2,1,0:T(1,128)}), f32[128,1,128]{2,1,0:T(1,128)S(1)}, u32[]{:S(2)}, u32[]{:S(2)}) %all-to-all-start.1) | async-done | bytes 65568 | tf_op jit(solution)/shard_map/all_to_all | solution.py:430
  48.1 0.7 %slice_reduce_fusion = f32[]{:T(128)} fusion(f32[128,1,128]{2,1,0:T(1,128)S(1)} %all-to-all-done.1), kind=kLoop, calls=%fused_computation | loop fusion | flops 127 | bytes 516 | tf_op jit(solution)/shard_map/reduce_sum | solution.py:433
  (5 shorter events, 0.0 us)
Async XLA Ops:
  3.4 15.6 %collective-permute-start = (f32[128,16]{1,0:T(8,128)S(1)}, f32[128,16]{1,0:T(8,128)S(1)}, u32[]{:S(2)}, u32[]{:S(2)}) collective-permute-start(f32[128,16]{1,0:T(8,128)S(1)} %get-tuple-element.13), channel_id=1, source_target_pairs={{0,1},{1,2},{2,3},{3,4},{4,5},{5,6},{6,7},{7,8},{8,9},{9,10},{10,1... | collective-permute-start | bytes 24584 | tf_op jit(solution)/shard_map/ppermute | solution.py:162
  6.1 12.8 %collective-permute-start.1 = (f32[128,16]{1,0:T(8,128)S(1)}, f32[128,16]{1,0:T(8,128)S(1)}, u32[]{:S(2)}, u32[]{:S(2)}) collective-permute-start(f32[128,16]{1,0:T(8,128)S(1)} %get-tuple-element.14), channel_id=1, source_target_pairs={{1,0},{2,1},{3,2},{4,3},{5,4},{6,5},{7,6},{8,7},{9,8},{10,9},{11,1... | collective-permute-start | bytes 24584 | tf_op jit(solution)/shard_map/ppermute | solution.py:162
  6.1 20.6 %all-to-all-start = ((s32[128,2,128]{2,1,0:T(2,128)}), s32[128,2,128]{2,1,0:T(2,128)S(1)}, u32[]{:S(2)}, u32[]{:S(2)}) async-start(s32[128,2,128]{2,1,0:T(2,128)} %get-tuple-element.11), calls=%async_computation | async-start | bytes 262144 | tf_op jit(solution)/shard_map/all_to_all | solution.py:425
  16.7 0.9 %copy-start = (bf16[8,33,33]{2,0,1:T(8,128)(2,1)S(1)}, bf16[8,33,33]{2,0,1:T(8,128)(2,1)}, u32[]{:S(2)}) copy-start(bf16[8,33,33]{2,0,1:T(8,128)(2,1)} %param.12) | copy-start | bytes 52276
  17.6 1.2 %copy-start.1 = (f32[4]{0:T(128)S(1)}, f32[4]{0:T(128)}, u32[]{:S(2)}) copy-start(f32[4]{0:T(128)} %param.13) | copy-start | bytes 52
  19.0 19.4 %collective-permute-start.2 = (f32[16,544]{1,0:T(8,128)S(1)}, f32[16,544]{1,0:T(8,128)S(1)}, u32[]{:S(2)}, u32[]{:S(2)}) collective-permute-start(f32[16,544]{1,0:T(8,128)S(1)} %pad_maximum_fusion), channel_id=1, source_target_pairs={{0,16},{16,32},{32,48},{48,64},{64,80},{80,96},{96,112},{112,0},{1... | collective-permute-start | bytes 104456 | tf_op jit(solution)/shard_map/ppermute | solution.py:162
  22.0 16.5 %collective-permute-start.3 = (f32[16,544]{1,0:T(8,128)S(1)}, f32[16,544]{1,0:T(8,128)S(1)}, u32[]{:S(2)}, u32[]{:S(2)}) collective-permute-start(f32[16,544]{1,0:T(8,128)S(1)} %pad_maximum_fusion.1), channel_id=1, source_target_pairs={{16,0},{32,16},{48,32},{64,48},{80,64},{96,80},{112,96},{0,112},{1... | collective-permute-start | bytes 104456 | tf_op jit(solution)/shard_map/ppermute | solution.py:162
  32.8 15.3 %all-to-all-start.1 = ((f32[128,1,128]{2,1,0:T(1,128)}), f32[128,1,128]{2,1,0:T(1,128)S(1)}, u32[]{:S(2)}, u32[]{:S(2)}) async-start(f32[128,1,128]{2,1,0:T(1,128)} %get-tuple-element.19), calls=%async_computation.1 | async-start | bytes 131072 | tf_op jit(solution)/shard_map/all_to_all | solution.py:430

commit v7 on v6

--- a/solution.py
+++ b/solution.py
@@ -27,8 +27,8 @@
 
 
 def outbox_kernel(
-    tile_cols, counts_ref, rects_ref, owner_ref, target_ref, weight_ref,
-    out_ref, signed_ref, top_ref, bottom_ref, left_ref, right_ref,
+    tile_cols, counts_ref, rects_ref, owner_ref, target_ref, weight_ref, kernel_ref,
+    out_ref, signed_ref, top_ref, bottom_ref, left_ref, right_ref, kernel_out_ref,
     pad_ref, box_ref, target_buf, weight_buf, sems,
 ):
     rows, cols = signed_ref.shape
@@ -36,6 +36,8 @@
     load_weight = pltpu.make_async_copy(weight_ref, weight_buf, sems.at[1])
     load_target.start()
     load_weight.start()
+    load_kernel = pltpu.make_async_copy(kernel_ref, kernel_out_ref, sems.at[3])
+    load_kernel.start()
     slots = owner_ref.shape[1]
     tiles = out_ref.shape[0]
     live = iota((1, slots), 1) < counts_ref[0]
@@ -80,6 +82,7 @@
     bottom_ref[...] = signed_ref[rows - RAD : rows, :]
     left_ref[...] = signed_ref[:, 0:RAD]
     right_ref[...] = signed_ref[:, cols - RAD : cols]
+    load_kernel.wait()
     store.wait()
 
 
@@ -88,7 +91,7 @@
 ANYWHERE = pl.BlockSpec(memory_space=pl.ANY)
 
 
-def make_outbox(rects, owner, counts, target, weight, tiles, tile_cols):
+def make_outbox(rects, owner, counts, target, weight, kernel, tiles, tile_cols):
     slots = owner.shape[0]
     rows, cols = target.shape
     return pl.pallas_call(
@@ -100,18 +103,19 @@
             pltpu.VMEM((RAD, cols), F32),
             pltpu.VMEM((rows, RAD), F32),
             pltpu.VMEM((rows, RAD), F32),
+            pltpu.VMEM(kernel.shape, BF16),
         ),
-        in_specs=[SMALL, WHOLE, WHOLE, ANYWHERE, ANYWHERE],
-        out_specs=(ANYWHERE,) + (WHOLE,) * 5,
+        in_specs=[SMALL, WHOLE, WHOLE, ANYWHERE, ANYWHERE, ANYWHERE],
+        out_specs=(ANYWHERE,) + (WHOLE,) * 6,
         scratch_shapes=[
             pltpu.VMEM((tiles + 48, 128), jnp.int32),
             pltpu.VMEM((tiles, 2, 128), jnp.int32),
             pltpu.VMEM((rows, cols), jnp.int32),
             pltpu.VMEM((rows, cols), F32),
-            pltpu.SemaphoreType.DMA((3,)),
+            pltpu.SemaphoreType.DMA((4,)),
         ],
         cost_estimate=pl.CostEstimate(flops=10**8, bytes_accessed=10**6, transcendentals=0),
-    )(counts, rects, owner.reshape(1, slots), target, weight)
+    )(counts, rects, owner.reshape(1, slots), target, weight, kernel)
 
 
 def tables_kernel(kernel_ref, table_ref, wide_ref):
@@ -143,7 +147,7 @@
 
 
 def make_tables(kernel):
-    lanes = kernel.shape[0] * BLK
+    lanes = kernel.shape[1] * BLK
     return pl.pallas_call(
         tables_kernel,
         out_shape=pltpu.VMEM((KS, 2 * BLK, lanes), BF16),
@@ -151,7 +155,7 @@
         scratch_shapes=[pltpu.VMEM((lanes // 128, KS * WIDE + 8, 128), F32)],
         compiler_params=pltpu.CompilerParams(vmem_limit_bytes=VMEM_LIMIT // 2),
         cost_estimate=pl.CostEstimate(flops=10**10, bytes_accessed=10**6, transcendentals=0),
-    )(kernel.transpose(1, 0, 2))
+    )(kernel)
 
 
 def weight_strips(top_rows, bottom_rows, left_cols, right_cols):
@@ -161,6 +165,9 @@
         down = [(j, i) for i, j in up]
         return lax.ppermute(last, axis, up), lax.ppermute(first, axis, down)
 
+    c = lax.axis_index("col")
+    left_cols = jnp.where(c > 0, left_cols, 0.0)
+    right_cols = jnp.where(c < lax.axis_size("col") - 1, right_cols, 0.0)
     left, right = beside(left_cols, right_cols, "col")
     last = right.shape[0] - RAD
     top, bottom = beside(
@@ -421,9 +428,11 @@
     col_devices = lax.axis_size("col")
     devices = row_devices * col_devices
     rows, cols = target.shape
-    outbox, signed, *strips = make_outbox(rects, owner, counts, target, loss_weight, devices, col_devices)
+    outbox, signed, *strips, by_row = make_outbox(
+        rects, owner, counts, target, loss_weight, kernel.transpose(1, 0, 2), devices, col_devices
+    )
     inbox = lax.all_to_all(outbox, ("row", "col"), split_axis=0, concat_axis=0, tiled=True)
-    table = make_tables(kernel)
+    table = make_tables(by_row)
     top, bottom, left, right, inside = weight_strips(*strips)
     wv = jnp.repeat(socs_weight, 2 * BLK).reshape(1, kernel.shape[0] * BLK)
     local, edges, gs = imaging(inbox, table, signed, left, right, inside, wv, devices)

time: 50.9 us -> 50.1 us (0.984)
  local copies, waits for them, and re-layouts: 1.11 us -> 0.23 us
  waiting for transfers between devices: 5.17 us -> 6.03 us
  starting transfers between devices: 24.7 us -> 23.9 us
    unnamed x4 -> x2, local copies, waits for them, and re-layouts: 0.88 us -> 0.01 us
    all_to_all x1, starting transfers between devices: 5.7 us -> 4.84 us  [shards(): lax.all_to_all(local, ('row', 'col'), split_axis=0, concat_axis=0, tiled=...]
    all_to_all x1, waiting for transfers between devices: 1.89 us -> 2.76 us  [shards(): lax.all_to_all(outbox, ('row', 'col'), split_axis=0, concat_axis=0, tiled...]
  transfers between devices with their start and end apart: 6 -> 6, of which waited for: 2 -> 2; matrix products, arithmetic and copies ran while one was open for 1% -> 1% of each run, Pallas kernels for 26% -> 27%
where the time goes in v7:
time: 50.1 us; the launch traced here: 49.8 us
  starting transfers between devices  23.9 us (48%)
  Pallas kernels  15.5 us (31%)
  waiting for transfers between devices  6.03 us (12%)
  between operations  3.17 us (6%)
  other arithmetic  0.98 us (2%)
    all_to_all x1, starting transfers between devices, shards(): lax.all_to_all(outbox, ('row', 'col'), split_axis=0, concat_axis=0, tiled...  10.5 us
    ppermute x4, starting transfers between devices, beside(): return (lax.ppermute(last, axis, up), lax.ppermute(first, axis, down))  8.56 us
    pallas_call x1, Pallas kernels, adjoint(): pl.pallas_call(adjoint_kernel, out_shape=jax.ShapeDtypeStruct((rows, cols...  6.33 us
    pallas_call x1, Pallas kernels, imaging(): pl.pallas_call(imaging_kernel, out_shape=(pltpu.VMEM((devices, 1, 128), F...  5.96 us
    all_to_all x1, starting transfers between devices, shards(): lax.all_to_all(local, ('row', 'col'), split_axis=0, concat_axis=0, tiled=...  4.84 us
    all_to_all x1, waiting for transfers between devices, shards(): lax.all_to_all(local, ('row', 'col'), split_axis=0, concat_axis=0, tiled=...  3.26 us
    all_to_all x1, waiting for transfers between devices, shards(): lax.all_to_all(outbox, ('row', 'col'), split_axis=0, concat_axis=0, tiled...  2.76 us
    pallas_call x1, Pallas kernels, make_outbox(): pl.pallas_call(lambda *refs: outbox_kernel(tile_cols, *refs), out_shape=(...  2.11 us
  transfers between devices with their start and end apart: 6, of which 2 were waited for; matrix products, arithmetic and copies ran while one was open for 1% of the time, Pallas kernels for 27%

profile of v7, /device:TPU:1, one launch (start us, length us, event | category | flops | bytes accessed | tf_op | source)
XLA Modules:
  0.0 49.8 jit_solution(10601131300819883160)
XLA Ops:
  1.3 2.1 %shard_map.86 = (s32[128,2,128]{2,1,0:T(2,128)}, f32[128,512]{1,0:T(8,128)S(1)}, f32[16,512]{1,0:T(8,128)S(1)}, f32[16,512]{1,0:T(8,128)S(1)}, f32[128,16]{1,0:T...) custom-call(s32[1]{0:T(128)S(6)} %copy.9.refs_0_, s32[4,512]{1,0:T(4,128)} %refs_1_.1, ...), custom_call_target="tpu_custom_call" | custom-call | flops 100000000 | bytes 1000000 | tf_op jit(solution)/shard_map/pallas_call | solution.py:97
  3.4 2.8 %collective-permute-start = (f32[128,16]{1,0:T(8,128)S(1)}, f32[128,16]{1,0:T(8,128)S(1)}, u32[]{:S(2)}, u32[]{:S(2)}) collective-permute-start(f32[128,16]{1,0:T(8,128)S(1)} %broadcast_select_fusion.1), channel_id=1, source_target_pairs={{0,1},{1,2},{2,3},{3,4},{4,5},{5,6},{6,7},{7,8},{8,9},{9,10},{10,1... | collective-permute-start | bytes 24584 | tf_op jit(solution)/shard_map/ppermute | solution.py:166
  6.2 0.1 collective-permute-start.1
  6.3 10.5 %all-to-all-start = ((s32[128,2,128]{2,1,0:T(2,128)}), s32[128,2,128]{2,1,0:T(2,128)S(1)}, u32[]{:S(2)}, u32[]{:S(2)}) async-start(s32[128,2,128]{2,1,0:T(2,128)} %get-tuple-element.12), calls=%async_computation | async-start | bytes 262144 | tf_op jit(solution)/shard_map/all_to_all | solution.py:434
  16.8 0.0 copy-start
  16.8 1.1 %shard_map.87.table_ref = bf16[33,64,256]{2,1,0:T(8,128)(2,1)S(1)} custom-call(bf16[33,8,33]{2,1,0:T(8,128)(2,1)S(1)} %get-tuple-element.13.kernel_ref), custom_call_target="tpu_custom_call" | custom-call | flops 10000000000 | bytes 1000000 | tf_op jit(solution)/shard_map/pallas_call | solution.py:151
  17.9 0.1 add_convert_fusion
  18.0 0.1 broadcast_in_dim.16
  18.1 0.1 reshape_reshape.3.wv_ref
  18.2 0.0 collective-permute-done.1.right_ref
  18.2 0.0 collective-permute-done.left_ref
  18.2 0.1 pad_maximum_fusion
  18.3 2.9 %collective-permute-start.2 = (f32[16,544]{1,0:T(8,128)S(1)}, f32[16,544]{1,0:T(8,128)S(1)}, u32[]{:S(2)}, u32[]{:S(2)}) collective-permute-start(f32[16,544]{1,0:T(8,128)S(1)} %pad_maximum_fusion), channel_id=1, source_target_pairs={{0,16},{16,32},{32,48},{48,64},{64,80},{80,96},{96,112},{112,0},{1... | collective-permute-start | bytes 104456 | tf_op jit(solution)/shard_map/ppermute | solution.py:166
  21.2 0.1 pad_maximum_fusion.1
  21.3 2.8 %collective-permute-start.3 = (f32[16,544]{1,0:T(8,128)S(1)}, f32[16,544]{1,0:T(8,128)S(1)}, u32[]{:S(2)}, u32[]{:S(2)}) collective-permute-start(f32[16,544]{1,0:T(8,128)S(1)} %pad_maximum_fusion.1), channel_id=1, source_target_pairs={{16,0},{32,16},{48,32},{64,48},{80,64},{96,80},{112,96},{0,112},{1... | collective-permute-start | bytes 104456 | tf_op jit(solution)/shard_map/ppermute | solution.py:166
  24.1 2.8 %all-to-all-done.inbox_ref = s32[128,2,128]{2,1,0:T(2,128)S(1)} async-done(((s32[128,2,128]{2,1,0:T(2,128)}), s32[128,2,128]{2,1,0:T(2,128)S(1)}, u32[]{:S(2)}, u32[]{:S(2)}) %all-to-all-start) | async-done | bytes 131104 | tf_op jit(solution)/shard_map/all_to_all | solution.py:434
  26.8 0.1 broadcast_in_dim.15.inside_ref
  26.9 6.0 %shard_map.88 = (f32[128,1,128]{2,1,0:T(1,128)}, bf16[112,640]{1,0:T(8,128)(2,1)S(1)}, bf16[2304,256]{1,0:T(8,128)(2,1)S(1)}) custom-call(s32[128,2,128]{2,1,0:T(2,128)S(1)} %all-to-all-done.inbox_ref, bf16[33,64,256]{2,1,0:T(8,128)(2,1)S(1)} %shard_map.87.table_ref, f32[128,512]{1,0:T(8,128)S(1)} %get-tuple-element.14.signed_ref, ...), custom_call_target="tpu_custom_call" | custom-call | flops 4000000000 | bytes 8000000 | tf_op jit(solution)/shard_map/pallas_call | solution.py:329
  32.9 4.8 %all-to-all-start.1 = ((f32[128,1,128]{2,1,0:T(1,128)}), f32[128,1,128]{2,1,0:T(1,128)S(1)}, u32[]{:S(2)}, u32[]{:S(2)}) async-start(f32[128,1,128]{2,1,0:T(1,128)} %get-tuple-element.21), calls=%async_computation.1 | async-start | bytes 131072 | tf_op jit(solution)/shard_map/all_to_all | solution.py:439
  37.7 0.0 collective-permute-done.2.top_ref
  37.7 0.0 collective-permute-done.3.bottom_ref
  37.7 6.3 %shard_map.89 = f32[128,512]{1,0:T(8,128)} custom-call(bf16[112,640]{1,0:T(8,128)(2,1)S(1)} %get-tuple-element.17.edges_ref, bf16[33,64,256]{2,1,0:T(8,128)(2,1)S(1)} %shard_map.87.table_ref, bf16[2304,256]{1,0:T(8,128)(2,1)S(1)} %get-tuple-element.18.gs_ref, f32[16,544]{1,0:T(8,128)S(1)} %collective-permute-done.2.top_ref, ...), custom_call_target="tpu_custom_call" | custom-call | flops 4000000000 | bytes 10000000 | tf_op jit(solution)/shard_map/pallas_call | solution.py:407
  44.1 3.3 %all-to-all-done.1 = f32[128,1,128]{2,1,0:T(1,128)S(1)} async-done(((f32[128,1,128]{2,1,0:T(1,128)}), f32[128,1,128]{2,1,0:T(1,128)S(1)}, u32[]{:S(2)}, u32[]{:S(2)}) %all-to-all-start.1) | async-done | bytes 65568 | tf_op jit(solution)/shard_map/all_to_all | solution.py:439
  47.3 0.7 %slice_reduce_fusion = f32[]{:T(128)} fusion(f32[128,1,128]{2,1,0:T(1,128)S(1)} %all-to-all-done.1), kind=kLoop, calls=%fused_computation | loop fusion | flops 127 | bytes 516 | tf_op jit(solution)/shard_map/reduce_sum | solution.py:442
  (5 shorter events, 0.0 us)
Async XLA Ops:
  3.4 14.8 %collective-permute-start = (f32[128,16]{1,0:T(8,128)S(1)}, f32[128,16]{1,0:T(8,128)S(1)}, u32[]{:S(2)}, u32[]{:S(2)}) collective-permute-start(f32[128,16]{1,0:T(8,128)S(1)} %broadcast_select_fusion.1), channel_id=1, source_target_pairs={{0,1},{1,2},{2,3},{3,4},{4,5},{5,6},{6,7},{7,8},{8,9},{9,10},{10,1... | collective-permute-start | bytes 24584 | tf_op jit(solution)/shard_map/ppermute | solution.py:166
  6.2 12.0 %collective-permute-start.1 = (f32[128,16]{1,0:T(8,128)S(1)}, f32[128,16]{1,0:T(8,128)S(1)}, u32[]{:S(2)}, u32[]{:S(2)}) collective-permute-start(f32[128,16]{1,0:T(8,128)S(1)} %broadcast_select_fusion), channel_id=1, source_target_pairs={{1,0},{2,1},{3,2},{4,3},{5,4},{6,5},{7,6},{8,7},{9,8},{10,9},{11,1... | collective-permute-start | bytes 24584 | tf_op jit(solution)/shard_map/ppermute | solution.py:166
  6.3 20.6 %all-to-all-start = ((s32[128,2,128]{2,1,0:T(2,128)}), s32[128,2,128]{2,1,0:T(2,128)S(1)}, u32[]{:S(2)}, u32[]{:S(2)}) async-start(s32[128,2,128]{2,1,0:T(2,128)} %get-tuple-element.12), calls=%async_computation | async-start | bytes 262144 | tf_op jit(solution)/shard_map/all_to_all | solution.py:434
  16.8 1.2 %copy-start = (f32[4]{0:T(128)S(1)}, f32[4]{0:T(128)}, u32[]{:S(2)}) copy-start(f32[4]{0:T(128)} %param.13) | copy-start | bytes 52
  18.3 19.4 %collective-permute-start.2 = (f32[16,544]{1,0:T(8,128)S(1)}, f32[16,544]{1,0:T(8,128)S(1)}, u32[]{:S(2)}, u32[]{:S(2)}) collective-permute-start(f32[16,544]{1,0:T(8,128)S(1)} %pad_maximum_fusion), channel_id=1, source_target_pairs={{0,16},{16,32},{32,48},{48,64},{64,80},{80,96},{96,112},{112,0},{1... | collective-permute-start | bytes 104456 | tf_op jit(solution)/shard_map/ppermute | solution.py:166
  21.3 16.5 %collective-permute-start.3 = (f32[16,544]{1,0:T(8,128)S(1)}, f32[16,544]{1,0:T(8,128)S(1)}, u32[]{:S(2)}, u32[]{:S(2)}) collective-permute-start(f32[16,544]{1,0:T(8,128)S(1)} %pad_maximum_fusion.1), channel_id=1, source_target_pairs={{16,0},{32,16},{48,32},{64,48},{80,64},{96,80},{112,96},{0,112},{1... | collective-permute-start | bytes 104456 | tf_op jit(solution)/shard_map/ppermute | solution.py:166
  32.9 14.4 %all-to-all-start.1 = ((f32[128,1,128]{2,1,0:T(1,128)}), f32[128,1,128]{2,1,0:T(1,128)S(1)}, u32[]{:S(2)}, u32[]{:S(2)}) async-start(f32[128,1,128]{2,1,0:T(1,128)} %get-tuple-element.21), calls=%async_computation.1 | async-start | bytes 131072 | tf_op jit(solution)/shard_map/all_to_all | solution.py:439

commit v8 on v7

--- a/solution.py
+++ b/solution.py
@@ -258,7 +258,7 @@
 
 
 def imaging_kernel(
-    inbox_ref, table_ref, signed_ref, left_ref, right_ref, inside_ref, wv_ref,
+    inbox_ref, table_ref, signed_ref, left_ref, right_ref, wv_ref,
     loss_ref, edges_ref, gs_ref, mask_ref, s_ref, a_ref, sw_ref,
 ):
     rows, cols = signed_ref.shape
@@ -299,9 +299,7 @@
     edges_ref[64:112, :] = mask_ref[tall - 48 : tall, :].astype(BF16)
     windows(mask_ref[RAD : tall - RAD + 8, :], s_ref, RAD, cols)
     group_rows(s_ref, a_ref, RAD * PITCH, (tall - RAD) * PITCH, 16 * PITCH)
-    left = jnp.where(inside_ref[2:3, 0:1] > 0.0, left_ref[...], 0.0)
-    right = jnp.where(inside_ref[3:4, 0:1] > 0.0, right_ref[...], 0.0)
-    spread(signed_ref, left, right, sw_ref, rows, cols)
+    spread(signed_ref, left_ref[...], right_ref[...], sw_ref, rows, cols)
 
     wv = wv_ref[...]
     chunk = rows // 8 * PITCH
@@ -323,7 +321,7 @@
     loss_ref[...] = jnp.broadcast_to(total, loss_ref.shape)
 
 
-def imaging(inbox, table, signed, left, right, inside, wv, devices):
+def imaging(inbox, table, signed, left, right, wv, devices):
     rows, cols = signed.shape
     tall = rows + 4 * RAD
     return pl.pallas_call(
@@ -333,7 +331,7 @@
             pltpu.VMEM((112, cols + 128), BF16),
             pltpu.VMEM((rows * PITCH, 256), BF16),
         ),
-        in_specs=[WHOLE] * 7,
+        in_specs=[WHOLE] * 6,
         scratch_shapes=[
             pltpu.VMEM((tall, cols + 128), F32),
             pltpu.VMEM(((tall + 8) * PITCH, 128), F32),
@@ -342,7 +340,7 @@
         ],
         compiler_params=pltpu.CompilerParams(vmem_limit_bytes=VMEM_LIMIT),
         cost_estimate=pl.CostEstimate(flops=4 * 10**9, bytes_accessed=8 * 10**6, transcendentals=10**6),
-    )(inbox, table, signed, left, right, inside, wv)
+    )(inbox, table, signed, left, right, wv)
 
 
 def adjoint_taps(table_ref, start, at):
@@ -435,7 +433,7 @@
     table = make_tables(by_row)
     top, bottom, left, right, inside = weight_strips(*strips)
     wv = jnp.repeat(socs_weight, 2 * BLK).reshape(1, kernel.shape[0] * BLK)
-    local, edges, gs = imaging(inbox, table, signed, left, right, inside, wv, devices)
+    local, edges, gs = imaging(inbox, table, signed, left, right, wv, devices)
     losses = lax.all_to_all(local, ("row", "col"), split_axis=0, concat_axis=0, tiled=True)
     mask_grad = adjoint(edges, table, gs, top, bottom, inside, wv, rows, cols)
     window_area = rows * row_devices * cols * col_devices

time: 50.1 us -> 50 us (level)
  no operation moved by 1% of the time
where the time goes in v8:
time: 50 us; the launch traced here: 49.7 us
  starting transfers between devices  23.9 us (48%)
  Pallas kernels  15.4 us (31%)
  waiting for transfers between devices  5.98 us (12%)
  between operations  3.16 us (6%)
  other arithmetic  0.98 us (2%)
    all_to_all x1, starting transfers between devices, shards(): lax.all_to_all(outbox, ('row', 'col'), split_axis=0, concat_axis=0, tiled...  10.5 us
    ppermute x4, starting transfers between devices, beside(): return (lax.ppermute(last, axis, up), lax.ppermute(first, axis, down))  8.56 us
    pallas_call x1, Pallas kernels, adjoint(): pl.pallas_call(adjoint_kernel, out_shape=jax.ShapeDtypeStruct((rows, cols...  6.32 us
    pallas_call x1, Pallas kernels, imaging(): pl.pallas_call(imaging_kernel, out_shape=(pltpu.VMEM((devices, 1, 128), F...  5.95 us
    all_to_all x1, starting transfers between devices, shards(): lax.all_to_all(local, ('row', 'col'), split_axis=0, concat_axis=0, tiled=...  4.82 us
    all_to_all x1, waiting for transfers between devices, shards(): lax.all_to_all(local, ('row', 'col'), split_axis=0, concat_axis=0, tiled=...  3.19 us
    all_to_all x1, waiting for transfers between devices, shards(): lax.all_to_all(outbox, ('row', 'col'), split_axis=0, concat_axis=0, tiled...  2.78 us
    pallas_call x1, Pallas kernels, make_outbox(): pl.pallas_call(lambda *refs: outbox_kernel(tile_cols, *refs), out_shape=(...  2.11 us
  transfers between devices with their start and end apart: 6, of which 2 were waited for; matrix products, arithmetic and copies ran while one was open for 1% of the time, Pallas kernels for 27%

profile of v8, /device:TPU:1, one launch (start us, length us, event | category | flops | bytes accessed | tf_op | source)
XLA Modules:
  0.0 49.7 jit_solution(17208234120078448802)
XLA Ops:
  1.3 2.1 %shard_map.86 = (s32[128,2,128]{2,1,0:T(2,128)}, f32[128,512]{1,0:T(8,128)S(1)}, f32[16,512]{1,0:T(8,128)S(1)}, f32[16,512]{1,0:T(8,128)S(1)}, f32[128,16]{1,0:T...) custom-call(s32[1]{0:T(128)S(6)} %copy.9.refs_0_, s32[4,512]{1,0:T(4,128)} %refs_1_.1, ...), custom_call_target="tpu_custom_call" | custom-call | flops 100000000 | bytes 1000000 | tf_op jit(solution)/shard_map/pallas_call | solution.py:97
  3.4 2.8 %collective-permute-start = (f32[128,16]{1,0:T(8,128)S(1)}, f32[128,16]{1,0:T(8,128)S(1)}, u32[]{:S(2)}, u32[]{:S(2)}) collective-permute-start(f32[128,16]{1,0:T(8,128)S(1)} %broadcast_select_fusion.1), channel_id=1, source_target_pairs={{0,1},{1,2},{2,3},{3,4},{4,5},{5,6},{6,7},{7,8},{8,9},{9,10},{10,1... | collective-permute-start | bytes 24584 | tf_op jit(solution)/shard_map/ppermute | solution.py:166
  6.2 0.1 collective-permute-start.1
  6.3 10.5 %all-to-all-start = ((s32[128,2,128]{2,1,0:T(2,128)}), s32[128,2,128]{2,1,0:T(2,128)S(1)}, u32[]{:S(2)}, u32[]{:S(2)}) async-start(s32[128,2,128]{2,1,0:T(2,128)} %get-tuple-element.12), calls=%async_computation | async-start | bytes 262144 | tf_op jit(solution)/shard_map/all_to_all | solution.py:432
  16.8 0.0 copy-start
  16.8 1.1 %shard_map.87.table_ref = bf16[33,64,256]{2,1,0:T(8,128)(2,1)S(1)} custom-call(bf16[33,8,33]{2,1,0:T(8,128)(2,1)S(1)} %get-tuple-element.13.kernel_ref), custom_call_target="tpu_custom_call" | custom-call | flops 10000000000 | bytes 1000000 | tf_op jit(solution)/shard_map/pallas_call | solution.py:151
  17.9 0.1 add_convert_fusion
  18.0 0.1 broadcast_in_dim.15
  18.1 0.1 reshape_reshape.3.wv_ref
  18.1 0.0 collective-permute-done.1.right_ref
  18.2 0.0 collective-permute-done.left_ref
  18.2 0.1 pad_maximum_fusion
  18.2 2.9 %collective-permute-start.2 = (f32[16,544]{1,0:T(8,128)S(1)}, f32[16,544]{1,0:T(8,128)S(1)}, u32[]{:S(2)}, u32[]{:S(2)}) collective-permute-start(f32[16,544]{1,0:T(8,128)S(1)} %pad_maximum_fusion), channel_id=1, source_target_pairs={{0,16},{16,32},{32,48},{48,64},{64,80},{80,96},{96,112},{112,0},{1... | collective-permute-start | bytes 104456 | tf_op jit(solution)/shard_map/ppermute | solution.py:166
  21.2 0.1 pad_maximum_fusion.1
  21.2 2.8 %collective-permute-start.3 = (f32[16,544]{1,0:T(8,128)S(1)}, f32[16,544]{1,0:T(8,128)S(1)}, u32[]{:S(2)}, u32[]{:S(2)}) collective-permute-start(f32[16,544]{1,0:T(8,128)S(1)} %pad_maximum_fusion.1), channel_id=1, source_target_pairs={{16,0},{32,16},{48,32},{64,48},{80,64},{96,80},{112,96},{0,112},{1... | collective-permute-start | bytes 104456 | tf_op jit(solution)/shard_map/ppermute | solution.py:166
  24.1 2.8 %all-to-all-done.inbox_ref = s32[128,2,128]{2,1,0:T(2,128)S(1)} async-done(((s32[128,2,128]{2,1,0:T(2,128)}), s32[128,2,128]{2,1,0:T(2,128)S(1)}, u32[]{:S(2)}, u32[]{:S(2)}) %all-to-all-start) | async-done | bytes 131104 | tf_op jit(solution)/shard_map/all_to_all | solution.py:432
  26.8 5.9 %shard_map.88 = (f32[128,1,128]{2,1,0:T(1,128)}, bf16[112,640]{1,0:T(8,128)(2,1)S(1)}, bf16[2304,256]{1,0:T(8,128)(2,1)S(1)}) custom-call(s32[128,2,128]{2,1,0:T(2,128)S(1)} %all-to-all-done.inbox_ref, bf16[33,64,256]{2,1,0:T(8,128)(2,1)S(1)} %shard_map.87.table_ref, f32[128,512]{1,0:T(8,128)S(1)} %get-tuple-element.14.signed_ref, ...), custom_call_target="tpu_custom_call" | custom-call | flops 4000000000 | bytes 8000000 | tf_op jit(solution)/shard_map/pallas_call | solution.py:327
  32.8 4.8 %all-to-all-start.1 = ((f32[128,1,128]{2,1,0:T(1,128)}), f32[128,1,128]{2,1,0:T(1,128)S(1)}, u32[]{:S(2)}, u32[]{:S(2)}) async-start(f32[128,1,128]{2,1,0:T(1,128)} %get-tuple-element.21), calls=%async_computation.1 | async-start | bytes 131072 | tf_op jit(solution)/shard_map/all_to_all | solution.py:437
  37.6 0.0 collective-permute-done.2.top_ref
  37.6 0.0 collective-permute-done.3.bottom_ref
  37.6 0.1 broadcast_in_dim.16.inside_ref
  37.7 6.3 %shard_map.89 = f32[128,512]{1,0:T(8,128)} custom-call(bf16[112,640]{1,0:T(8,128)(2,1)S(1)} %get-tuple-element.17.edges_ref, bf16[33,64,256]{2,1,0:T(8,128)(2,1)S(1)} %shard_map.87.table_ref, bf16[2304,256]{1,0:T(8,128)(2,1)S(1)} %get-tuple-element.18.gs_ref, f32[16,544]{1,0:T(8,128)S(1)} %collective-permute-done.2.top_ref, ...), custom_call_target="tpu_custom_call" | custom-call | flops 4000000000 | bytes 10000000 | tf_op jit(solution)/shard_map/pallas_call | solution.py:405
  44.0 3.2 %all-to-all-done.1 = f32[128,1,128]{2,1,0:T(1,128)S(1)} async-done(((f32[128,1,128]{2,1,0:T(1,128)}), f32[128,1,128]{2,1,0:T(1,128)S(1)}, u32[]{:S(2)}, u32[]{:S(2)}) %all-to-all-start.1) | async-done | bytes 65568 | tf_op jit(solution)/shard_map/all_to_all | solution.py:437
  47.2 0.7 %slice_reduce_fusion = f32[]{:T(128)} fusion(f32[128,1,128]{2,1,0:T(1,128)S(1)} %all-to-all-done.1), kind=kLoop, calls=%fused_computation | loop fusion | flops 127 | bytes 516 | tf_op jit(solution)/shard_map/reduce_sum | solution.py:440
  (5 shorter events, 0.0 us)
Async XLA Ops:
  3.4 14.7 %collective-permute-start = (f32[128,16]{1,0:T(8,128)S(1)}, f32[128,16]{1,0:T(8,128)S(1)}, u32[]{:S(2)}, u32[]{:S(2)}) collective-permute-start(f32[128,16]{1,0:T(8,128)S(1)} %broadcast_select_fusion.1), channel_id=1, source_target_pairs={{0,1},{1,2},{2,3},{3,4},{4,5},{5,6},{6,7},{7,8},{8,9},{9,10},{10,1... | collective-permute-start | bytes 24584 | tf_op jit(solution)/shard_map/ppermute | solution.py:166
  6.2 12.0 %collective-permute-start.1 = (f32[128,16]{1,0:T(8,128)S(1)}, f32[128,16]{1,0:T(8,128)S(1)}, u32[]{:S(2)}, u32[]{:S(2)}) collective-permute-start(f32[128,16]{1,0:T(8,128)S(1)} %broadcast_select_fusion), channel_id=1, source_target_pairs={{1,0},{2,1},{3,2},{4,3},{5,4},{6,5},{7,6},{8,7},{9,8},{10,9},{11,1... | collective-permute-start | bytes 24584 | tf_op jit(solution)/shard_map/ppermute | solution.py:166
  6.3 20.6 %all-to-all-start = ((s32[128,2,128]{2,1,0:T(2,128)}), s32[128,2,128]{2,1,0:T(2,128)S(1)}, u32[]{:S(2)}, u32[]{:S(2)}) async-start(s32[128,2,128]{2,1,0:T(2,128)} %get-tuple-element.12), calls=%async_computation | async-start | bytes 262144 | tf_op jit(solution)/shard_map/all_to_all | solution.py:432
  16.8 1.2 %copy-start = (f32[4]{0:T(128)S(1)}, f32[4]{0:T(128)}, u32[]{:S(2)}) copy-start(f32[4]{0:T(128)} %param.13) | copy-start | bytes 52
  18.2 19.4 %collective-permute-start.2 = (f32[16,544]{1,0:T(8,128)S(1)}, f32[16,544]{1,0:T(8,128)S(1)}, u32[]{:S(2)}, u32[]{:S(2)}) collective-permute-start(f32[16,544]{1,0:T(8,128)S(1)} %pad_maximum_fusion), channel_id=1, source_target_pairs={{0,16},{16,32},{32,48},{48,64},{64,80},{80,96},{96,112},{112,0},{1... | collective-permute-start | bytes 104456 | tf_op jit(solution)/shard_map/ppermute | solution.py:166
  21.2 16.4 %collective-permute-start.3 = (f32[16,544]{1,0:T(8,128)S(1)}, f32[16,544]{1,0:T(8,128)S(1)}, u32[]{:S(2)}, u32[]{:S(2)}) collective-permute-start(f32[16,544]{1,0:T(8,128)S(1)} %pad_maximum_fusion.1), channel_id=1, source_target_pairs={{16,0},{32,16},{48,32},{64,48},{80,64},{96,80},{112,96},{0,112},{1... | collective-permute-start | bytes 104456 | tf_op jit(solution)/shard_map/ppermute | solution.py:166
  32.8 14.4 %all-to-all-start.1 = ((f32[128,1,128]{2,1,0:T(1,128)}), f32[128,1,128]{2,1,0:T(1,128)S(1)}, u32[]{:S(2)}, u32[]{:S(2)}) async-start(f32[128,1,128]{2,1,0:T(1,128)} %get-tuple-element.21), calls=%async_computation.1 | async-start | bytes 131072 | tf_op jit(solution)/shard_map/all_to_all | solution.py:437
